TPU v7x, 128 devices: a whole 4x4x4 slice. The times are simulated.
128 devices in a mesh: lon: 16 (over z, y), lat: 8 (over x, core).
Axes of the slice: x: 4, y: 4, z: 4, core: 2. Of those that a mesh axis runs over, the one named last changes fastest.
Arguments:
- forcing: float32 [2, 8192, 4096], P(None, 'lon', 'lat'), may hold values from -6 to 6
- velocity: float32 [2, 32, 32, 16384], P(None, None, None, ('lon', 'lat')), may hold values from -4 to 4
- stress: float32 [3, 32, 32, 16384], P(None, None, None, ('lon', 'lat')), may hold values from -4 to 4
- mass: float32 [32, 32, 16384], P(None, None, ('lon', 'lat')), may hold values from 0.5 to 4
- strength: float32 [32, 32, 16384], P(None, None, ('lon', 'lat')), may hold values from 0.2 to 2
- owner: int32 [256, 128], replicated, may hold values from -1 to 16383, as said below
Outputs:
- new_velocity: float32 [2, 8192, 4096], P(None, 'lon', 'lat')
- new_stress: float32 [3, 32, 32, 16384], P(None, None, None, ('lon', 'lat'))
Inputs may be any that keep to these rules, and one draw needn't show every extreme that they name: `owner`: the ice-covered blocks, taken ocean tile by ocean tile (tiles in the order of lon+lat, each tile the 16 x 16 blocks of one device of the forcing, row by row with latitude fastest) are numbered 0, 1, 2, ... in that order; all other blocks hold -1. There are exactly 16384 ice-covered blocks; a tile holds anywhere from none to all of its blocks, and some tile is fully ice-covered.
All inputs are finite; a program needn't handle non-finite values.
Results may differ from a plain program's by a relative error of at most 0.000073.
Values sent between devices are 32-bit elements; how exact they have to be, the bound alone decides.
No kernel may reach another device: no remote copies, remote signals or barrier semaphores. Data moves between devices by JAX's collectives and lax.ppermute only.
A program may use at most 192 MiB of HBM per device.

v0:
```python
import jax
import jax.numpy as jnp
from jax import lax
from jax.sharding import PartitionSpec as P

B = 32
BX_DEV = 16
BY_DEV = 16
ITERS = 6


ECC_SQUARED = 4.0
DELTA_MIN = 0.5
RELAX_RATE = 1.0
TIME_STEP = 0.5
WATER_DRAG = 1.0
CORIOLIS = 0.5


def extended(cells, sides, width):
    for axis, dim in sides:
        count = lax.axis_size(axis)
        head = lax.slice_in_dim(cells, 0, width, axis=dim)
        tail = lax.slice_in_dim(cells, cells.shape[dim] - width, cells.shape[dim], axis=dim)
        cells = jnp.concatenate(
            [
                lax.ppermute(tail, axis, [(i, (i + 1) % count) for i in range(count)]),
                cells,
                lax.ppermute(head, axis, [((i + 1) % count, i) for i in range(count)]),
            ],
            axis=dim,
        )
    return cells


def stress_step(
    zonal_vel,
    merid_vel,
    zonal_east,
    merid_east,
    zonal_north,
    merid_north,
    stress_sum,
    stress_diff,
    stress_shear,
    strength,
):
    grad_zonal_x = zonal_east - zonal_vel
    grad_merid_y = merid_north - merid_vel
    grad_zonal_y = zonal_north - zonal_vel
    grad_merid_x = merid_east - merid_vel
    divergence = grad_zonal_x + grad_merid_y
    tension = grad_zonal_x - grad_merid_y
    shearing = grad_zonal_y + grad_merid_x
    spread = jnp.sqrt(
        divergence * divergence
        + (tension * tension + shearing * shearing) / ECC_SQUARED
        + DELTA_MIN * DELTA_MIN
    )
    weight = strength / spread
    new_sum = (stress_sum + RELAX_RATE * (weight * divergence - strength)) / (1.0 + RELAX_RATE)
    new_diff = (stress_diff + RELAX_RATE * weight * tension / ECC_SQUARED) / (1.0 + RELAX_RATE)
    new_shear = (stress_shear + RELAX_RATE * 0.5 * weight * shearing / ECC_SQUARED) / (
        1.0 + RELAX_RATE
    )
    return (new_sum, new_diff, new_shear)


def momentum_step(
    zonal_vel,
    merid_vel,
    stress_sum,
    stress_diff,
    stress_shear,
    west_sum,
    west_diff,
    west_shear,
    south_sum,
    south_diff,
    south_shear,
    mass,
    force_zonal,
    force_merid,
    coriolis,
):
    normal_xx = 0.5 * (stress_sum + stress_diff)
    normal_xx_west = 0.5 * (west_sum + west_diff)
    normal_yy = 0.5 * (stress_sum - stress_diff)
    normal_yy_south = 0.5 * (south_sum - south_diff)
    push_zonal = normal_xx - normal_xx_west + (stress_shear - south_shear)
    push_merid = stress_shear - west_shear + (normal_yy - normal_yy_south)
    damping = mass + TIME_STEP * WATER_DRAG
    new_zonal = (
        mass * zonal_vel
        + TIME_STEP * (push_zonal + force_zonal)
        + TIME_STEP * mass * coriolis * merid_vel
    ) / damping
    new_merid = (
        mass * merid_vel
        + TIME_STEP * (push_merid + force_merid)
        - TIME_STEP * mass * coriolis * zonal_vel
    ) / damping
    return (new_zonal, new_merid)


def one_hot(places, length):
    return (places[:, None] == jnp.arange(length, dtype=jnp.int32)[None, :]).astype(jnp.float32)


def place_columns(data, table):
    return jnp.dot(data, table, precision=lax.Precision.HIGHEST, preferred_element_type=jnp.float32)


def pick_columns(data, table):
    return lax.dot_general(
        data,
        table,
        (((1,), (1,)), ((), ())),
        precision=lax.Precision.HIGHEST,
        preferred_element_type=jnp.float32,
    )


def on_device(forcing, velocity, stress, mass, strength, owner):
    lon_count = lax.axis_size("lon")
    lat_count = lax.axis_size("lat")
    devices = lon_count * lat_count
    lat_index = lax.axis_index("lat")
    lon_index = lax.axis_index("lon")
    own_index = lon_index * lat_count + lat_index
    tile_count = BX_DEV * BY_DEV
    capacity = tile_count // devices
    slot_count = velocity.shape[-1]
    buffer_len = devices * capacity
    cells_x = BX_DEV * B
    cells_y = BY_DEV * B
    tile_table = (
        owner.reshape(lon_count, BX_DEV, lat_count, BY_DEV)
        .transpose(0, 2, 1, 3)
        .reshape(devices, tile_count)
    )
    counts = jnp.sum((tile_table >= 0).astype(jnp.int32), axis=1)
    starts = jnp.cumsum(counts) - counts
    my_tile = lax.dynamic_index_in_dim(tile_table, own_index, 0, keepdims=False)
    my_start = lax.dynamic_index_in_dim(starts, own_index, 0, keepdims=False)
    tile_pos = jnp.where(
        my_tile >= 0, my_tile % devices * capacity + (my_tile - my_start) // devices, buffer_len
    )
    slot_number = jnp.arange(slot_count, dtype=jnp.int32) * devices + own_index
    flat_table = tile_table.reshape(-1)
    matches = flat_table[None, :] == slot_number[:, None]
    source = jnp.sum(
        jnp.where(matches, jnp.arange(devices * tile_count, dtype=jnp.int32)[None, :], 0), axis=1
    )
    src_tile = source // tile_count
    src_block = source % tile_count
    slot_pos = src_tile * capacity + (slot_number - jnp.take(starts, src_tile)) // devices
    tile_matrix = one_hot(tile_pos, buffer_len)
    slot_matrix = one_hot(slot_pos, buffer_len)

    def to_blocks(row_data):
        outgoing = place_columns(row_data, tile_matrix).reshape(
            row_data.shape[0], devices, capacity
        )
        incoming = lax.all_to_all(outgoing, ("lon", "lat"), split_axis=1, concat_axis=1, tiled=True)
        return pick_columns(incoming.reshape(row_data.shape[0], buffer_len), slot_matrix)

    def to_tiles(row_data):
        outgoing = place_columns(row_data, slot_matrix).reshape(
            row_data.shape[0], devices, capacity
        )
        incoming = lax.all_to_all(outgoing, ("lon", "lat"), split_axis=1, concat_axis=1, tiled=True)
        return pick_columns(incoming.reshape(row_data.shape[0], buffer_len), tile_matrix)

    def edge_keep(length, edge_row, edge_dev):
        return jnp.where(
            (jnp.arange(length) == edge_row) & (lat_index == edge_dev), 0.0, 1.0
        ).astype(jnp.float32)

    def neighbour_strips(strips, upper):
        comps = strips.shape[0]
        rows = comps * 2 * B
        tiled = to_tiles(strips.reshape(rows, slot_count)).T.reshape(BX_DEV, BY_DEV, rows)
        rim = extended(tiled, (("lon", 0), ("lat", 1)), 1)
        rim = rim.reshape(BX_DEV + 2, BY_DEV + 2, comps, 2, B)
        if upper:
            across = rim[2:, 1:-1, :, 0]
            along = (
                rim[1:-1, 2:, :, 1]
                * edge_keep(BY_DEV, BY_DEV - 1, lat_count - 1)[None, :, None, None]
            )
        else:
            across = rim[:-2, 1:-1, :, 0]
            along = rim[1:-1, :-2, :, 1] * edge_keep(BY_DEV, 0, 0)[None, :, None, None]
        both = jnp.stack((across, along), axis=3).reshape(tile_count, rows).T
        return to_blocks(both).reshape(comps, 2, B, slot_count)

    comps = forcing.shape[0]
    force_blocks = to_blocks(
        forcing.reshape(comps, BX_DEV, B, BY_DEV, B)
        .transpose(0, 2, 4, 1, 3)
        .reshape(comps * B * B, tile_count)
    ).reshape(2, B, B, slot_count)
    lat_block = src_tile % lat_count * BY_DEV + src_block % BY_DEV
    lat_cell = lat_block[None, :] * B + jnp.arange(B, dtype=jnp.int32)[:, None]
    coriolis = (
        CORIOLIS * (2.0 * (lat_cell.astype(jnp.float32) + 0.5) / (cells_y * lat_count) - 1.0)
    )[None]
    zonal, merid = (velocity[0], velocity[1])
    stress_sum, stress_diff, stress_shear = (stress[0], stress[1], stress[2])
    for step in range(ITERS):
        vel_strips = jnp.stack([jnp.stack((field[0], field[:, 0])) for field in (zonal, merid)])
        got_vel = neighbour_strips(vel_strips, True)
        zonal_east = jnp.concatenate((zonal[1:], got_vel[0, 0][None]), axis=0)
        merid_east = jnp.concatenate((merid[1:], got_vel[1, 0][None]), axis=0)
        zonal_north = jnp.concatenate((zonal[:, 1:], got_vel[0, 1][:, None]), axis=1)
        merid_north = jnp.concatenate((merid[:, 1:], got_vel[1, 1][:, None]), axis=1)
        stress_sum, stress_diff, stress_shear = stress_step(
            zonal,
            merid,
            zonal_east,
            merid_east,
            zonal_north,
            merid_north,
            stress_sum,
            stress_diff,
            stress_shear,
            strength,
        )
        fields = (stress_sum, stress_diff, stress_shear)
        str_strips = jnp.stack([jnp.stack((field[-1], field[:, -1])) for field in fields])
        got_str = neighbour_strips(str_strips, False)
        wests = [
            jnp.concatenate((got_str[index, 0][None], fields[index][:-1]), axis=0)
            for index in range(3)
        ]
        souths = [
            jnp.concatenate((got_str[index, 1][:, None], fields[index][:, :-1]), axis=1)
            for index in range(3)
        ]
        zonal, merid = momentum_step(
            zonal,
            merid,
            stress_sum,
            stress_diff,
            stress_shear,
            wests[0],
            wests[1],
            wests[2],
            souths[0],
            souths[1],
            souths[2],
            mass,
            force_blocks[0],
            force_blocks[1],
            coriolis,
        )
    moved = to_tiles(jnp.stack((zonal, merid)).reshape(2 * B * B, slot_count))
    new_velocity = (
        moved.reshape(2, B, B, BX_DEV, BY_DEV).transpose(0, 3, 1, 4, 2).reshape(2, cells_x, cells_y)
    )
    new_stress = jnp.stack((stress_sum, stress_diff, stress_shear))
    return (new_velocity, new_stress)


def solution(mesh):
    in_specs = (
        P(None, "lon", "lat"),
        P(None, None, None, ("lon", "lat")),
        P(None, None, None, ("lon", "lat")),
        P(None, None, ("lon", "lat")),
        P(None, None, ("lon", "lat")),
        P(),
    )
    out_specs = (P(None, "lon", "lat"), P(None, None, None, ("lon", "lat")))
    return jax.shard_map(
        on_device, mesh=mesh, in_specs=in_specs, out_specs=out_specs, check_vma=False
    )
```

profile of v0, /device:TPU:1, one launch (start us, length us, event | category | flops | bytes accessed | tf_op | source)
XLA Modules:
  0.0 874.6 jit_solution(15351678885613495409)
XLA Ops:
  11.3 11.5 %all-to-all-start = ((f32[128,128,2]{0,2,1:T(2,128)}), f32[128,128,2]{0,2,1:T(2,128)S(1)}, u32[]{:S(2)}, u32[]{:S(2)}) async-start(f32[128,128,2]{0,2,1:T(2,128)} %copy.319), calls=%async_computation | async-start | bytes 262144 | tf_op jit(solution)/shard_map/all_to_all | solution.py:172
  26.2 6.6 all-to-all-done
  46.9 6.6 all-to-all-start.1
  56.1 7.6 all-to-all-done.1
  70.9 15.2 %all_to_all.130 = f32[192,128,2]{0,2,1:T(2,128)} all-to-all(f32[192,128,2]{0,2,1:T(2,128)S(1)} %copy.327), channel_id=1, replica_groups=mesh['lon'=16,'lat'=8] {'lon','lat'}, dimensions={1} | all-to-all | bytes 393216 | tf_op jit(solution)/shard_map/all_to_all | solution.py:172
  99.5 6.1 reshape.697
  105.6 9.2 %copy.515 = f32[2,16,32,16,32]{4,2,0,3,1:T(8,128)} copy(f32[2,16,32,16,32]{4,3,2,1,0:T(8,128)} %reshape.697) | data formatting | bytes 4194304 | tf_op jit(solution)/shard_map/reshape | solution.py:200
  114.8 7.5 reshape.698
  149.7 6.8 all-to-all-start.4
  160.6 26.1 %all-to-all-done.4 = f32[2048,128,2]{0,2,1:T(2,128)} async-done(((f32[2048,128,2]{0,2,1:T(2,128)}), f32[2048,128,2]{0,2,1:T(2,128)}, u32[]{:S(2)}, u32[]{:S(2)}) %all-to-all-start.4) | async-done | bytes 2097184 | tf_op jit(solution)/shard_map/all_to_all | solution.py:165
  196.6 14.0 %all_to_all.131 = f32[128,128,2]{0,2,1:T(2,128)S(1)} all-to-all(f32[128,128,2]{0,2,1:T(2,128)S(1)} %copy.339), channel_id=1, replica_groups=mesh['lon'=16,'lat'=8] {'lon','lat'}, dimensions={1} | all-to-all | bytes 262144 | tf_op jit(solution)/shard_map/all_to_all | solution.py:172
  224.7 6.5 all-to-all-start.6
  233.8 7.5 all-to-all-done.6
  249.4 15.2 %all_to_all.132 = f32[192,128,2]{0,2,1:T(2,128)} all-to-all(f32[192,128,2]{0,2,1:T(2,128)S(1)} %copy.347), channel_id=1, replica_groups=mesh['lon'=16,'lat'=8] {'lon','lat'}, dimensions={1} | all-to-all | bytes 393216 | tf_op jit(solution)/shard_map/all_to_all | solution.py:172
  291.7 6.7 all-to-all-start.8
  302.1 7.4 all-to-all-done.8
  318.3 14.4 %all_to_all.133 = f32[128,128,2]{0,2,1:T(2,128)S(1)} all-to-all(f32[128,128,2]{0,2,1:T(2,128)S(1)} %copy.358), channel_id=1, replica_groups=mesh['lon'=16,'lat'=8] {'lon','lat'}, dimensions={1} | all-to-all | bytes 262144 | tf_op jit(solution)/shard_map/all_to_all | solution.py:172
  350.8 6.2 all-to-all-start.10
  360.3 6.8 all-to-all-done.10
  372.7 15.2 %all_to_all.134 = f32[192,128,2]{0,2,1:T(2,128)S(1)} all-to-all(f32[192,128,2]{0,2,1:T(2,128)S(1)} %copy.366), channel_id=1, replica_groups=mesh['lon'=16,'lat'=8] {'lon','lat'}, dimensions={1} | all-to-all | bytes 393216 | tf_op jit(solution)/shard_map/all_to_all | solution.py:172
  412.9 6.2 all-to-all-start.12
  423.6 6.7 all-to-all-done.12
  437.8 14.4 %all_to_all.135 = f32[128,128,2]{0,2,1:T(2,128)S(1)} all-to-all(f32[128,128,2]{0,2,1:T(2,128)S(1)} %copy.377), channel_id=1, replica_groups=mesh['lon'=16,'lat'=8] {'lon','lat'}, dimensions={1} | all-to-all | bytes 262144 | tf_op jit(solution)/shard_map/all_to_all | solution.py:172
  455.0 4.7 collective-permute-done.24
  470.4 6.2 all-to-all-start.14
  480.0 6.8 all-to-all-done.14
  493.9 15.2 %all_to_all.136 = f32[192,128,2]{0,2,1:T(2,128)S(1)} all-to-all(f32[192,128,2]{0,2,1:T(2,128)S(1)} %copy.385), channel_id=1, replica_groups=mesh['lon'=16,'lat'=8] {'lon','lat'}, dimensions={1} | all-to-all | bytes 393216 | tf_op jit(solution)/shard_map/all_to_all | solution.py:172
  533.9 6.6 all-to-all-start.16
  544.1 7.6 all-to-all-done.16
  559.3 14.4 %all_to_all.137 = f32[128,128,2]{0,2,1:T(2,128)S(1)} all-to-all(f32[128,128,2]{0,2,1:T(2,128)S(1)} %copy.396), channel_id=1, replica_groups=mesh['lon'=16,'lat'=8] {'lon','lat'}, dimensions={1} | all-to-all | bytes 262144 | tf_op jit(solution)/shard_map/all_to_all | solution.py:172
  591.7 6.2 all-to-all-start.18
  601.2 6.8 all-to-all-done.18
  616.7 15.4 %all_to_all.138 = f32[192,128,2]{0,2,1:T(2,128)} all-to-all(f32[192,128,2]{0,2,1:T(2,128)S(1)} %copy.404), channel_id=1, replica_groups=mesh['lon'=16,'lat'=8] {'lon','lat'}, dimensions={1} | all-to-all | bytes 393216 | tf_op jit(solution)/shard_map/all_to_all | solution.py:172
  638.1 4.7 collective-permute-done.36
  659.3 6.2 all-to-all-start.20
  670.0 6.7 all-to-all-done.20
  684.2 14.4 %all_to_all.139 = f32[128,128,2]{0,2,1:T(2,128)S(1)} all-to-all(f32[128,128,2]{0,2,1:T(2,128)S(1)} %copy.415), channel_id=1, replica_groups=mesh['lon'=16,'lat'=8] {'lon','lat'}, dimensions={1} | all-to-all | bytes 262144 | tf_op jit(solution)/shard_map/all_to_all | solution.py:172
  701.5 4.7 collective-permute-done.40
  716.8 6.2 all-to-all-start.22
  726.4 6.8 all-to-all-done.22
  740.2 15.2 %all_to_all.140 = f32[192,128,2]{0,2,1:T(2,128)S(1)} all-to-all(f32[192,128,2]{0,2,1:T(2,128)S(1)} %copy.423), channel_id=1, replica_groups=mesh['lon'=16,'lat'=8] {'lon','lat'}, dimensions={1} | all-to-all | bytes 393216 | tf_op jit(solution)/shard_map/all_to_all | solution.py:172
  776.4 6.4 all-to-all-start.24
  786.4 7.7 all-to-all-done.24
  807.4 5.3 all-to-all-start.25
  814.7 28.3 %all-to-all-done.25 = f32[2048,128,2]{0,2,1:T(2,128)} async-done(((f32[2048,128,2]{0,2,1:T(2,128)}), f32[2048,128,2]{0,2,1:T(2,128)}, u32[]{:S(2)}, u32[]{:S(2)}) %all-to-all-start.25) | async-done | bytes 2097184 | tf_op jit(solution)/shard_map/all_to_all | solution.py:172
  843.0 6.9 dot_general.248
  849.9 12.6 %fusion.2 = f32[2,16,32,16,32]{4,3,1,2,0:T(8,128)S(1)} fusion(f32[2,32,32,256,1]{2,1,0,3,4:T(8,128)} %bitcast.623, s32[16,16]{1,0:T(8,128)S(1)} %fusion.306), kind=kOutput, calls=%fused_computation.5 | convolution fusion | flops 1610678272 | bytes 4195328 | tf_op jit(solution)/shard_map/dot_general | solution.py:115
  866.8 7.3 reshape.752
  (693 shorter events, 410.9 us)
Async XLA Ops:
  11.3 21.5 %all-to-all-start = ((f32[128,128,2]{0,2,1:T(2,128)}), f32[128,128,2]{0,2,1:T(2,128)S(1)}, u32[]{:S(2)}, u32[]{:S(2)}) async-start(f32[128,128,2]{0,2,1:T(2,128)} %copy.319), calls=%async_computation | async-start | bytes 262144 | tf_op jit(solution)/shard_map/all_to_all | solution.py:172
  33.1 2.6 collective-permute-start.1
  34.4 5.8 collective-permute-start
  40.3 3.4 collective-permute-start.3
  46.9 16.8 %all-to-all-start.1 = ((f32[128,128,2]{0,2,1:T(2,128)}), f32[128,128,2]{0,2,1:T(2,128)S(1)}, u32[]{:S(2)}, u32[]{:S(2)}) async-start(f32[128,128,2]{0,2,1:T(2,128)} %copy.321), calls=%async_computation.1 | async-start | bytes 262144 | tf_op jit(solution)/shard_map/all_to_all | solution.py:165
  89.0 3.8 collective-permute-start.5
  90.3 7.0 collective-permute-start.4
  97.4 24.9 %collective-permute-start.7 = (f32[18,1,192]{2,1,0:T(1,128)S(1)}, f32[18,1,192]{2,1,0:T(1,128)S(1)}, u32[]{:S(2)}, u32[]{:S(2)}) collective-permute-start(f32[18,1,192]{2,1,0:T(1,128)S(1)} %get-tuple-element.79), channel_id=1, source_target_pairs={{1,0},{2,1},{3,2},{4,3},{5,4},{6,5},{7,6},{0,7},{9,8},{10,9},{11,1... | collective-permute-start | bytes 41480 | tf_op jit(solution)/shard_map/ppermute | solution.py:29
  99.3 23.0 %collective-permute-start.6 = (f32[18,1,192]{2,1,0:T(1,128)S(1)}, f32[18,1,192]{2,1,0:T(1,128)S(1)}, u32[]{:S(2)}, u32[]{:S(2)}) collective-permute-start(f32[18,1,192]{2,1,0:T(1,128)S(1)} %get-tuple-element.78), channel_id=1, source_target_pairs={{0,1},{1,2},{2,3},{3,4},{4,5},{5,6},{6,7},{7,0},{8,9},{9,10},{10,1... | collective-permute-start | bytes 41480 | tf_op jit(solution)/shard_map/ppermute | solution.py:27
  134.2 15.4 %all-to-all-start.3 = ((f32[192,128,2]{0,2,1:T(2,128)}), f32[192,128,2]{0,2,1:T(2,128)S(1)}, u32[]{:S(2)}, u32[]{:S(2)}) async-start(f32[192,128,2]{0,2,1:T(2,128)} %copy.332), calls=%async_computation.3 | async-start | bytes 524288 | tf_op jit(solution)/shard_map/all_to_all | solution.py:165
  149.7 37.0 %all-to-all-start.4 = ((f32[2048,128,2]{0,2,1:T(2,128)}), f32[2048,128,2]{0,2,1:T(2,128)}, u32[]{:S(2)}, u32[]{:S(2)}) async-start(f32[2048,128,2]{0,2,1:T(2,128)} %reshape.699), calls=%async_computation.4 | async-start | bytes 4194304 | tf_op jit(solution)/shard_map/all_to_all | solution.py:165
  212.2 5.8 collective-permute-start.8
  218.0 3.4 collective-permute-start.11
  224.7 16.6 %all-to-all-start.6 = ((f32[128,128,2]{0,2,1:T(2,128)}), f32[128,128,2]{0,2,1:T(2,128)S(1)}, u32[]{:S(2)}, u32[]{:S(2)}) async-start(f32[128,128,2]{0,2,1:T(2,128)} %copy.341), calls=%async_computation.6 | async-start | bytes 262144 | tf_op jit(solution)/shard_map/all_to_all | solution.py:165
  266.9 3.7 collective-permute-start.13
  268.2 7.1 collective-permute-start.12
  276.3 3.5 collective-permute-start.15
  291.7 17.8 %all-to-all-start.8 = ((f32[192,128,2]{0,2,1:T(2,128)}), f32[192,128,2]{0,2,1:T(2,128)S(1)}, u32[]{:S(2)}, u32[]{:S(2)}) async-start(f32[192,128,2]{0,2,1:T(2,128)} %copy.352), calls=%async_computation.8 | async-start | bytes 524288 | tf_op jit(solution)/shard_map/all_to_all | solution.py:165
  333.0 2.6 collective-permute-start.17
  334.3 5.8 collective-permute-start.16
  340.2 3.4 collective-permute-start.19
  350.8 16.3 %all-to-all-start.10 = ((f32[128,128,2]{0,2,1:T(2,128)}), f32[128,128,2]{0,2,1:T(2,128)S(1)}, u32[]{:S(2)}, u32[]{:S(2)}) async-start(f32[128,128,2]{0,2,1:T(2,128)} %copy.360), calls=%async_computation.10 | async-start | bytes 262144 | tf_op jit(solution)/shard_map/all_to_all | solution.py:165
  389.2 3.8 collective-permute-start.21
  390.5 6.8 collective-permute-start.20
  397.4 3.5 collective-permute-start.23
  412.9 17.4 %all-to-all-start.12 = ((f32[192,128,2]{0,2,1:T(2,128)}), f32[192,128,2]{0,2,1:T(2,128)S(1)}, u32[]{:S(2)}, u32[]{:S(2)}) async-start(f32[192,128,2]{0,2,1:T(2,128)} %copy.371), calls=%async_computation.12 | async-start | bytes 524288 | tf_op jit(solution)/shard_map/all_to_all | solution.py:165
  453.8 6.0 collective-permute-start.24
  459.8 3.4 collective-permute-start.27
  470.4 16.3 %all-to-all-start.14 = ((f32[128,128,2]{0,2,1:T(2,128)}), f32[128,128,2]{0,2,1:T(2,128)S(1)}, u32[]{:S(2)}, u32[]{:S(2)}) async-start(f32[128,128,2]{0,2,1:T(2,128)} %copy.379), calls=%async_computation.14 | async-start | bytes 262144 | tf_op jit(solution)/shard_map/all_to_all | solution.py:165
  510.4 3.7 collective-permute-start.29
  511.5 6.8 collective-permute-start.28
  518.4 3.5 collective-permute-start.31
  533.9 17.8 %all-to-all-start.16 = ((f32[192,128,2]{0,2,1:T(2,128)}), f32[192,128,2]{0,2,1:T(2,128)S(1)}, u32[]{:S(2)}, u32[]{:S(2)}) async-start(f32[192,128,2]{0,2,1:T(2,128)} %copy.390), calls=%async_computation.16 | async-start | bytes 524288 | tf_op jit(solution)/shard_map/all_to_all | solution.py:165
  575.2 5.8 collective-permute-start.32
  581.1 3.4 collective-permute-start.35
  591.7 16.4 %all-to-all-start.18 = ((f32[128,128,2]{0,2,1:T(2,128)}), f32[128,128,2]{0,2,1:T(2,128)S(1)}, u32[]{:S(2)}, u32[]{:S(2)}) async-start(f32[128,128,2]{0,2,1:T(2,128)} %copy.398), calls=%async_computation.18 | async-start | bytes 262144 | tf_op jit(solution)/shard_map/all_to_all | solution.py:165
  634.4 3.7 collective-permute-start.37
  635.7 7.1 collective-permute-start.36
  643.8 3.5 collective-permute-start.39
  659.3 17.4 %all-to-all-start.20 = ((f32[192,128,2]{0,2,1:T(2,128)}), f32[192,128,2]{0,2,1:T(2,128)S(1)}, u32[]{:S(2)}, u32[]{:S(2)}) async-start(f32[192,128,2]{0,2,1:T(2,128)} %copy.409), calls=%async_computation.20 | async-start | bytes 524288 | tf_op jit(solution)/shard_map/all_to_all | solution.py:165
  700.2 6.0 collective-permute-start.40
  706.2 3.4 collective-permute-start.43
  716.8 16.3 %all-to-all-start.22 = ((f32[128,128,2]{0,2,1:T(2,128)}), f32[128,128,2]{0,2,1:T(2,128)S(1)}, u32[]{:S(2)}, u32[]{:S(2)}) async-start(f32[128,128,2]{0,2,1:T(2,128)} %copy.417), calls=%async_computation.22 | async-start | bytes 262144 | tf_op jit(solution)/shard_map/all_to_all | solution.py:165
  756.2 3.5 collective-permute-start.45
  757.4 6.8 collective-permute-start.44
  764.3 3.5 collective-permute-start.47
  776.4 17.7 %all-to-all-start.24 = ((f32[192,128,2]{0,2,1:T(2,128)}), f32[192,128,2]{0,2,1:T(2,128)S(1)}, u32[]{:S(2)}, u32[]{:S(2)}) async-start(f32[192,128,2]{0,2,1:T(2,128)} %copy.428), calls=%async_computation.24 | async-start | bytes 524288 | tf_op jit(solution)/shard_map/all_to_all | solution.py:165
  807.4 35.6 %all-to-all-start.25 = ((f32[2048,128,2]{0,2,1:T(2,128)}), f32[2048,128,2]{0,2,1:T(2,128)}, u32[]{:S(2)}, u32[]{:S(2)}) async-start(f32[2048,128,2]{0,2,1:T(2,128)} %copy.433), calls=%async_computation.25 | async-start | bytes 4194304 | tf_op jit(solution)/shard_map/all_to_all | solution.py:172
  (111 other events, 918.3 us)
where the time goes:
time: 887 us; the launch traced here: 875 us
  waiting for transfers between devices  227 us (26%)
  local copies, waits for them, and re-layouts  193 us (22%)
  blocking collectives  163 us (18%)
  starting transfers between devices  141 us (16%)
  other arithmetic  87.8 us (10%)
  matrix products  59.4 us (7%)
    all_to_all x11, blocking collectives, to_tiles(): lax.all_to_all(outgoing, ('lon', 'lat'), split_axis=1, concat_axis=1, til...  163 us
    all_to_all x13, waiting for transfers between devices, to_blocks(): lax.all_to_all(outgoing, ('lon', 'lat'), split_axis=1, concat_axis=1, til...  108 us
    all_to_all x13, starting transfers between devices, to_blocks(): lax.all_to_all(outgoing, ('lon', 'lat'), split_axis=1, concat_axis=1, til...  81.1 us
    ppermute x24, waiting for transfers between devices, extended(): lax.ppermute(tail, axis, [(i, (i + 1) % count) for i in range(count)])  53.3 us
    dot_general x26, matrix products, pick_columns(): lax.dot_general(data, table, (((1,), (1,)), ((), ())), precision=lax.Prec...  38.9 us
    ppermute x24, starting transfers between devices, extended(): lax.ppermute(head, axis, [((i + 1) % count, i) for i in range(count)])  37.3 us
    all_to_all x2, waiting for transfers between devices, to_tiles(): lax.all_to_all(outgoing, ('lon', 'lat'), split_axis=1, concat_axis=1, til...  34.9 us
    ppermute x24, waiting for transfers between devices, extended(): lax.ppermute(head, axis, [((i + 1) % count, i) for i in range(count)])  30.4 us
  transfers between devices with their start and end apart: 63, of which 50 were waited for; matrix products, arithmetic and copies ran while one was open for 9% of the time, Pallas kernels for 0%

commit v1 on v0

v1 whole, which is shorter than its diff:
```python
import jax
import jax.numpy as jnp
from jax import lax
from jax.experimental import pallas as pl
from jax.experimental.pallas import tpu as pltpu
from jax.sharding import PartitionSpec as P

B = 32
BX_DEV = 16
BY_DEV = 16
ITERS = 6
LANES = 128
CORIOLIS = 0.5
HALO = 6
FIELDS = 7
ROWS = BX_DEV * B
COLS = BY_DEV * B
WIDE = COLS + LANES
RIM = 4 * (FIELDS + 2)
GROUPS = ROWS // 8 + 2
CHUNK = 24
TAIL = CHUNK + 8


def lane_ids(shape):
    return lax.broadcasted_iota(jnp.int32, shape, len(shape) - 1)


def row_ids(shape):
    return lax.broadcasted_iota(jnp.int32, shape, len(shape) - 2)


def swap_groups(parts):
    lane = lane_ids((8, LANES))
    low = lane < 64
    even = (lane // 32) % 2 == 0
    lo, hi = [], []
    for p in range(2):
        lo.append(jnp.where(low, parts[p], pltpu.roll(parts[p + 2], 64, 1)))
        hi.append(jnp.where(low, pltpu.roll(parts[p], 64, 1), parts[p + 2]))
    out = []
    for pair in (lo, hi):
        out.append(jnp.where(even, pair[0], pltpu.roll(pair[1], 32, 1)))
        out.append(jnp.where(even, pltpu.roll(pair[0], 96, 1), pair[1]))
    return out


def pack_kernel(pos_ref, vel_ref, str_ref, mass_ref, strength_ref, out_ref, scr_ref):
    slots = vel_ref.shape[-1]

    def turn(field, load):
        for s in range(8):
            rows = jnp.concatenate([load(8 * q + s) for q in range(4)], axis=0)
            scr_ref[field, pl.ds(s, slots, stride=8), :] = rows.T

    for c in range(2):
        turn(c, lambda ci, c=c: vel_ref[c, ci])
    for c in range(3):
        turn(2 + c, lambda ci, c=c: str_ref[c, ci])
    turn(5, lambda ci: mass_ref[ci])
    turn(6, lambda ci: strength_ref[ci])

    def scatter(slot, carry):
        place = pos_ref[slot]
        for field in range(FIELDS):
            out_ref[place, field] = scr_ref[field, pl.ds(pl.multiple_of(slot * 8, 8), 8), :]
        return carry

    lax.fori_loop(0, slots, scatter, 0, unroll=4)


def block_of(tile_ref, recv_ref, bx, by, half, field):
    number = tile_ref[bx, by]
    source = number & (recv_ref.shape[0] // 2 - 1)
    value = recv_ref[source * 2 + half, field]
    return jnp.where(number >= 0, value, 0.0)


def strips_kernel(tile_ref, recv_ref, force_ref, north_ref, south_ref, east_ref, west_ref):
    lane = lane_ids((8, LANES))
    in_group = lane % 32

    for bx, ref, group in ((0, east_ref, 0), (BX_DEV - 1, west_ref, 3)):
        for part in range(4):
            cols = pl.ds(part * LANES, LANES)
            for field in range(FIELDS):
                total = jnp.zeros((8, LANES), jnp.float32)
                for p in range(4):
                    got = block_of(tile_ref, recv_ref, bx, part * 4 + p, int(bx >= 8), field)
                    turned = pltpu.roll(got, ((p - group) * 32) % LANES, 1) if p != group else got
                    total = jnp.where(lane // 32 == p, turned, total)
                ref[field * 4 + part] = total
            for c in range(2):
                ref[(FIELDS + c) * 4 + part] = force_ref[c, pl.ds(bx * B + group * 8, 8), cols]

    def lat_rims(half):
        def body(bx, carry):
            for by, ref, first in ((0, north_ref, 0), (BY_DEV - 1, south_ref, B - HALO)):
                for v in range(2):
                    total = jnp.zeros((8, LANES), jnp.float32)
                    for k in range(5):
                        field = v * 5 + k
                        if field >= FIELDS + 2:
                            continue
                        mine = (in_group >= HALO * k) & (in_group < HALO * (k + 1))
                        if field < FIELDS:
                            got = block_of(tile_ref, recv_ref, bx, by, half, field)
                            got = pltpu.roll(got, (HALO * k - first) % LANES, 1)
                            total = jnp.where(mine, got, total)
                        else:
                            col = (by // 4) * LANES
                            lead = (by % 4) * 32 + first
                            for q in range(4):
                                rows = pl.ds(pl.multiple_of(bx * B + q * 8, 8), 8)
                                got = force_ref[field - FIELDS, rows, pl.ds(col, LANES)]
                                got = pltpu.roll(got, (q * 32 + HALO * k - lead) % LANES, 1)
                                total = jnp.where(mine & (lane // 32 == q), got, total)
                    ref[bx, v] = total
            return carry

        return body

    lax.fori_loop(0, BX_DEV // 2, lat_rims(0), 0)
    lax.fori_loop(BX_DEV // 2, BX_DEV, lat_rims(1), 0)


def tile_kernel(
    tile_ref,
    lat_ref,
    recv_ref,
    force_ref,
    north_ref,
    south_ref,
    east_ref,
    west_ref,
    vel_out_ref,
    send_out_ref,
    z_ref,
    m_ref,
    p_ref,
    q_ref,
    s_ref,
    a_ref,
    b_ref,
    fx_ref,
    fy_ref,
    w_ref,
    send_ref,
    sems,
):
    lane = lane_ids((8, LANES))
    count = recv_ref.shape[0] // 2
    states = (z_ref, m_ref, p_ref, q_ref, s_ref)

    def prepare(row, cols, zonal, merid, total, diff, shear, mass, strength, fzonal, fmerid):
        drag = jnp.where(mass > 0.0, 0.5 / (mass + 0.5), 0.0)
        rows = pl.ds(row, 8)
        z_ref[rows, cols] = zonal
        m_ref[rows, cols] = merid
        p_ref[rows, cols] = 0.5 * (total + diff)
        q_ref[rows, cols] = 0.5 * (total - diff)
        s_ref[rows, cols] = shear
        a_ref[rows, cols] = 2.0 * mass * drag
        b_ref[rows, cols] = drag
        fx_ref[rows, cols] = drag * fzonal
        fy_ref[rows, cols] = drag * fmerid
        w_ref[rows, cols] = 0.25 * strength

    def unpack(half):
        def body(bx, carry):
            for part in range(4):
                cols = pl.ds(part * LANES, LANES)
                numbers = [tile_ref[bx, part * 4 + p] for p in range(4)]
                sources = [(n & (count - 1)) * 2 + half for n in numbers]
                fields = []
                for field in range(FIELDS):
                    got = [
                        jnp.where(numbers[p] >= 0, recv_ref[sources[p], field], 0.0)
                        for p in range(4)
                    ]
                    fields.append(swap_groups(got))
                for q in range(4):
                    row = pl.multiple_of(bx * B + q * 8, 8)
                    force = [force_ref[c, pl.ds(row, 8), cols] for c in range(2)]
                    prepare(
                        pl.multiple_of(row + 16, 8), cols, *[field[q] for field in fields], *force
                    )
            return carry

        return body

    lax.fori_loop(0, BX_DEV // 2, unpack(0), 0)
    lax.fori_loop(BX_DEV // 2, BX_DEV, unpack(1), 0)

    side = pl.ds(COLS, LANES)
    is_north = lane < HALO
    is_south = lane >= LANES - HALO

    def side_columns(bx, carry):
        for q in range(4):
            fields = []
            for field in range(FIELDS + 2):
                v, k = divmod(field, 5)
                lead = q * 32 + HALO * k
                north = pltpu.roll(north_ref[bx, v], (-lead) % LANES, 1)
                south = pltpu.roll(south_ref[bx, v], (LANES - HALO - lead) % LANES, 1)
                fields.append(jnp.where(is_north, north, jnp.where(is_south, south, 0.0)))
            prepare(pl.multiple_of(bx * B + q * 8 + 16, 8), side, *fields)
        return carry

    lax.fori_loop(0, BX_DEV, side_columns, 0)

    for ref, row, group in ((west_ref, 8, 3), (east_ref, ROWS + 16, 0)):
        for part in range(4):
            cols = pl.ds(part * LANES, LANES)
            prepare(row, cols, *[ref[field * 4 + part] for field in range(FIELDS + 2)])
        fields = []
        for field in range(FIELDS + 2):
            v, k = divmod(field, 5)
            lead = group * 32 + HALO * k
            north = pltpu.roll(ref[RIM + v], (-lead) % LANES, 1)
            south = pltpu.roll(ref[RIM + 2 + v], (LANES - HALO - lead) % LANES, 1)
            fields.append(jnp.where(is_north, north, jnp.where(is_south, south, 0.0)))
        prepare(row, side, *fields)

    for ref in states + (w_ref,):
        ref[pl.ds(0, 8), :] = jnp.zeros((8, WIDE), jnp.float32)
        ref[pl.ds(ROWS + 24, TAIL), :] = jnp.zeros((TAIL, WIDE), jnp.float32)

    wide_lane = lane_ids((1, WIDE))
    cell = jnp.where(wide_lane < COLS + 8, wide_lane, wide_lane - WIDE) + lat_ref[0] * COLS
    half_coriolis = (0.5 * CORIOLIS) * (
        2.0 * (cell.astype(jnp.float32) + 0.5) / (lat_ref[1] * COLS).astype(jnp.float32) - 1.0
    )
    sub = row_ids((CHUNK, WIDE))
    first_row = sub == 0
    last_row = sub == CHUNK - 1

    def stress_part(row):
        here = pl.ds(row, CHUNK)
        after = pl.ds(pl.multiple_of(row + CHUNK, 8), 8)
        z, m, w = z_ref[here, :], m_ref[here, :], w_ref[here, :]
        p, q, s = p_ref[here, :], q_ref[here, :], s_ref[here, :]
        z_next, m_next = z_ref[after, :], m_ref[after, :]

        def east(x, follow):
            return pltpu.roll(jnp.where(first_row, jnp.broadcast_to(follow[:1], x.shape), x), CHUNK - 1, 0)

        def run():
            gx = east(z, z_next) - z
            hx = east(m, m_next) - m
            gy = pltpu.roll(m, WIDE - 1, 1) - m
            hy = pltpu.roll(z, WIDE - 1, 1) - z
            div = gx + gy
            ten = gx - gy
            she = hy + hx
            weight = w * lax.rsqrt(div * div + 0.25 * (ten * ten + she * she) + 0.25)
            quarter = 0.25 * weight
            mean = weight * div - w
            dev = quarter * ten
            return 0.5 * p + (mean + dev), 0.5 * q + (mean - dev), 0.5 * s + quarter * she

        def keep(values):
            p_ref[here, :], q_ref[here, :], s_ref[here, :] = values

        return run, keep

    def momentum_part(row):
        here = pl.ds(row, CHUNK)
        before = pl.ds(pl.multiple_of(row - 8, 8), 8)
        z, m, a, b = z_ref[here, :], m_ref[here, :], a_ref[here, :], b_ref[here, :]
        p, q, s = p_ref[here, :], q_ref[here, :], s_ref[here, :]
        fx, fy = fx_ref[here, :], fy_ref[here, :]
        p_last, s_last = p_ref[before, :], s_ref[before, :]

        def west(x, lead):
            return pltpu.roll(jnp.where(last_row, jnp.broadcast_to(lead[7:], x.shape), x), 1, 0)

        def run():
            push_x = (p - west(p, p_last)) + (s - pltpu.roll(s, 1, 1))
            push_y = (s - west(s, s_last)) + (q - pltpu.roll(q, 1, 1))
            turn = a * half_coriolis
            return a * z + b * push_x + fx + turn * m, a * m + b * push_y + fy - turn * z

        def keep(values):
            z_ref[here, :], m_ref[here, :] = values

        return run, keep

    def sweep(step, carry):
        run, keep = stress_part(8)
        keep(run())

        def body(c, carry):
            row = pl.multiple_of(8 + c * CHUNK, 8)
            run_stress, keep_stress = stress_part(pl.multiple_of(row + CHUNK, 8))
            run_momentum, keep_momentum = momentum_part(row)
            stresses = run_stress()
            velocities = run_momentum()
            keep_stress(stresses)
            keep_momentum(velocities)
            return carry

        return lax.fori_loop(0, 8 * GROUPS // CHUNK, body, carry)

    lax.fori_loop(0, ITERS, sweep, 0)

    copies = [
        pltpu.make_async_copy(
            ref.at[pl.ds(16, ROWS), pl.ds(0, COLS)], vel_out_ref.at[c], sems.at[c]
        )
        for c, ref in enumerate((z_ref, m_ref))
    ]
    for copy in copies:
        copy.start()

    def repack(half):
        def body(bx, carry):
            for part in range(4):
                cols = pl.ds(part * LANES, LANES)
                fields = ([], [], [])
                for q in range(4):
                    rows = pl.ds(pl.multiple_of(bx * B + q * 8 + 16, 8), 8)
                    pv, qv = p_ref[rows, cols], q_ref[rows, cols]
                    fields[0].append(pv + qv)
                    fields[1].append(pv - qv)
                    fields[2].append(s_ref[rows, cols])
                fields = [swap_groups(field) for field in fields]
                for p in range(4):
                    number = tile_ref[bx, part * 4 + p]
                    place = jnp.where(number >= 0, (number & (count - 1)) * 2 + half, 2 * count)
                    for c in range(3):
                        send_ref[place, c] = fields[c][p]
            return carry

        return body

    lax.fori_loop(0, BX_DEV // 2, repack(0), 0)
    lax.fori_loop(BX_DEV // 2, BX_DEV, repack(1), 0)
    last = pltpu.make_async_copy(send_ref.at[pl.ds(0, 2 * count)], send_out_ref, sems.at[2])
    last.start()
    for copy in copies + [last]:
        copy.wait()


def unpack_kernel(pos_ref, recv_ref, out_ref, scr_ref):
    slots = out_ref.shape[-1]

    def gather(slot, carry):
        place = pos_ref[slot]
        for c in range(3):
            scr_ref[c, pl.ds(pl.multiple_of(slot * 8, 8), 8), :] = recv_ref[place, c]
        return carry

    lax.fori_loop(0, slots, gather, 0, unroll=4)
    for c in range(3):
        for s in range(8):
            turned = scr_ref[c, pl.ds(s, slots, stride=8), :].T
            for q in range(4):
                out_ref[c, 8 * q + s] = turned[q * B : (q + 1) * B]


VMEM = pl.BlockSpec(memory_space=pltpu.VMEM)
SMEM = pl.BlockSpec(memory_space=pltpu.SMEM)
ANY = pl.BlockSpec(memory_space=pl.ANY)


def params(mebibytes):
    return pltpu.CompilerParams(vmem_limit_bytes=mebibytes * 1024 * 1024)


def f32(*shape):
    return jax.ShapeDtypeStruct(shape, jnp.float32)


def on_device(forcing, velocity, stress, mass, strength, owner):
    lon_count = lax.axis_size("lon")
    lat_count = lax.axis_size("lat")
    devices = lon_count * lat_count
    lat_index = lax.axis_index("lat")
    lon_index = lax.axis_index("lon")
    own_index = lon_index * lat_count + lat_index
    slots = velocity.shape[-1]

    iced = (owner >= 0).astype(jnp.int32)
    counts = jnp.sum(iced.reshape(lon_count, 2, BX_DEV // 2, lat_count, BY_DEV), axis=(2, 4))
    ends = jnp.cumsum(counts.transpose(0, 2, 1).reshape(-1))
    numbers = jnp.arange(slots, dtype=jnp.int32) * devices + own_index
    pos = jnp.sum((ends[None, :] <= numbers[:, None]).astype(jnp.int32), axis=1)
    my_tile = lax.dynamic_slice(owner, (lon_index * BX_DEV, lat_index * BY_DEV), (BX_DEV, BY_DEV))

    send = pl.pallas_call(
        pack_kernel,
        out_shape=f32(devices * 2, FIELDS, 8, LANES),
        in_specs=[SMEM] + [VMEM] * 4,
        out_specs=VMEM,
        scratch_shapes=[pltpu.VMEM((FIELDS, slots * 8, LANES), jnp.float32)],
        compiler_params=params(24),
    )(pos, velocity, stress, mass, strength)
    recv = lax.all_to_all(
        send.reshape(devices, 2 * FIELDS, 8, LANES), ("lon", "lat"), 0, 0, tiled=True
    ).reshape(devices * 2, FIELDS, 8, LANES)

    north, south, east, west = pl.pallas_call(
        strips_kernel,
        out_shape=(f32(BX_DEV, 2, 8, LANES),) * 2 + (f32(RIM, 8, LANES),) * 2,
        in_specs=[SMEM, VMEM, VMEM],
        out_specs=(VMEM,) * 4,
        compiler_params=params(16),
    )(my_tile, recv, forcing)

    ahead = [(j, j + 1) for j in range(lat_count - 1)]
    got_north = lax.ppermute(north, "lat", [(k, j) for j, k in ahead])
    got_south = lax.ppermute(south, "lat", ahead)
    ring = [(i, (i + 1) % lon_count) for i in range(lon_count)]
    east = jnp.concatenate((east, got_north[0], got_south[0]), axis=0)
    west = jnp.concatenate((west, got_north[-1], got_south[-1]), axis=0)
    got_east = lax.ppermute(east, "lon", [(k, i) for i, k in ring])
    got_west = lax.ppermute(west, "lon", ring)
    work = pltpu.VMEM((ROWS + 24 + TAIL, WIDE), jnp.float32)
    new_velocity, back = pl.pallas_call(
        tile_kernel,
        out_shape=(f32(2, ROWS, COLS), f32(devices * 2, 3, 8, LANES)),
        in_specs=[SMEM, SMEM] + [VMEM] * 6,
        out_specs=(ANY, ANY),
        scratch_shapes=[work] * 10
        + [
            pltpu.VMEM((devices * 2 + 1, 3, 8, LANES), jnp.float32),
            pltpu.SemaphoreType.DMA((3,)),
        ],
        compiler_params=params(40),
    )(
        my_tile,
        jnp.stack((lat_index, lat_count)).astype(jnp.int32),
        recv,
        forcing,
        got_north,
        got_south,
        got_east,
        got_west,
    )
    returned = lax.all_to_all(
        back.reshape(devices, 6, 8, LANES), ("lon", "lat"), 0, 0, tiled=True
    ).reshape(devices * 2, 3, 8, LANES)
    new_stress = pl.pallas_call(
        unpack_kernel,
        out_shape=f32(3, B, B, slots),
        in_specs=[SMEM, VMEM],
        out_specs=VMEM,
        scratch_shapes=[pltpu.VMEM((3, slots * 8, LANES), jnp.float32)],
        compiler_params=params(16),
    )(pos, returned)
    return (new_velocity, new_stress)


def solution(mesh):
    in_specs = (
        P(None, "lon", "lat"),
        P(None, None, None, ("lon", "lat")),
        P(None, None, None, ("lon", "lat")),
        P(None, None, ("lon", "lat")),
        P(None, None, ("lon", "lat")),
        P(),
    )
    out_specs = (P(None, "lon", "lat"), P(None, None, None, ("lon", "lat")))
    return jax.shard_map(
        on_device, mesh=mesh, in_specs=in_specs, out_specs=out_specs, check_vma=False
    )
```

time: 887 us -> 239 us (0.27); the launches traced: 875 us -> 239 us
  local copies, waits for them, and re-layouts: 193 us -> 7.66 us
  waiting for transfers between devices: 227 us -> 95.2 us
  starting transfers between devices: 141 us -> 22.6 us
  blocking collectives: 163 us -> 47.8 us
  other arithmetic: 87.8 us -> 3.63 us
  Pallas kernels: 0 us -> 61.2 us
  matrix products: 59.4 us -> 0 us
    all_to_all x11 -> x1, blocking collectives: 163 us -> 47.8 us  [on_device(): lax.all_to_all(back.reshape(devices, 6, 8, LANES), ('lon', 'lat'), 0, 0,...]
    all_to_all x15 -> x1, starting transfers between devices: 97.9 us -> 11.9 us  [on_device(): lax.all_to_all(send.reshape(devices, 2 * FIELDS, 8, LANES), ('lon', 'lat'...]
    reshape x39 -> x2, local copies, waits for them, and re-layouts: 81.4 us -> 1.42 us  [the longest x1 1.29 us: on_device(): iced.reshape(lon_count, 2, BX_DEV // 2, lat_count, BY_DEV)]
    ppermute x48 -> x4, waiting for transfers between devices: 83.8 us -> 9.32 us  [the longest x1 5.31 us: on_device(): got_west = lax.ppermute(west, 'lon', ring)]
    pallas_call x0 -> x4, Pallas kernels: none -> 61.2 us  [the longest x1 51.8 us: on_device(): pl.pallas_call(tile_kernel, out_shape=(f32(2, ROWS, COLS), f32(devices *...]
    dot_general x52 -> x0, matrix products: 59.4 us -> none  [the longest x26 38.9 us: pick_columns(): lax.dot_general(data, table, (((1,), (1,)), ((), ())), precision=lax.Prec...]
    all_to_all x15 -> x1, waiting for transfers between devices: 143 us -> 85.9 us  [on_device(): lax.all_to_all(send.reshape(devices, 2 * FIELDS, 8, LANES), ('lon', 'lat'...]
    dot_general x44 -> x0, local copies, waits for them, and re-layouts: 48.7 us -> none  [the longest x19 25.3 us: pick_columns(): lax.dot_general(data, table, (((1,), (1,)), ((), ())), precision=lax.Prec...]
  transfers between devices with their start and end apart: 63 -> 5, of which waited for: 50 -> 5; matrix products, arithmetic and copies ran while one was open for 9% -> 0% of each run, Pallas kernels for 0% -> 0%
where the time goes in v1:
time: 239 us
  waiting for transfers between devices  95.2 us (40%)
  Pallas kernels  61.2 us (26%)
  blocking collectives  47.8 us (20%)
  starting transfers between devices  22.6 us (9%)
  local copies, waits for them, and re-layouts  7.66 us (3%)
  other arithmetic  3.63 us (2%)
    all_to_all x1, waiting for transfers between devices, on_device(): lax.all_to_all(send.reshape(devices, 2 * FIELDS, 8, LANES), ('lon', 'lat'...  85.9 us
    pallas_call x1, Pallas kernels, on_device(): pl.pallas_call(tile_kernel, out_shape=(f32(2, ROWS, COLS), f32(devices *...  51.8 us
    all_to_all x1, blocking collectives, on_device(): lax.all_to_all(back.reshape(devices, 6, 8, LANES), ('lon', 'lat'), 0, 0,...  47.8 us
    all_to_all x1, starting transfers between devices, on_device(): lax.all_to_all(send.reshape(devices, 2 * FIELDS, 8, LANES), ('lon', 'lat'...  11.9 us
    ppermute x1, waiting for transfers between devices, on_device(): got_west = lax.ppermute(west, 'lon', ring)  5.31 us
    unnamed x12, local copies, waits for them, and re-layouts  5.1 us
    pallas_call x1, Pallas kernels, on_device(): pl.pallas_call(strips_kernel, out_shape=(f32(BX_DEV, 2, 8, LANES),) * 2 +...  4.92 us
  transfers between devices with their start and end apart: 5, of which 5 were waited for; matrix products, arithmetic and copies ran while one was open for 0% of the time, Pallas kernels for 0%

profile of v1, /device:TPU:1, one launch (start us, length us, event | category | flops | bytes accessed | tf_op | source)
XLA Modules:
  0.0 238.8 jit_solution(11215547803372842815)
XLA Ops:
  0.6 0.0 copy-start.2
  0.6 0.0 copy-start.3
  0.7 1.1 compare_convert_fusion
  1.7 1.3 reshape.62
  3.0 1.9 reduce_sum.18
  4.9 0.2 copy.9
  5.1 0.1 reshape.55
  5.2 0.3 reduce-window.9
  5.5 0.1 slice.19
  5.6 0.1 slice_reduce_fusion
  5.7 0.1 add_bitcast_fusion
  5.8 0.2 convert_reduce_fusion.pos_ref
  6.0 0.0 copy-done.2
  6.0 0.0 copy-done.3
  6.0 0.0 copy-start.4
  6.0 1.0 copy-done.4
  7.1 0.0 copy-start.5
  7.1 1.0 copy-done.5
  8.1 2.0 shard_map.77
  10.1 0.0 copy-start
  10.1 3.0 %copy-done = f32[256,7,8,128]{3,2,1,0:T(8,128)} copy-done((f32[256,7,8,128]{3,2,1,0:T(8,128)}, f32[256,7,8,128]{3,2,1,0:T(8,128)S(1)}, u32[]{:S(2)}) %copy-start) | copy-done | bytes 7340056
  13.1 0.0 copy-start.1
  13.1 11.9 %all-to-all-start = ((f32[128,14,8,128]{3,2,1,0:T(8,128)}), f32[128,14,8,128]{3,2,1,0:T(8,128)}, u32[]{:S(2)}, u32[]{:S(2)}) async-start(f32[128,14,8,128]{3,2,1,0:T(8,128)} %bitcast.16), calls=%async_computation | async-start | bytes 14680064 | tf_op jit(solution)/shard_map/all_to_all | solution.py:400
  25.0 0.8 dynamic_slice.3.tile_ref
  25.8 85.9 %all-to-all-done = f32[128,14,8,128]{3,2,1,0:T(8,128)} async-done(((f32[128,14,8,128]{3,2,1,0:T(8,128)}), f32[128,14,8,128]{3,2,1,0:T(8,128)}, u32[]{:S(2)}, u32[]{:S(2)}) %all-to-all-start) | async-done | bytes 7340064 | tf_op jit(solution)/shard_map/all_to_all | solution.py:400
  111.7 0.0 copy-done.1
  111.7 4.9 %shard_map.78 = (f32[16,2,8,128]{3,2,1,0:T(8,128)S(1)}, f32[16,2,8,128]{3,2,1,0:T(8,128)S(1)}, f32[36,8,128]{2,1,0:T(8,128)S(1)}, f32[36,8,128]{2,1,0:T(8,128)S(1)}) custom-call(s32[16,16]{1,0:T(8,128)S(1)} %dynamic_slice.3.tile_ref, f32[256,7,8,128]{3,2,1,0:T(8,128)} %bitcast.4.recv_ref, f32[2,512,512]{2,1,0:T(8,128)S(1)} %copy-done.1), custom_call_target="tpu_custom_call" | custom-call | tf_op jit(solution)/shard_map/pallas_call | solution.py:404
  116.7 2.8 %collective-permute-start = (f32[16,2,8,128]{3,2,1,0:T(8,128)S(1)}, f32[16,2,8,128]{3,2,1,0:T(8,128)S(1)}, u32[]{:S(2)}, u32[]{:S(2)}) collective-permute-start(f32[16,2,8,128]{3,2,1,0:T(8,128)S(1)} %get-tuple-element.8), channel_id=1, source_target_pairs={{1,0},{2,1},{3,2},{4,3},{5,4},{6,5},{7,6},{9,8},{10,9},{11,10},{12... | collective-permute-start | bytes 393224 | tf_op jit(solution)/shard_map/ppermute | solution.py:413
  119.5 3.8 %collective-permute-start.1 = (f32[16,2,8,128]{3,2,1,0:T(8,128)S(1)}, f32[16,2,8,128]{3,2,1,0:T(8,128)S(1)}, u32[]{:S(2)}, u32[]{:S(2)}) collective-permute-start(f32[16,2,8,128]{3,2,1,0:T(8,128)S(1)} %get-tuple-element.9), channel_id=1, source_target_pairs={{0,1},{1,2},{2,3},{3,4},{4,5},{5,6},{6,7},{8,9},{9,10},{10,11},{11... | collective-permute-start | bytes 393224 | tf_op jit(solution)/shard_map/ppermute | solution.py:414
  123.3 0.7 collective-permute-done.north_ref
  124.0 1.2 collective-permute-done.1.south_ref
  125.2 4.0 %collective-permute-start.2 = (f32[40,8,128]{2,1,0:T(8,128)S(1)}, f32[40,8,128]{2,1,0:T(8,128)S(1)}, u32[]{:S(2)}, u32[]{:S(2)}) collective-permute-start(f32[40,8,128]{2,1,0:T(8,128)S(1)} %pad_maximum_fusion), channel_id=1, source_target_pairs={{8,0},{16,8},{24,16},{32,24},{40,32},{48,40},{56,48},{64,56},{72,6... | collective-permute-start | bytes 491528 | tf_op jit(solution)/shard_map/ppermute | solution.py:418
  129.2 0.1 collective-permute-start.3
  129.3 0.1 pad_add_fusion.lat_ref
  129.4 2.1 collective-permute-done.2.east_ref
  131.5 5.3 %collective-permute-done.3.west_ref = f32[40,8,128]{2,1,0:T(8,128)S(1)} collective-permute-done((f32[40,8,128]{2,1,0:T(8,128)S(1)}, f32[40,8,128]{2,1,0:T(8,128)S(1)}, u32[]{:S(2)}, u32[]{:S(2)}) %collective-permute-start.3) | collective-permute-done | bytes 163872 | tf_op jit(solution)/shard_map/ppermute | solution.py:419
  136.8 51.8 %shard_map.79 = (f32[2,512,512]{2,1,0:T(8,128)}, f32[256,3,8,128]{3,2,1,0:T(8,128)S(1)}) custom-call(s32[16,16]{1,0:T(8,128)S(1)} %dynamic_slice.3.tile_ref, s32[2]{0:T(128)S(1)} %pad_add_fusion.lat_ref, f32[256,7,8,128]{3,2,1,0:T(8,128)} %bitcast.4.recv_ref, f32[2,512,512]{2,1,0:T(8,128)S(1)} %copy-done.1, ...), custom_call_target="tpu_custom_call" | custom-call | tf_op jit(solution)/shard_map/pallas_call | solution.py:421
  188.6 47.8 %all_to_all.10 = f32[128,6,8,128]{3,2,1,0:T(8,128)S(1)} all-to-all(f32[128,6,8,128]{3,2,1,0:T(8,128)S(1)} %bitcast.18), channel_id=1, replica_groups=mesh['lon'=16,'lat'=8] {'lon','lat'}, dimensions={0} | all-to-all | bytes 6291456 | tf_op jit(solution)/shard_map/all_to_all | solution.py:442
  236.4 2.5 %shard_map.80 = f32[3,32,32,128]{3,2,1,0:T(8,128)} custom-call(s32[128]{0:T(128)S(1)} %convert_reduce_fusion.pos_ref, f32[256,3,8,128]{3,2,1,0:T(8,128)S(1)} %bitcast.17), custom_call_target="tpu_custom_call" | custom-call | tf_op jit(solution)/shard_map/pallas_call | solution.py:445
  (6 shorter events, 0.1 us)
Async XLA Ops:
  0.6 5.4 %copy-start.2 = (f32[3,32,32,128]{3,2,1,0:T(8,128)S(1)}, f32[3,32,32,128]{3,2,1,0:T(8,128)}, u32[]{:S(2)}) copy-start(f32[3,32,32,128]{3,2,1,0:T(8,128)} %str_ref.1) | copy-start | bytes 4718596
  0.6 5.4 %copy-start.3 = (f32[2,32,32,128]{3,2,1,0:T(8,128)S(1)}, f32[2,32,32,128]{3,2,1,0:T(8,128)}, u32[]{:S(2)}) copy-start(f32[2,32,32,128]{3,2,1,0:T(8,128)} %vel_ref.1) | copy-start | bytes 3145732
  6.0 1.0 copy-start.4
  7.1 1.0 copy-start.5
  10.1 3.0 %copy-start = (f32[256,7,8,128]{3,2,1,0:T(8,128)}, f32[256,7,8,128]{3,2,1,0:T(8,128)S(1)}, u32[]{:S(2)}) copy-start(f32[256,7,8,128]{3,2,1,0:T(8,128)S(1)} %shard_map.77) | copy-start | bytes 22020100
  13.1 98.6 %copy-start.1 = (f32[2,512,512]{2,1,0:T(8,128)S(1)}, f32[2,512,512]{2,1,0:T(8,128)}, u32[]{:S(2)}) copy-start(f32[2,512,512]{2,1,0:T(8,128)} %force_ref.3) | copy-start | bytes 6291460
  13.1 98.6 %all-to-all-start = ((f32[128,14,8,128]{3,2,1,0:T(8,128)}), f32[128,14,8,128]{3,2,1,0:T(8,128)}, u32[]{:S(2)}, u32[]{:S(2)}) async-start(f32[128,14,8,128]{3,2,1,0:T(8,128)} %bitcast.16), calls=%async_computation | async-start | bytes 14680064 | tf_op jit(solution)/shard_map/all_to_all | solution.py:400
  116.7 7.3 %collective-permute-start = (f32[16,2,8,128]{3,2,1,0:T(8,128)S(1)}, f32[16,2,8,128]{3,2,1,0:T(8,128)S(1)}, u32[]{:S(2)}, u32[]{:S(2)}) collective-permute-start(f32[16,2,8,128]{3,2,1,0:T(8,128)S(1)} %get-tuple-element.8), channel_id=1, source_target_pairs={{1,0},{2,1},{3,2},{4,3},{5,4},{6,5},{7,6},{9,8},{10,9},{11,10},{12... | collective-permute-start | bytes 393224 | tf_op jit(solution)/shard_map/ppermute | solution.py:413
  119.5 5.8 %collective-permute-start.1 = (f32[16,2,8,128]{3,2,1,0:T(8,128)S(1)}, f32[16,2,8,128]{3,2,1,0:T(8,128)S(1)}, u32[]{:S(2)}, u32[]{:S(2)}) collective-permute-start(f32[16,2,8,128]{3,2,1,0:T(8,128)S(1)} %get-tuple-element.9), channel_id=1, source_target_pairs={{0,1},{1,2},{2,3},{3,4},{4,5},{5,6},{6,7},{8,9},{9,10},{10,11},{11... | collective-permute-start | bytes 393224 | tf_op jit(solution)/shard_map/ppermute | solution.py:414
  125.2 6.3 %collective-permute-start.2 = (f32[40,8,128]{2,1,0:T(8,128)S(1)}, f32[40,8,128]{2,1,0:T(8,128)S(1)}, u32[]{:S(2)}, u32[]{:S(2)}) collective-permute-start(f32[40,8,128]{2,1,0:T(8,128)S(1)} %pad_maximum_fusion), channel_id=1, source_target_pairs={{8,0},{16,8},{24,16},{32,24},{40,32},{48,40},{56,48},{64,56},{72,6... | collective-permute-start | bytes 491528 | tf_op jit(solution)/shard_map/ppermute | solution.py:418
  129.2 7.6 %collective-permute-start.3 = (f32[40,8,128]{2,1,0:T(8,128)S(1)}, f32[40,8,128]{2,1,0:T(8,128)S(1)}, u32[]{:S(2)}, u32[]{:S(2)}) collective-permute-start(f32[40,8,128]{2,1,0:T(8,128)S(1)} %pad_maximum_fusion.1), channel_id=1, source_target_pairs={{0,8},{8,16},{16,24},{24,32},{32,40},{40,48},{48,56},{56,64},{64,7... | collective-permute-start | bytes 491528 | tf_op jit(solution)/shard_map/ppermute | solution.py:419

commit v2 on v1

v2 whole, which is shorter than its diff:
```python
import jax
import jax.numpy as jnp
import numpy as np
from jax import lax
from jax.experimental import pallas as pl
from jax.experimental.pallas import tpu as pltpu
from jax.sharding import PartitionSpec as P

B = 32
BX_DEV = 16
BY_DEV = 16
ITERS = 6
LANES = 128
CORIOLIS = 0.5
HALO = 6
FIELDS = 7
ROWS = BX_DEV * B
COLS = BY_DEV * B
RIM = 4 * (FIELDS + 2)
SIDE = BX_DEV + 2
GRID_LANES = -(-SIDE * SIDE // LANES) * LANES


def lane_ids(shape):
    return lax.broadcasted_iota(jnp.int32, shape, len(shape) - 1)


def row_ids(shape):
    return lax.broadcasted_iota(jnp.int32, shape, len(shape) - 2)


def swap_groups(parts):
    lane = lane_ids((8, LANES))
    low = lane < 64
    even = (lane // 32) % 2 == 0
    lo, hi = [], []
    for p in range(2):
        lo.append(jnp.where(low, parts[p], pltpu.roll(parts[p + 2], 64, 1)))
        hi.append(jnp.where(low, pltpu.roll(parts[p], 64, 1), parts[p + 2]))
    out = []
    for pair in (lo, hi):
        out.append(jnp.where(even, pair[0], pltpu.roll(pair[1], 32, 1)))
        out.append(jnp.where(even, pltpu.roll(pair[0], 96, 1), pair[1]))
    return out


def grid_rows(bx, by):
    return pl.ds(pl.multiple_of(((bx + 1) * SIDE + by + 1) * 8, 8), 8)


def pack_kernel(
    own_ref,
    owner_ref,
    vel_hbm,
    str_hbm,
    mass_hbm,
    strength_hbm,
    send_ref,
    pos_ref,
    vel_ref,
    str_ref,
    mass_ref,
    strength_ref,
    scr_ref,
    place_ref,
    sems,
):
    slots = vel_ref.shape[-1]
    lon_count = owner_ref.shape[0] // BX_DEV
    lat_count = owner_ref.shape[1] // BY_DEV
    devices = lon_count * lat_count
    fetches = [
        pltpu.make_async_copy(src, dst, sems.at[i])
        for i, (src, dst) in enumerate(
            (
                (vel_hbm, vel_ref),
                (str_hbm, str_ref),
                (mass_hbm, mass_ref),
                (strength_hbm, strength_ref),
            )
        )
    ]
    for fetch in fetches:
        fetch.start()

    half_rows = BX_DEV // 2
    columns = owner_ref.shape[1]

    def dot(x, y):
        return jnp.dot(
            x.astype(jnp.bfloat16), y.astype(jnp.bfloat16), preferred_element_type=jnp.float32
        )

    def square(rows, cols):
        return (
            lax.broadcasted_iota(jnp.int32, (rows, cols), 0),
            lax.broadcasted_iota(jnp.int32, (rows, cols), 1),
        )

    row, col = square(columns, devices)
    of_lat = jnp.where(row // BY_DEV == col % lat_count, 1.0, 0.0)
    iced = jnp.where(owner_ref[...] >= 0, 1.0, 0.0)
    row, col = square(2 * lon_count, owner_ref.shape[0])
    of_half = jnp.where(col // half_rows == row, 1.0, 0.0)
    per_tile = dot(dot(of_half, iced), of_lat)
    row, col = square(2 * lon_count, devices)
    mine = row // 2 == col // lat_count
    counts = [
        jnp.sum(jnp.where(mine & (row % 2 == h), per_tile, 0.0), axis=0, keepdims=True)
        for h in range(2)
    ]
    row, col = square(devices, devices)
    upto = jnp.where(row <= col, 1.0, 0.0)
    both = jnp.broadcast_to(counts[0] + counts[1], (8, devices))
    end_second = dot(both, upto)[:1]
    end_first = end_second - counts[1]
    number = (lax.broadcasted_iota(jnp.int32, (devices, slots), 1) * devices + own_ref[0]).astype(
        jnp.float32
    )
    place = jnp.zeros((1, slots), jnp.float32)
    for end in (end_first, end_second):
        column = jnp.broadcast_to(end, (devices, devices)).T[:, :1]
        place = place + jnp.sum(jnp.where(column <= number, 1.0, 0.0), axis=0, keepdims=True)
    pos_ref[...] = place.astype(jnp.int32)
    to_scalar = pltpu.make_async_copy(pos_ref, place_ref, sems.at[4])
    to_scalar.start()

    def turn(field, load):
        for s in range(8):
            rows = jnp.concatenate([load(8 * q + s) for q in range(4)], axis=0)
            scr_ref[field, pl.ds(s, slots, stride=8), :] = rows.T

    fetches[0].wait()
    for c in range(2):
        turn(c, lambda ci, c=c: vel_ref[c, ci])
    fetches[1].wait()
    for c in range(3):
        turn(2 + c, lambda ci, c=c: str_ref[c, ci])
    fetches[2].wait()
    turn(5, lambda ci: mass_ref[ci])
    fetches[3].wait()
    turn(6, lambda ci: strength_ref[ci])
    to_scalar.wait()

    def scatter(slot, carry):
        spot = place_ref[0, slot]
        rows = pl.ds(pl.multiple_of(slot * 8, 8), 8)
        pltpu.make_async_copy(scr_ref.at[:, rows, :], send_ref.at[spot], sems.at[5]).start()
        return carry

    lax.fori_loop(0, slots, scatter, 0, unroll=4)
    pltpu.make_async_copy(send_ref.at[pl.ds(0, slots)], send_ref.at[pl.ds(0, slots)], sems.at[5]).wait()


def strips_kernel(
    tile_ref,
    recv_hbm,
    force_ref,
    north_ref,
    south_ref,
    east_ref,
    west_ref,
    edge_ref,
    sem,
):
    lane = lane_ids((8, LANES))
    in_group = lane % 32
    count = recv_hbm.shape[0] // 2
    half = BX_DEV // 2

    def fetch(i, carry):
        for side, (bx, by) in enumerate(((i, 0), (i, BY_DEV - 1), (0, i), (BX_DEV - 1, i))):
            source = (tile_ref[bx, by] & (count - 1)) * 2 + jnp.int32(bx >= half)
            pltpu.make_async_copy(recv_hbm.at[source], edge_ref.at[side * BX_DEV + i], sem).start()
        return carry

    lax.fori_loop(0, BX_DEV, fetch, 0)
    pltpu.make_async_copy(recv_hbm.at[pl.ds(0, 4 * BX_DEV)], edge_ref, sem).wait()

    def block_of(side, bx, by, field):
        if field >= FIELDS:
            return force_ref[bx * BY_DEV + by, field - FIELDS]
        value = edge_ref[side * BX_DEV + (bx if side < 2 else by), field]
        return jnp.where(tile_ref[bx, by] >= 0, value, 0.0)

    for side, bx, ref, group in ((2, 0, east_ref, 0), (3, BX_DEV - 1, west_ref, 3)):
        for part in range(4):
            for field in range(FIELDS + 2):
                total = jnp.zeros((8, LANES), jnp.float32)
                for p in range(4):
                    got = block_of(side, bx, part * 4 + p, field)
                    turned = pltpu.roll(got, ((p - group) * 32) % LANES, 1) if p != group else got
                    total = jnp.where(lane // 32 == p, turned, total)
                ref[field * 4 + part] = total

    def lat_rims(bx, carry):
        for side, by, ref, first in (
            (0, 0, north_ref, 0),
            (1, BY_DEV - 1, south_ref, B - HALO),
        ):
            for v in range(2):
                total = jnp.zeros((8, LANES), jnp.float32)
                for k in range(min(5, FIELDS + 2 - v * 5)):
                    mine = (in_group >= HALO * k) & (in_group < HALO * (k + 1))
                    got = block_of(side, bx, by, v * 5 + k)
                    got = pltpu.roll(got, (HALO * k - first) % LANES, 1)
                    total = jnp.where(mine, got, total)
                ref[bx, v] = total
        return carry

    lax.fori_loop(0, BX_DEV, lat_rims, 0)


def collect_kernel(tile_ref, recv_ref, force_ref, scr_ref):
    count = recv_ref.shape[0] // 2
    rest = SIDE * SIDE * 8
    for field in range(FIELDS + 2):
        scr_ref[field, pl.ds(rest, GRID_LANES * 8 - rest), :] = jnp.zeros(
            (GRID_LANES * 8 - rest, LANES), jnp.float32
        )

    def collect(bx, carry):
        half = jnp.int32(bx >= BX_DEV // 2)
        for by in range(BY_DEV):
            number = tile_ref[bx, by]
            source = (number & (count - 1)) * 2 + half
            iced = number >= 0
            for field in range(FIELDS):
                scr_ref[field, grid_rows(bx, by), :] = jnp.where(
                    iced, recv_ref[source, field], 0.0
                )
            for c in range(2):
                scr_ref[FIELDS + c, grid_rows(bx, by), :] = force_ref[bx * BY_DEV + by, c]
        return carry

    lax.fori_loop(0, BX_DEV, collect, 0)


def force_kernel(force_ref, out_ref):
    def body(bx, carry):
        for part in range(4):
            for c in range(2):
                rows = [
                    force_ref[
                        c,
                        pl.ds(pl.multiple_of(bx * B + 8 * q, 8), 8),
                        pl.ds(part * LANES, LANES),
                    ]
                    for q in range(4)
                ]
                for p, block in enumerate(swap_groups(rows)):
                    out_ref[bx * BY_DEV + part * 4 + p, c] = block
        return carry

    lax.fori_loop(0, BX_DEV, body, 0)


def velocity_kernel(vel_ref, out_ref, scr_ref):
    for c in range(2):
        for t in range(GRID_LANES // LANES):
            for s in range(8):
                cells = [vel_ref[c, 8 * q + s, :, pl.ds(t * LANES, LANES)] for q in range(4)]
                scr_ref[c, pl.ds(t * 8 * LANES + s, LANES, stride=8), :] = jnp.concatenate(
                    cells, axis=0
                ).T

    def body(bx, carry):
        for part in range(4):
            for c in range(2):
                blocks = [
                    scr_ref[
                        c,
                        pl.ds(pl.multiple_of(((bx + 1) * SIDE + part * 4 + p + 1) * 8, 8), 8),
                        :,
                    ]
                    for p in range(4)
                ]
                for q, rows in enumerate(swap_groups(blocks)):
                    out_ref[
                        c,
                        pl.ds(pl.multiple_of(bx * B + 8 * q, 8), 8),
                        pl.ds(part * LANES, LANES),
                    ] = rows
        return carry

    lax.fori_loop(0, BX_DEV, body, 0)


def tile_kernel(
    tile_ref,
    lat_ref,
    blocks_ref,
    cell_ref,
    north_ref,
    south_ref,
    east_ref,
    west_ref,
    scr_ref,
    vel_out_ref,
    send_out_ref,
    z_ref,
    m_ref,
    p_ref,
    q_ref,
    s_ref,
    a_ref,
    b_ref,
    fx_ref,
    fy_ref,
    w_ref,
    turn_ref,
    send_ref,
    sems,
):
    del blocks_ref
    lane = lane_ids((8, LANES))
    count = send_out_ref.shape[0] // 2
    tiles = GRID_LANES // LANES
    fields = FIELDS + 2
    spot = grid_rows
    in_group = lane % 32

    def lat_rim(bx, north, south):
        for field in range(fields):
            v, k = divmod(field, 5)
            got = pltpu.roll(north(v), (-HALO * k) % LANES, 1)
            scr_ref[field, spot(bx, BY_DEV), :] = jnp.where(in_group < HALO, got, 0.0)
            got = pltpu.roll(south(v), (B - HALO - HALO * k) % LANES, 1)
            scr_ref[field, spot(bx, -1), :] = jnp.where(in_group >= B - HALO, got, 0.0)

    def lat_rims(bx, carry):
        lat_rim(bx, lambda v: north_ref[bx, v], lambda v: south_ref[bx, v])
        return carry

    lax.fori_loop(0, BX_DEV, lat_rims, 0)
    for ref, bx, group in ((west_ref, -1, 3), (east_ref, BX_DEV, 0)):
        for field in range(fields):
            for part in range(4):
                for p in range(4):
                    got = ref[field * 4 + part]
                    got = pltpu.roll(got, ((group - p) * 32) % LANES, 1)
                    scr_ref[field, spot(bx, part * 4 + p), :] = jnp.where(
                        lane // 32 == group, got, 0.0
                    )
        lat_rim(bx, lambda v: ref[RIM + v], lambda v: ref[RIM + 2 + v])

    def prepare(t, carry):
        cols = pl.ds(pl.multiple_of(t * LANES, LANES), LANES)
        for s in range(8):
            start = pl.multiple_of(t * 8 * LANES, 8 * LANES) + s
            turned = [
                scr_ref[field, pl.ds(start, LANES, stride=8), :].T for field in range(fields)
            ]
            for q in range(4):
                plane = 8 * q + s
                zonal, merid, total, diff, shear, mass, strength, fzonal, fmerid = [
                    x[q * B : (q + 1) * B] for x in turned
                ]
                drag = jnp.where(mass > 0.0, 0.5 / (mass + 0.5), 0.0)
                z_ref[plane + 1, :, cols] = zonal
                m_ref[plane + 1, :, cols] = merid
                p_ref[plane + 1, :, cols] = 0.5 * (total + diff)
                q_ref[plane + 1, :, cols] = 0.5 * (total - diff)
                s_ref[plane + 1, :, cols] = shear
                a_ref[plane, :, cols] = 2.0 * mass * drag
                b_ref[plane, :, cols] = drag
                fx_ref[plane, :, cols] = drag * fzonal
                fy_ref[plane, :, cols] = drag * fmerid
                w_ref[plane, :, cols] = 0.25 * strength
        return carry

    lax.fori_loop(0, tiles, prepare, 0)

    cell = cell_ref[...] + lat_ref[0] * COLS
    turn_ref[...] = (0.5 * CORIOLIS) * (
        2.0 * (cell.astype(jnp.float32) + 0.5) / (lat_ref[1] * COLS).astype(jnp.float32) - 1.0
    )

    sub = row_ids((8, LANES))
    first_row = sub == 0
    last_row = sub == 7

    def north_of(x, edge):
        top = jnp.where(first_row, edge, x[:8])
        return pltpu.roll(jnp.concatenate((top, x[8:]), axis=0), B - 1, 0)

    def south_of(x, edge):
        bottom = jnp.where(last_row, edge, x[B - 8 :])
        return pltpu.roll(jnp.concatenate((x[: B - 8], bottom), axis=0), 1, 0)

    def stress_plane(k):
        z_edge = pltpu.roll(z_ref[k, pl.ds(0, 8), :], GRID_LANES - 1, 1)
        m_edge = pltpu.roll(m_ref[k, pl.ds(0, 8), :], GRID_LANES - 1, 1)
        for t in range(tiles):
            cols = slice(t * LANES, (t + 1) * LANES)
            z, m, w = z_ref[k, :, cols], m_ref[k, :, cols], w_ref[k - 1, :, cols]
            gx = z_ref[k + 1, :, cols] - z
            hx = m_ref[k + 1, :, cols] - m
            gy = north_of(m, m_edge[:, cols]) - m
            hy = north_of(z, z_edge[:, cols]) - z
            div = gx + gy
            ten = gx - gy
            she = hy + hx
            weight = w * lax.rsqrt(div * div + 0.25 * (ten * ten + she * she) + 0.25)
            quarter = 0.25 * weight
            mean = weight * div - w
            dev = quarter * ten
            p_ref[k, :, cols] = 0.5 * p_ref[k, :, cols] + (mean + dev)
            q_ref[k, :, cols] = 0.5 * q_ref[k, :, cols] + (mean - dev)
            s_ref[k, :, cols] = 0.5 * s_ref[k, :, cols] + quarter * she

    def momentum_plane(k):
        s_edge = pltpu.roll(s_ref[k, pl.ds(B - 8, 8), :], 1, 1)
        q_edge = pltpu.roll(q_ref[k, pl.ds(B - 8, 8), :], 1, 1)
        for t in range(tiles):
            cols = slice(t * LANES, (t + 1) * LANES)
            z, m = z_ref[k, :, cols], m_ref[k, :, cols]
            a, b = a_ref[k - 1, :, cols], b_ref[k - 1, :, cols]
            s, q = s_ref[k, :, cols], q_ref[k, :, cols]
            push_x = (p_ref[k, :, cols] - p_ref[k - 1, :, cols]) + (
                s - south_of(s, s_edge[:, cols])
            )
            push_y = (s - s_ref[k - 1, :, cols]) + (q - south_of(q, q_edge[:, cols]))
            turn = a * turn_ref[:, cols]
            z_ref[k, :, cols] = a * z + b * push_x + fx_ref[k - 1, :, cols] + turn * m
            m_ref[k, :, cols] = a * m + b * push_y + fy_ref[k - 1, :, cols] - turn * z

    def sweep(step, carry):
        for ref in (z_ref, m_ref):
            ref[B + 1] = pltpu.roll(ref[1], GRID_LANES - SIDE, 1)
        stress_plane(B)
        for ref in (p_ref, s_ref):
            ref[0] = pltpu.roll(ref[B], SIDE, 1)
        stress_plane(1)

        def body(k, carry):
            stress_plane(k + 1)
            momentum_plane(k)
            return carry

        lax.fori_loop(1, B - 1, body, 0, unroll=True)
        for k in (B - 1, B):
            momentum_plane(k)
        return carry

    lax.fori_loop(0, ITERS, sweep, 0)
    copies = [
        pltpu.make_async_copy(ref.at[pl.ds(1, B)], vel_out_ref.at[c], sems.at[c])
        for c, ref in enumerate((z_ref, m_ref))
    ]
    for copy in copies:
        copy.start()

    def turn_back(t, carry):
        cols = pl.ds(pl.multiple_of(t * LANES, LANES), LANES)
        for s in range(8):
            rows = pl.ds(pl.multiple_of(t * 8 * LANES, 8 * LANES) + s, LANES, stride=8)
            planes = [8 * q + s + 1 for q in range(4)]
            p_all = jnp.concatenate([p_ref[k, :, cols] for k in planes], axis=0)
            q_all = jnp.concatenate([q_ref[k, :, cols] for k in planes], axis=0)
            s_all = jnp.concatenate([s_ref[k, :, cols] for k in planes], axis=0)
            scr_ref[0, rows, :] = (p_all + q_all).T
            scr_ref[1, rows, :] = (p_all - q_all).T
            scr_ref[2, rows, :] = s_all.T
        return carry

    lax.fori_loop(0, tiles, turn_back, 0)

    def deal(half):
        def body(bx, carry):
            for by in range(BY_DEV):
                number = tile_ref[bx, by]
                place = jnp.where(number >= 0, (number & (count - 1)) * 2 + half, 2 * count)
                for c in range(3):
                    send_ref[place, c] = scr_ref[c, spot(bx, by), :]
            return carry

        return body

    lax.fori_loop(0, BX_DEV // 2, deal(0), 0)
    lax.fori_loop(BX_DEV // 2, BX_DEV, deal(1), 0)
    copies.append(
        pltpu.make_async_copy(send_ref.at[pl.ds(0, 2 * count)], send_out_ref, sems.at[2])
    )
    copies[2].start()
    for copy in copies:
        copy.wait()


def unpack_kernel(pos_ref, recv_ref, out_ref, scr_ref):
    slots = out_ref.shape[-1]

    def gather(slot, carry):
        place = pos_ref[0, slot]
        for c in range(3):
            scr_ref[c, pl.ds(pl.multiple_of(slot * 8, 8), 8), :] = recv_ref[place, c]
        return carry

    lax.fori_loop(0, slots, gather, 0, unroll=4)
    for c in range(3):
        for s in range(8):
            turned = scr_ref[c, pl.ds(s, slots, stride=8), :].T
            for q in range(4):
                out_ref[c, 8 * q + s] = turned[q * B : (q + 1) * B]


VMEM = pl.BlockSpec(memory_space=pltpu.VMEM)
SMEM = pl.BlockSpec(memory_space=pltpu.SMEM)
ANY = pl.BlockSpec(memory_space=pl.ANY)
HBM = pl.BlockSpec(memory_space=pltpu.HBM)


def params(mebibytes):
    return pltpu.CompilerParams(vmem_limit_bytes=mebibytes * 1024 * 1024)


def cost(mebibytes):
    return pl.CostEstimate(flops=10**7, bytes_accessed=mebibytes * 2**20, transcendentals=0)


def f32(*shape):
    return jax.ShapeDtypeStruct(shape, jnp.float32)


def on_device(forcing, velocity, stress, mass, strength, owner):
    lon_count = lax.axis_size("lon")
    lat_count = lax.axis_size("lat")
    devices = lon_count * lat_count
    lat_index = lax.axis_index("lat")
    lon_index = lax.axis_index("lon")
    own_index = lon_index * lat_count + lat_index
    slots = velocity.shape[-1]

    my_tile = lax.dynamic_slice(owner, (lon_index * BX_DEV, lat_index * BY_DEV), (BX_DEV, BY_DEV))

    block = (B, B, slots)
    send, pos = pl.pallas_call(
        pack_kernel,
        out_shape=(
            f32(devices * 2, FIELDS, 8, LANES),
            jax.ShapeDtypeStruct((1, slots), jnp.int32),
        ),
        in_specs=[SMEM, VMEM] + [HBM] * 4,
        out_specs=(HBM, VMEM),
        scratch_shapes=[
            pltpu.VMEM((2,) + block, jnp.float32),
            pltpu.VMEM((3,) + block, jnp.float32),
            pltpu.VMEM(block, jnp.float32),
            pltpu.VMEM(block, jnp.float32),
            pltpu.VMEM((FIELDS, slots * 8, LANES), jnp.float32),
            pltpu.SMEM((1, slots), jnp.int32),
            pltpu.SemaphoreType.DMA((6,)),
        ],
        compiler_params=params(61),
    )(own_index.reshape(1).astype(jnp.int32), owner, velocity, stress, mass, strength)
    recv = lax.all_to_all(
        send.reshape(devices, 2 * FIELDS, 8, LANES), ("lon", "lat"), 0, 0, tiled=True
    ).reshape(devices * 2, FIELDS, 8, LANES)

    force_blocks = pl.pallas_call(
        force_kernel,
        out_shape=f32(BX_DEV * BY_DEV, 2, 8, LANES),
        in_specs=[VMEM],
        out_specs=VMEM,
        cost_estimate=cost(4),
        compiler_params=params(12),
    )(forcing)
    north, south, east, west = pl.pallas_call(
        strips_kernel,
        out_shape=(f32(BX_DEV, 2, 8, LANES),) * 2 + (f32(RIM, 8, LANES),) * 2,
        in_specs=[SMEM, HBM, VMEM],
        out_specs=(VMEM,) * 4,
        scratch_shapes=[
            pltpu.VMEM((4 * BX_DEV, FIELDS, 8, LANES), jnp.float32),
            pltpu.SemaphoreType.DMA(()),
        ],
        cost_estimate=cost(4),
        compiler_params=params(10),
    )(my_tile, recv, force_blocks)
    blocks = pl.pallas_call(
        collect_kernel,
        out_shape=f32(FIELDS + 2, GRID_LANES * 8, LANES),
        in_specs=[SMEM, VMEM, VMEM],
        out_specs=VMEM,
        cost_estimate=cost(24),
        compiler_params=params(12),
    )(my_tile, recv, force_blocks)

    ahead = [(j, j + 1) for j in range(lat_count - 1)]
    got_north = lax.ppermute(north, "lat", [(k, j) for j, k in ahead])
    got_south = lax.ppermute(south, "lat", ahead)
    ring = [(i, (i + 1) % lon_count) for i in range(lon_count)]
    east = jnp.concatenate((east, got_north[0], got_south[0]), axis=0)
    west = jnp.concatenate((west, got_north[-1], got_south[-1]), axis=0)
    got_east = lax.ppermute(east, "lon", [(k, i) for i, k in ring])
    got_west = lax.ppermute(west, "lon", ring)
    grid = np.arange(GRID_LANES) % SIDE - 1
    cells = jnp.asarray(grid[None, :] * B + np.arange(B)[:, None], jnp.int32)
    state = (B + 2, B, GRID_LANES)
    constant = (B, B, GRID_LANES)
    _, cell_velocity, back = pl.pallas_call(
        tile_kernel,
        out_shape=(
            f32(FIELDS + 2, GRID_LANES * 8, LANES),
            f32(2, B, B, GRID_LANES),
            f32(devices * 2, 3, 8, LANES),
        ),
        in_specs=[SMEM, SMEM] + [VMEM] * 6,
        out_specs=(VMEM, HBM, ANY),
        input_output_aliases={2: 0},
        scratch_shapes=[pltpu.VMEM(state, jnp.float32)] * 5
        + [pltpu.VMEM(constant, jnp.float32)] * 5
        + [
            pltpu.VMEM((B, GRID_LANES), jnp.float32),
            pltpu.VMEM((devices * 2 + 1, 3, 8, LANES), jnp.float32),
            pltpu.SemaphoreType.DMA((3,)),
        ],
        compiler_params=params(26),
    )(
        my_tile,
        jnp.stack((lat_index, lat_count)).astype(jnp.int32),
        blocks,
        cells,
        got_north,
        got_south,
        got_east,
        got_west,
    )
    returned = lax.all_to_all(
        back.reshape(devices, 6, 8, LANES), ("lon", "lat"), 0, 0, tiled=True
    ).reshape(devices * 2, 3, 8, LANES)
    new_velocity = pl.pallas_call(
        velocity_kernel,
        out_shape=f32(2, ROWS, COLS),
        in_specs=[VMEM],
        out_specs=VMEM,
        scratch_shapes=[pltpu.VMEM((2, GRID_LANES * 8, LANES), jnp.float32)],
        cost_estimate=cost(6),
        compiler_params=params(16),
    )(cell_velocity)
    new_stress = pl.pallas_call(
        unpack_kernel,
        out_shape=f32(3, B, B, slots),
        in_specs=[SMEM, VMEM],
        out_specs=VMEM,
        scratch_shapes=[pltpu.VMEM((3, slots * 8, LANES), jnp.float32)],
        compiler_params=params(16),
    )(pos, returned)
    return (new_velocity, new_stress)


def solution(mesh):
    in_specs = (
        P(None, "lon", "lat"),
        P(None, None, None, ("lon", "lat")),
        P(None, None, None, ("lon", "lat")),
        P(None, None, ("lon", "lat")),
        P(None, None, ("lon", "lat")),
        P(),
    )
    out_specs = (P(None, "lon", "lat"), P(None, None, None, ("lon", "lat")))
    return jax.shard_map(
        on_device, mesh=mesh, in_specs=in_specs, out_specs=out_specs, check_vma=False
    )
```

time: 239 us -> 213 us (0.89)
  blocking collectives: 47.8 us -> 0 us
  waiting for transfers between devices: 95.2 us -> 121 us
  Pallas kernels: 61.2 us -> 52.4 us
  starting transfers between devices: 22.6 us -> 30 us
  other arithmetic: 3.63 us -> 0.1 us
    all_to_all x1 -> x0, blocking collectives: 47.8 us -> none  [on_device(): lax.all_to_all(back.reshape(devices, 6, 8, LANES), ('lon', 'lat'), 0, 0,...]
    all_to_all x0 -> x1, waiting for transfers between devices: none -> 34.7 us  [on_device(): lax.all_to_all(back.reshape(devices, 6, 8, LANES), ('lon', 'lat'), 0, 0,...]
    pallas_call x2 -> x5, Pallas kernels: 53.8 us -> 45.6 us  [the longest x1 27.4 us: on_device(): pl.pallas_call(tile_kernel, out_shape=(f32(FIELDS + 2, GRID_LANES * 8, LA...]
    all_to_all x0 -> x1, starting transfers between devices: none -> 7.86 us  [on_device(): lax.all_to_all(back.reshape(devices, 6, 8, LANES), ('lon', 'lat'), 0, 0,...]
    all_to_all x1, waiting for transfers between devices: 85.9 us -> 81.4 us  [on_device(): lax.all_to_all(send.reshape(devices, 2 * FIELDS, 8, LANES), ('lon', 'lat'...]
  transfers between devices with their start and end apart: 5 -> 6, of which waited for: 5 -> 5; matrix products, arithmetic and copies ran while one was open for 0% -> 0% of each run, Pallas kernels for 0% -> 6%
where the time goes in v2:
time: 213 us; the launch traced here: 212 us
  waiting for transfers between devices  121 us (57%)
  Pallas kernels  52.4 us (25%)
  starting transfers between devices  30 us (14%)
  local copies, waits for them, and re-layouts  7.58 us (4%)
    all_to_all x1, waiting for transfers between devices, on_device(): lax.all_to_all(send.reshape(devices, 2 * FIELDS, 8, LANES), ('lon', 'lat'...  81.4 us
    all_to_all x1, waiting for transfers between devices, on_device(): lax.all_to_all(back.reshape(devices, 6, 8, LANES), ('lon', 'lat'), 0, 0,...  34.7 us
    pallas_call x1, Pallas kernels, on_device(): pl.pallas_call(tile_kernel, out_shape=(f32(FIELDS + 2, GRID_LANES * 8, LA...  27.4 us
    all_to_all x1, starting transfers between devices, on_device(): lax.all_to_all(send.reshape(devices, 2 * FIELDS, 8, LANES), ('lon', 'lat'...  11.9 us
    all_to_all x1, starting transfers between devices, on_device(): lax.all_to_all(back.reshape(devices, 6, 8, LANES), ('lon', 'lat'), 0, 0,...  7.86 us
    unnamed x12, local copies, waits for them, and re-layouts  6.8 us
    pallas_call x1, Pallas kernels, on_device(): pl.pallas_call(pack_kernel, out_shape=(f32(devices * 2, FIELDS, 8, LANES)...  6.02 us
    pallas_call x1, Pallas kernels, on_device(): pl.pallas_call(velocity_kernel, out_shape=f32(2, ROWS, COLS), in_specs=[V...  4.96 us
  transfers between devices with their start and end apart: 6, of which 5 were waited for; matrix products, arithmetic and copies ran while one was open for 0% of the time, Pallas kernels for 6%

profile of v2, /device:TPU:1, one launch (start us, length us, event | category | flops | bytes accessed | tf_op | source)
XLA Modules:
  0.0 211.9 jit_solution(16770843002653104989)
XLA Ops:
  0.6 6.0 %shard_map.86 = (f32[256,7,8,128]{3,2,1,0:T(8,128)}, s32[1,128]{1,0:T(1,128)}) custom-call(s32[1]{0:T(128)} %bitcast.1.own_ref, s32[256,128]{1,0:T(8,128)} %owner_ref.1, f32[2,32,32,128]{3,2,1,0:T(8,128)} %vel_hbm.1, f32[3,32,32,128]{3,2,1,0:T(8,128)} %str_hbm.1, f32[32,32,128]{2,1,0:T(8,128)} %mass_hbm.1, f32[32,32,128]{2,1,0:T(8,128)} %strength_hbm.1), custom_call_target="tpu_custom_call" | custom-call | tf_op jit(solution)/shard_map/pallas_call | solution.py:537
  6.7 11.9 %all-to-all-start = ((f32[128,14,8,128]{3,2,1,0:T(8,128)}), f32[128,14,8,128]{3,2,1,0:T(8,128)}, u32[]{:S(2)}, u32[]{:S(2)}) async-start(f32[128,14,8,128]{3,2,1,0:T(8,128)} %bitcast.16), calls=%async_computation | async-start | bytes 14680064 | tf_op jit(solution)/shard_map/all_to_all | solution.py:556
  18.6 0.8 dynamic_slice.3.tile_ref
  19.4 0.0 copy-start.3
  19.4 1.6 copy-done.3
  21.0 2.9 %shard_map.87.force_ref = f32[256,2,8,128]{3,2,1,0:T(8,128)S(1)} custom-call(f32[2,512,512]{2,1,0:T(8,128)S(1)} %copy-done.3), custom_call_target="tpu_custom_call" | custom-call | flops 10000000 | bytes 4194304 | tf_op jit(solution)/shard_map/pallas_call | solution.py:560
  23.9 81.4 %all-to-all-done = f32[128,14,8,128]{3,2,1,0:T(8,128)} async-done(((f32[128,14,8,128]{3,2,1,0:T(8,128)}), f32[128,14,8,128]{3,2,1,0:T(8,128)}, u32[]{:S(2)}, u32[]{:S(2)}) %all-to-all-start) | async-done | bytes 7340064 | tf_op jit(solution)/shard_map/all_to_all | solution.py:556
  105.3 4.3 %shard_map.89 = (f32[16,2,8,128]{3,2,1,0:T(8,128)S(1)}, f32[16,2,8,128]{3,2,1,0:T(8,128)S(1)}, f32[36,8,128]{2,1,0:T(8,128)S(1)}, f32[36,8,128]{2,1,0:T(8,128)S(1)}) custom-call(s32[16,16]{1,0:T(8,128)S(1)} %dynamic_slice.3.tile_ref, f32[256,7,8,128]{3,2,1,0:T(8,128)} %bitcast.3.recv_ref.recv_hbm, f32[256,2,8,128]{3,2,1,0:T(8,128)S(1)} %shard_map.87.force_ref), custom_call_target="tpu_custom_call" | custom-call | flops 10000000 | bytes 4194304 | tf_op jit(solution)/shard_map/pallas_call | solution.py:568
  109.6 3.1 %collective-permute-start = (f32[16,2,8,128]{3,2,1,0:T(8,128)S(1)}, f32[16,2,8,128]{3,2,1,0:T(8,128)S(1)}, u32[]{:S(2)}, u32[]{:S(2)}) collective-permute-start(f32[16,2,8,128]{3,2,1,0:T(8,128)S(1)} %get-tuple-element.11), channel_id=1, source_target_pairs={{1,0},{2,1},{3,2},{4,3},{5,4},{6,5},{7,6},{9,8},{10,9},{11,10},{12... | collective-permute-start | bytes 393224 | tf_op jit(solution)/shard_map/ppermute | solution.py:590
  112.8 4.1 %collective-permute-start.1 = (f32[16,2,8,128]{3,2,1,0:T(8,128)S(1)}, f32[16,2,8,128]{3,2,1,0:T(8,128)S(1)}, u32[]{:S(2)}, u32[]{:S(2)}) collective-permute-start(f32[16,2,8,128]{3,2,1,0:T(8,128)S(1)} %get-tuple-element.12), channel_id=1, source_target_pairs={{0,1},{1,2},{2,3},{3,4},{4,5},{5,6},{6,7},{8,9},{9,10},{10,11},{11... | collective-permute-start | bytes 393224 | tf_op jit(solution)/shard_map/ppermute | solution.py:591
  116.9 0.7 collective-permute-done.north_ref
  117.7 1.2 collective-permute-done.1.south_ref
  118.9 2.8 %collective-permute-start.2 = (f32[40,8,128]{2,1,0:T(8,128)S(1)}, f32[40,8,128]{2,1,0:T(8,128)S(1)}, u32[]{:S(2)}, u32[]{:S(2)}) collective-permute-start(f32[40,8,128]{2,1,0:T(8,128)S(1)} %pad_maximum_fusion), channel_id=1, source_target_pairs={{8,0},{16,8},{24,16},{32,24},{40,32},{48,40},{56,48},{64,56},{72,6... | collective-permute-start | bytes 491528 | tf_op jit(solution)/shard_map/ppermute | solution.py:595
  121.7 0.1 collective-permute-start.3
  121.8 0.1 pad_add_fusion.lat_ref
  121.9 0.0 copy-start.4
  121.9 4.3 %shard_map.88.blocks_ref = f32[9,3072,128]{2,1,0:T(8,128)S(1)} custom-call(s32[16,16]{1,0:T(8,128)S(1)} %dynamic_slice.3.tile_ref, f32[256,7,8,128]{3,2,1,0:T(8,128)} %bitcast.3.recv_ref.recv_hbm, f32[256,2,8,128]{3,2,1,0:T(8,128)S(1)} %shard_map.87.force_ref), custom_call_target="tpu_custom_call" | custom-call | flops 10000000 | bytes 25165824 | tf_op jit(solution)/shard_map/pallas_call | solution.py:580
  126.2 0.0 collective-permute-done.2.east_ref
  126.2 3.1 %collective-permute-done.3.west_ref = f32[40,8,128]{2,1,0:T(8,128)S(1)} collective-permute-done((f32[40,8,128]{2,1,0:T(8,128)S(1)}, f32[40,8,128]{2,1,0:T(8,128)S(1)}, u32[]{:S(2)}, u32[]{:S(2)}) %collective-permute-start.3) | collective-permute-done | bytes 163872 | tf_op jit(solution)/shard_map/ppermute | solution.py:596
  129.3 0.0 copy-done.4
  129.3 27.4 %shard_map.90 = (f32[9,3072,128]{2,1,0:T(8,128)S(1)}, f32[2,32,32,384]{3,2,1,0:T(8,128)S(1)}, f32[256,3,8,128]{3,2,1,0:T(8,128)S(1)}) custom-call(s32[16,16]{1,0:T(8,128)S(1)} %dynamic_slice.3.tile_ref, s32[2]{0:T(128)S(1)} %pad_add_fusion.lat_ref, f32[9,3072,128]{2,1,0:T(8,128)S(1)} %shard_map.88.blocks_ref, ...), custom_call_target="tpu_custom_call", output_to_operand_aliasing={{0}: (2, {})} | custom-call | tf_op jit(solution)/shard_map/pallas_call | solution.py:601
  156.7 0.0 copy-start
  156.7 1.6 copy-done
  158.4 0.0 copy-start.2
  158.4 1.7 copy-done.2
  160.1 7.9 %all-to-all-start.1 = ((f32[128,6,8,128]{3,2,1,0:T(8,128)}), f32[128,6,8,128]{3,2,1,0:T(8,128)S(1)}, u32[]{:S(2)}, u32[]{:S(2)}) async-start(f32[128,6,8,128]{3,2,1,0:T(8,128)} %bitcast.15), calls=%async_computation.1 | async-start | bytes 6291456 | tf_op jit(solution)/shard_map/all_to_all | solution.py:629
  167.9 0.0 copy-start.5
  167.9 0.0 copy-start.1
  167.9 1.9 copy-done.1
  169.8 5.0 %shard_map.91 = f32[2,512,512]{2,1,0:T(8,128)} custom-call(f32[2,32,32,384]{3,2,1,0:T(8,128)S(1)} %copy-done.1), custom_call_target="tpu_custom_call" | custom-call | flops 10000000 | bytes 6291456 | tf_op jit(solution)/shard_map/pallas_call | solution.py:632
  174.8 34.7 %all-to-all-done.1 = f32[128,6,8,128]{3,2,1,0:T(8,128)S(1)} async-done(((f32[128,6,8,128]{3,2,1,0:T(8,128)}), f32[128,6,8,128]{3,2,1,0:T(8,128)S(1)}, u32[]{:S(2)}, u32[]{:S(2)}) %all-to-all-start.1) | async-done | bytes 3145760 | tf_op jit(solution)/shard_map/all_to_all | solution.py:629
  209.4 0.0 copy-done.5
  209.4 2.5 %shard_map.92 = f32[3,32,32,128]{3,2,1,0:T(8,128)} custom-call(s32[1,128]{1,0:T(1,128)S(1)} %copy-done.5, f32[256,3,8,128]{3,2,1,0:T(8,128)S(1)} %bitcast.14), custom_call_target="tpu_custom_call" | custom-call | tf_op jit(solution)/shard_map/pallas_call | solution.py:641
  (4 shorter events, 0.0 us)
Async XLA Ops:
  6.7 98.6 %all-to-all-start = ((f32[128,14,8,128]{3,2,1,0:T(8,128)}), f32[128,14,8,128]{3,2,1,0:T(8,128)}, u32[]{:S(2)}, u32[]{:S(2)}) async-start(f32[128,14,8,128]{3,2,1,0:T(8,128)} %bitcast.16), calls=%async_computation | async-start | bytes 14680064 | tf_op jit(solution)/shard_map/all_to_all | solution.py:556
  19.4 1.6 copy-start.3
  109.6 8.0 %collective-permute-start = (f32[16,2,8,128]{3,2,1,0:T(8,128)S(1)}, f32[16,2,8,128]{3,2,1,0:T(8,128)S(1)}, u32[]{:S(2)}, u32[]{:S(2)}) collective-permute-start(f32[16,2,8,128]{3,2,1,0:T(8,128)S(1)} %get-tuple-element.11), channel_id=1, source_target_pairs={{1,0},{2,1},{3,2},{4,3},{5,4},{6,5},{7,6},{9,8},{10,9},{11,10},{12... | collective-permute-start | bytes 393224 | tf_op jit(solution)/shard_map/ppermute | solution.py:590
  112.8 6.1 %collective-permute-start.1 = (f32[16,2,8,128]{3,2,1,0:T(8,128)S(1)}, f32[16,2,8,128]{3,2,1,0:T(8,128)S(1)}, u32[]{:S(2)}, u32[]{:S(2)}) collective-permute-start(f32[16,2,8,128]{3,2,1,0:T(8,128)S(1)} %get-tuple-element.12), channel_id=1, source_target_pairs={{0,1},{1,2},{2,3},{3,4},{4,5},{5,6},{6,7},{8,9},{9,10},{10,11},{11... | collective-permute-start | bytes 393224 | tf_op jit(solution)/shard_map/ppermute | solution.py:591
  118.9 7.3 %collective-permute-start.2 = (f32[40,8,128]{2,1,0:T(8,128)S(1)}, f32[40,8,128]{2,1,0:T(8,128)S(1)}, u32[]{:S(2)}, u32[]{:S(2)}) collective-permute-start(f32[40,8,128]{2,1,0:T(8,128)S(1)} %pad_maximum_fusion), channel_id=1, source_target_pairs={{8,0},{16,8},{24,16},{32,24},{40,32},{48,40},{56,48},{64,56},{72,6... | collective-permute-start | bytes 491528 | tf_op jit(solution)/shard_map/ppermute | solution.py:595
  121.7 7.6 %collective-permute-start.3 = (f32[40,8,128]{2,1,0:T(8,128)S(1)}, f32[40,8,128]{2,1,0:T(8,128)S(1)}, u32[]{:S(2)}, u32[]{:S(2)}) collective-permute-start(f32[40,8,128]{2,1,0:T(8,128)S(1)} %pad_maximum_fusion.1), channel_id=1, source_target_pairs={{0,8},{8,16},{16,24},{24,32},{32,40},{40,48},{48,56},{56,64},{64,7... | collective-permute-start | bytes 491528 | tf_op jit(solution)/shard_map/ppermute | solution.py:596
  121.9 7.4 %copy-start.4 = (s32[32,384]{1,0:T(8,128)S(1)}, s32[32,384]{1,0:T(8,128)}, u32[]{:S(2)}) copy-start(s32[32,384]{1,0:T(8,128)} %constant.23.clone.cell_ref) | copy-start | bytes 147460
  156.7 1.6 copy-start
  158.4 1.7 copy-start.2
  160.1 49.4 %all-to-all-start.1 = ((f32[128,6,8,128]{3,2,1,0:T(8,128)}), f32[128,6,8,128]{3,2,1,0:T(8,128)S(1)}, u32[]{:S(2)}, u32[]{:S(2)}) async-start(f32[128,6,8,128]{3,2,1,0:T(8,128)} %bitcast.15), calls=%async_computation.1 | async-start | bytes 6291456 | tf_op jit(solution)/shard_map/all_to_all | solution.py:629
  167.9 41.5 %copy-start.5 = (s32[1,128]{1,0:T(1,128)S(1)}, s32[1,128]{1,0:T(1,128)}, u32[]{:S(2)}) copy-start(s32[1,128]{1,0:T(1,128)} %get-tuple-element.16.pos_ref) | copy-start | bytes 1540
  167.9 1.9 copy-start.1

commit v3 on v2

--- a/solution.py
+++ b/solution.py
@@ -130,85 +130,95 @@
             rows = jnp.concatenate([load(8 * q + s) for q in range(4)], axis=0)
             scr_ref[field, pl.ds(s, slots, stride=8), :] = rows.T
 
+    def scatter(first, fields, sem):
+        def body(slot, carry):
+            rows = pl.ds(pl.multiple_of(slot * 8, 8), 8)
+            pltpu.make_async_copy(
+                scr_ref.at[pl.ds(first, fields), rows, :],
+                send_ref.at[place_ref[0, slot], pl.ds(first, fields)],
+                sem,
+            ).start()
+            return carry
+
+        lax.fori_loop(0, slots, body, 0, unroll=8)
+        everything = send_ref.at[pl.ds(0, slots), pl.ds(first, fields)]
+        return pltpu.make_async_copy(everything, everything, sem)
+
     fetches[0].wait()
     for c in range(2):
         turn(c, lambda ci, c=c: vel_ref[c, ci])
     fetches[1].wait()
     for c in range(3):
         turn(2 + c, lambda ci, c=c: str_ref[c, ci])
+    to_scalar.wait()
+    early = scatter(0, 5, sems.at[5])
     fetches[2].wait()
     turn(5, lambda ci: mass_ref[ci])
     fetches[3].wait()
     turn(6, lambda ci: strength_ref[ci])
-    to_scalar.wait()
-
-    def scatter(slot, carry):
-        spot = place_ref[0, slot]
-        rows = pl.ds(pl.multiple_of(slot * 8, 8), 8)
-        pltpu.make_async_copy(scr_ref.at[:, rows, :], send_ref.at[spot], sems.at[5]).start()
-        return carry
-
-    lax.fori_loop(0, slots, scatter, 0, unroll=4)
-    pltpu.make_async_copy(send_ref.at[pl.ds(0, slots)], send_ref.at[pl.ds(0, slots)], sems.at[5]).wait()
-
-
-def strips_kernel(
-    tile_ref,
-    recv_hbm,
-    force_ref,
-    north_ref,
-    south_ref,
-    east_ref,
-    west_ref,
-    edge_ref,
-    sem,
-):
-    lane = lane_ids((8, LANES))
-    in_group = lane % 32
+    late = scatter(5, 2, sems.at[6])
+    early.wait()
+    late.wait()
+
+
+def fetch_edges(tile_ref, recv_hbm, edge_ref, sem, places):
     count = recv_hbm.shape[0] // 2
-    half = BX_DEV // 2
 
     def fetch(i, carry):
-        for side, (bx, by) in enumerate(((i, 0), (i, BY_DEV - 1), (0, i), (BX_DEV - 1, i))):
-            source = (tile_ref[bx, by] & (count - 1)) * 2 + jnp.int32(bx >= half)
+        for side, (bx, by) in enumerate(places(i)):
+            source = (tile_ref[bx, by] & (count - 1)) * 2 + jnp.int32(bx >= BX_DEV // 2)
             pltpu.make_async_copy(recv_hbm.at[source], edge_ref.at[side * BX_DEV + i], sem).start()
         return carry
 
-    lax.fori_loop(0, BX_DEV, fetch, 0)
-    pltpu.make_async_copy(recv_hbm.at[pl.ds(0, 4 * BX_DEV)], edge_ref, sem).wait()
-
-    def block_of(side, bx, by, field):
-        if field >= FIELDS:
-            return force_ref[bx * BY_DEV + by, field - FIELDS]
-        value = edge_ref[side * BX_DEV + (bx if side < 2 else by), field]
-        return jnp.where(tile_ref[bx, by] >= 0, value, 0.0)
-
-    for side, bx, ref, group in ((2, 0, east_ref, 0), (3, BX_DEV - 1, west_ref, 3)):
+    lax.fori_loop(0, BX_DEV, fetch, 0, unroll=4)
+    pltpu.make_async_copy(recv_hbm.at[pl.ds(0, 2 * BX_DEV)], edge_ref, sem).wait()
+
+
+def lat_kernel(tile_ref, recv_hbm, force_ref, north_ref, south_ref, edge_ref, sem):
+    in_group = lane_ids((8, LANES)) % 32
+    edges = (0, BY_DEV - 1)
+    fetch_edges(tile_ref, recv_hbm, edge_ref, sem, lambda i: [(i, by) for by in edges])
+
+    def lat_rims(bx, carry):
+        for side, (by, ref, first) in enumerate(
+            zip(edges, (north_ref, south_ref), (0, B - HALO))
+        ):
+            for v in range(2):
+                total = jnp.zeros((8, LANES), jnp.float32)
+                for k in range(min(5, FIELDS + 2 - v * 5)):
+                    field = v * 5 + k
+                    if field >= FIELDS:
+                        got = force_ref[bx * BY_DEV + by, field - FIELDS]
+                    else:
+                        got = edge_ref[side * BX_DEV + bx, field]
+                        got = jnp.where(tile_ref[bx, by] >= 0, got, 0.0)
+                    mine = (in_group >= HALO * k) & (in_group < HALO * (k + 1))
+                    got = pltpu.roll(got, (HALO * k - first) % LANES, 1)
+                    total = jnp.where(mine, got, total)
+                ref[bx, v] = total
+        return carry
+
+    lax.fori_loop(0, BX_DEV, lat_rims, 0, unroll=2)
+
+
+def lon_kernel(tile_ref, recv_hbm, force_ref, east_ref, west_ref, edge_ref, sem):
+    group_of = lane_ids((8, LANES)) // 32
+    edges = (0, BX_DEV - 1)
+    fetch_edges(tile_ref, recv_hbm, edge_ref, sem, lambda i: [(bx, i) for bx in edges])
+    for side, (bx, ref, group) in enumerate(zip(edges, (east_ref, west_ref), (0, 3))):
         for part in range(4):
             for field in range(FIELDS + 2):
                 total = jnp.zeros((8, LANES), jnp.float32)
                 for p in range(4):
-                    got = block_of(side, bx, part * 4 + p, field)
+                    by = part * 4 + p
+                    if field >= FIELDS:
+                        got = force_ref[bx * BY_DEV + by, field - FIELDS]
+                    else:
+                        got = edge_ref[side * BX_DEV + by, field]
+                        got = jnp.where(tile_ref[bx, by] >= 0, got, 0.0)
                     turned = pltpu.roll(got, ((p - group) * 32) % LANES, 1) if p != group else got
-                    total = jnp.where(lane // 32 == p, turned, total)
+                    total = jnp.where(group_of == p, turned, total)
                 ref[field * 4 + part] = total
-
-    def lat_rims(bx, carry):
-        for side, by, ref, first in (
-            (0, 0, north_ref, 0),
-            (1, BY_DEV - 1, south_ref, B - HALO),
-        ):
-            for v in range(2):
-                total = jnp.zeros((8, LANES), jnp.float32)
-                for k in range(min(5, FIELDS + 2 - v * 5)):
-                    mine = (in_group >= HALO * k) & (in_group < HALO * (k + 1))
-                    got = block_of(side, bx, by, v * 5 + k)
-                    got = pltpu.roll(got, (HALO * k - first) % LANES, 1)
-                    total = jnp.where(mine, got, total)
-                ref[bx, v] = total
-        return carry
-
-    lax.fori_loop(0, BX_DEV, lat_rims, 0)
 
 
 def collect_kernel(tile_ref, recv_ref, force_ref, scr_ref):
@@ -506,7 +516,6 @@
 
 VMEM = pl.BlockSpec(memory_space=pltpu.VMEM)
 SMEM = pl.BlockSpec(memory_space=pltpu.SMEM)
-ANY = pl.BlockSpec(memory_space=pl.ANY)
 HBM = pl.BlockSpec(memory_space=pltpu.HBM)
 
 
@@ -537,7 +546,7 @@
     send, pos = pl.pallas_call(
         pack_kernel,
         out_shape=(
-            f32(devices * 2, FIELDS, 8, LANES),
+            pltpu.HBM((devices * 2, FIELDS, 8, LANES), jnp.float32),
             jax.ShapeDtypeStruct((1, slots), jnp.int32),
         ),
         in_specs=[SMEM, VMEM] + [HBM] * 4,
@@ -549,7 +558,7 @@
             pltpu.VMEM(block, jnp.float32),
             pltpu.VMEM((FIELDS, slots * 8, LANES), jnp.float32),
             pltpu.SMEM((1, slots), jnp.int32),
-            pltpu.SemaphoreType.DMA((6,)),
+            pltpu.SemaphoreType.DMA((7,)),
         ],
         compiler_params=params(61),
     )(own_index.reshape(1).astype(jnp.int32), owner, velocity, stress, mass, strength)
@@ -565,21 +574,31 @@
         cost_estimate=cost(4),
         compiler_params=params(12),
     )(forcing)
-    north, south, east, west = pl.pallas_call(
-        strips_kernel,
-        out_shape=(f32(BX_DEV, 2, 8, LANES),) * 2 + (f32(RIM, 8, LANES),) * 2,
+    edge_scratch = [
+        pltpu.VMEM((2 * BX_DEV, FIELDS, 8, LANES), jnp.float32),
+        pltpu.SemaphoreType.DMA(()),
+    ]
+    north, south = pl.pallas_call(
+        lat_kernel,
+        out_shape=(f32(BX_DEV, 2, 8, LANES),) * 2,
         in_specs=[SMEM, HBM, VMEM],
-        out_specs=(VMEM,) * 4,
-        scratch_shapes=[
-            pltpu.VMEM((4 * BX_DEV, FIELDS, 8, LANES), jnp.float32),
-            pltpu.SemaphoreType.DMA(()),
-        ],
+        out_specs=(VMEM,) * 2,
+        scratch_shapes=edge_scratch,
         cost_estimate=cost(4),
-        compiler_params=params(10),
+        compiler_params=params(8),
+    )(my_tile, recv, force_blocks)
+    east, west = pl.pallas_call(
+        lon_kernel,
+        out_shape=(f32(RIM, 8, LANES),) * 2,
+        in_specs=[SMEM, HBM, VMEM],
+        out_specs=(VMEM,) * 2,
+        scratch_shapes=edge_scratch,
+        cost_estimate=cost(6),
+        compiler_params=params(8),
     )(my_tile, recv, force_blocks)
     blocks = pl.pallas_call(
         collect_kernel,
-        out_shape=f32(FIELDS + 2, GRID_LANES * 8, LANES),
+        out_shape=pltpu.VMEM((FIELDS + 2, GRID_LANES * 8, LANES), jnp.float32),
         in_specs=[SMEM, VMEM, VMEM],
         out_specs=VMEM,
         cost_estimate=cost(24),
@@ -601,12 +620,12 @@
     _, cell_velocity, back = pl.pallas_call(
         tile_kernel,
         out_shape=(
-            f32(FIELDS + 2, GRID_LANES * 8, LANES),
-            f32(2, B, B, GRID_LANES),
-            f32(devices * 2, 3, 8, LANES),
+            pltpu.VMEM((FIELDS + 2, GRID_LANES * 8, LANES), jnp.float32),
+            pltpu.HBM((2, B, B, GRID_LANES), jnp.float32),
+            pltpu.HBM((devices * 2, 3, 8, LANES), jnp.float32),
         ),
         in_specs=[SMEM, SMEM] + [VMEM] * 6,
-        out_specs=(VMEM, HBM, ANY),
+        out_specs=(VMEM, HBM, HBM),
         input_output_aliases={2: 0},
         scratch_shapes=[pltpu.VMEM(state, jnp.float32)] * 5
         + [pltpu.VMEM(constant, jnp.float32)] * 5

time: 213 us -> 209 us (0.981)
  waiting for transfers between devices: 121 us -> 116 us
  local copies, waits for them, and re-layouts: 7.58 us -> 4.27 us
  starting transfers between devices: 30 us -> 33.3 us
    unnamed x12 -> x8, local copies, waits for them, and re-layouts: 6.8 us -> 3.48 us
    ppermute x1, waiting for transfers between devices: 3.08 us -> 0.01 us  [on_device(): got_west = lax.ppermute(west, 'lon', ring)]
    pallas_call x4 -> x5, Pallas kernels: 42.1 us -> 43.4 us  [the longest x1 28.6 us: on_device(): pl.pallas_call(tile_kernel, out_shape=(pltpu.VMEM((FIELDS + 2, GRID_LANES...]
  transfers between devices with their start and end apart: 6 -> 6, of which waited for: 5 -> 2; matrix products, arithmetic and copies ran while one was open for 0% -> 0% of each run, Pallas kernels for 6% -> 7%
where the time goes in v3:
time: 209 us; the launch traced here: 208 us
  waiting for transfers between devices  116 us (56%)
  Pallas kernels  53.8 us (26%)
  starting transfers between devices  33.3 us (16%)
  local copies, waits for them, and re-layouts  4.27 us (2%)
    all_to_all x1, waiting for transfers between devices, on_device(): lax.all_to_all(send.reshape(devices, 2 * FIELDS, 8, LANES), ('lon', 'lat'...  81.4 us
    all_to_all x1, waiting for transfers between devices, on_device(): lax.all_to_all(back.reshape(devices, 6, 8, LANES), ('lon', 'lat'), 0, 0,...  34.7 us
    pallas_call x1, Pallas kernels, on_device(): pl.pallas_call(tile_kernel, out_shape=(pltpu.VMEM((FIELDS + 2, GRID_LANES...  28.6 us
    all_to_all x1, starting transfers between devices, on_device(): lax.all_to_all(send.reshape(devices, 2 * FIELDS, 8, LANES), ('lon', 'lat'...  11.9 us
    all_to_all x1, starting transfers between devices, on_device(): lax.all_to_all(back.reshape(devices, 6, 8, LANES), ('lon', 'lat'), 0, 0,...  9.86 us
    pallas_call x1, Pallas kernels, on_device(): pl.pallas_call(pack_kernel, out_shape=(pltpu.HBM((devices * 2, FIELDS, 8,...  5.66 us
    pallas_call x1, Pallas kernels, on_device(): pl.pallas_call(velocity_kernel, out_shape=f32(2, ROWS, COLS), in_specs=[V...  4.96 us
    ppermute x1, starting transfers between devices, on_device(): got_east = lax.ppermute(east, 'lon', [(k, i) for i, k in ring])  4.83 us
  transfers between devices with their start and end apart: 6, of which 2 were waited for; matrix products, arithmetic and copies ran while one was open for 0% of the time, Pallas kernels for 7%

profile of v3, /device:TPU:1, one launch (start us, length us, event | category | flops | bytes accessed | tf_op | source)
XLA Modules:
  0.0 208.3 jit_solution(1159308127734465561)
XLA Ops:
  0.6 5.7 %shard_map.86 = (f32[256,7,8,128]{3,2,1,0:T(8,128)}, s32[1,128]{1,0:T(1,128)}) custom-call(s32[1]{0:T(128)} %bitcast.1.own_ref, s32[256,128]{1,0:T(8,128)} %owner_ref.1, f32[2,32,32,128]{3,2,1,0:T(8,128)} %vel_hbm.1, f32[3,32,32,128]{3,2,1,0:T(8,128)} %str_hbm.1, f32[32,32,128]{2,1,0:T(8,128)} %mass_hbm.1, f32[32,32,128]{2,1,0:T(8,128)} %strength_hbm.1), custom_call_target="tpu_custom_call" | custom-call | tf_op jit(solution)/shard_map/pallas_call | solution.py:546
  6.3 11.9 %all-to-all-start = ((f32[128,14,8,128]{3,2,1,0:T(8,128)}), f32[128,14,8,128]{3,2,1,0:T(8,128)}, u32[]{:S(2)}, u32[]{:S(2)}) async-start(f32[128,14,8,128]{3,2,1,0:T(8,128)} %bitcast.15), calls=%async_computation | async-start | bytes 14680064 | tf_op jit(solution)/shard_map/all_to_all | solution.py:565
  18.2 0.8 dynamic_slice.3.tile_ref
  19.0 0.0 copy-start.1
  19.0 1.6 copy-done.1
  20.6 2.9 %shard_map.87.force_ref = f32[256,2,8,128]{3,2,1,0:T(8,128)S(1)} custom-call(f32[2,512,512]{2,1,0:T(8,128)S(1)} %copy-done.1), custom_call_target="tpu_custom_call" | custom-call | flops 10000000 | bytes 4194304 | tf_op jit(solution)/shard_map/pallas_call | solution.py:569
  23.5 81.4 %all-to-all-done = f32[128,14,8,128]{3,2,1,0:T(8,128)} async-done(((f32[128,14,8,128]{3,2,1,0:T(8,128)}), f32[128,14,8,128]{3,2,1,0:T(8,128)}, u32[]{:S(2)}, u32[]{:S(2)}) %all-to-all-start) | async-done | bytes 7340064 | tf_op jit(solution)/shard_map/all_to_all | solution.py:565
  104.9 2.7 %shard_map.89 = (f32[16,2,8,128]{3,2,1,0:T(8,128)S(1)}, f32[16,2,8,128]{3,2,1,0:T(8,128)S(1)}) custom-call(s32[16,16]{1,0:T(8,128)S(1)} %dynamic_slice.3.tile_ref, f32[256,7,8,128]{3,2,1,0:T(8,128)} %bitcast.3.recv_ref.recv_hbm, f32[256,2,8,128]{3,2,1,0:T(8,128)S(1)} %shard_map.87.force_ref), custom_call_target="tpu_custom_call" | custom-call | flops 10000000 | bytes 4194304 | tf_op jit(solution)/shard_map/pallas_call | solution.py:581
  107.6 3.2 %collective-permute-start = (f32[16,2,8,128]{3,2,1,0:T(8,128)S(1)}, f32[16,2,8,128]{3,2,1,0:T(8,128)S(1)}, u32[]{:S(2)}, u32[]{:S(2)}) collective-permute-start(f32[16,2,8,128]{3,2,1,0:T(8,128)S(1)} %get-tuple-element.11), channel_id=1, source_target_pairs={{1,0},{2,1},{3,2},{4,3},{5,4},{6,5},{7,6},{9,8},{10,9},{11,10},{12... | collective-permute-start | bytes 393224 | tf_op jit(solution)/shard_map/ppermute | solution.py:609
  110.8 3.4 %collective-permute-start.1 = (f32[16,2,8,128]{3,2,1,0:T(8,128)S(1)}, f32[16,2,8,128]{3,2,1,0:T(8,128)S(1)}, u32[]{:S(2)}, u32[]{:S(2)}) collective-permute-start(f32[16,2,8,128]{3,2,1,0:T(8,128)S(1)} %get-tuple-element.12), channel_id=1, source_target_pairs={{0,1},{1,2},{2,3},{3,4},{4,5},{5,6},{6,7},{8,9},{9,10},{10,11},{11... | collective-permute-start | bytes 393224 | tf_op jit(solution)/shard_map/ppermute | solution.py:610
  114.2 2.1 %shard_map.90 = (f32[36,8,128]{2,1,0:T(8,128)S(1)}, f32[36,8,128]{2,1,0:T(8,128)S(1)}) custom-call(s32[16,16]{1,0:T(8,128)S(1)} %dynamic_slice.3.tile_ref, f32[256,7,8,128]{3,2,1,0:T(8,128)} %bitcast.3.recv_ref.recv_hbm, f32[256,2,8,128]{3,2,1,0:T(8,128)S(1)} %shard_map.87.force_ref), custom_call_target="tpu_custom_call" | custom-call | flops 10000000 | bytes 6291456 | tf_op jit(solution)/shard_map/pallas_call | solution.py:590
  116.4 0.0 collective-permute-done.north_ref
  116.4 0.0 collective-permute-done.1.south_ref
  116.4 0.1 collective-permute-start.3
  116.5 4.8 %collective-permute-start.2 = (f32[40,8,128]{2,1,0:T(8,128)S(1)}, f32[40,8,128]{2,1,0:T(8,128)S(1)}, u32[]{:S(2)}, u32[]{:S(2)}) collective-permute-start(f32[40,8,128]{2,1,0:T(8,128)S(1)} %pad_maximum_fusion), channel_id=1, source_target_pairs={{8,0},{16,8},{24,16},{32,24},{40,32},{48,40},{56,48},{64,56},{72,6... | collective-permute-start | bytes 491528 | tf_op jit(solution)/shard_map/ppermute | solution.py:614
  121.4 0.1 pad_add_fusion.lat_ref
  121.4 0.0 copy-start.2
  121.5 4.3 %shard_map.88.blocks_ref = f32[9,3072,128]{2,1,0:T(8,128)S(1)} custom-call(s32[16,16]{1,0:T(8,128)S(1)} %dynamic_slice.3.tile_ref, f32[256,7,8,128]{3,2,1,0:T(8,128)} %bitcast.3.recv_ref.recv_hbm, f32[256,2,8,128]{3,2,1,0:T(8,128)S(1)} %shard_map.87.force_ref), custom_call_target="tpu_custom_call" | custom-call | flops 10000000 | bytes 25165824 | tf_op jit(solution)/shard_map/pallas_call | solution.py:599
  125.8 0.0 collective-permute-done.3.west_ref
  125.8 0.0 collective-permute-done.2.east_ref
  125.8 0.0 copy-done.2
  125.8 28.6 %shard_map.91 = (f32[9,3072,128]{2,1,0:T(8,128)S(1)}, f32[2,32,32,384]{3,2,1,0:T(8,128)}, f32[256,3,8,128]{3,2,1,0:T(8,128)}) custom-call(s32[16,16]{1,0:T(8,128)S(1)} %dynamic_slice.3.tile_ref, s32[2]{0:T(128)S(1)} %pad_add_fusion.lat_ref, f32[9,3072,128]{2,1,0:T(8,128)S(1)} %shard_map.88.blocks_ref, ...), custom_call_target="tpu_custom_call", output_to_operand_aliasing={{0}: (2, {})} | custom-call | tf_op jit(solution)/shard_map/pallas_call | solution.py:620
  154.4 9.9 %all-to-all-start.1 = ((f32[128,6,8,128]{3,2,1,0:T(8,128)}), f32[128,6,8,128]{3,2,1,0:T(8,128)S(1)}, u32[]{:S(2)}, u32[]{:S(2)}) async-start(f32[128,6,8,128]{3,2,1,0:T(8,128)} %bitcast.16), calls=%async_computation.1 | async-start | bytes 6291456 | tf_op jit(solution)/shard_map/all_to_all | solution.py:648
  164.3 0.0 copy-start.3
  164.3 0.0 copy-start
  164.3 1.9 copy-done
  166.2 5.0 %shard_map.92 = f32[2,512,512]{2,1,0:T(8,128)} custom-call(f32[2,32,32,384]{3,2,1,0:T(8,128)S(1)} %copy-done), custom_call_target="tpu_custom_call" | custom-call | flops 10000000 | bytes 6291456 | tf_op jit(solution)/shard_map/pallas_call | solution.py:651
  171.2 34.7 %all-to-all-done.1 = f32[128,6,8,128]{3,2,1,0:T(8,128)S(1)} async-done(((f32[128,6,8,128]{3,2,1,0:T(8,128)}), f32[128,6,8,128]{3,2,1,0:T(8,128)S(1)}, u32[]{:S(2)}, u32[]{:S(2)}) %all-to-all-start.1) | async-done | bytes 3145760 | tf_op jit(solution)/shard_map/all_to_all | solution.py:648
  205.8 0.0 copy-done.3
  205.8 2.5 %shard_map.93 = f32[3,32,32,128]{3,2,1,0:T(8,128)} custom-call(s32[1,128]{1,0:T(1,128)S(1)} %copy-done.3, f32[256,3,8,128]{3,2,1,0:T(8,128)S(1)} %bitcast.14), custom_call_target="tpu_custom_call" | custom-call | tf_op jit(solution)/shard_map/pallas_call | solution.py:660
  (4 shorter events, 0.0 us)
Async XLA Ops:
  6.3 98.6 %all-to-all-start = ((f32[128,14,8,128]{3,2,1,0:T(8,128)}), f32[128,14,8,128]{3,2,1,0:T(8,128)}, u32[]{:S(2)}, u32[]{:S(2)}) async-start(f32[128,14,8,128]{3,2,1,0:T(8,128)} %bitcast.15), calls=%async_computation | async-start | bytes 14680064 | tf_op jit(solution)/shard_map/all_to_all | solution.py:565
  19.0 1.6 copy-start.1
  107.6 8.8 %collective-permute-start = (f32[16,2,8,128]{3,2,1,0:T(8,128)S(1)}, f32[16,2,8,128]{3,2,1,0:T(8,128)S(1)}, u32[]{:S(2)}, u32[]{:S(2)}) collective-permute-start(f32[16,2,8,128]{3,2,1,0:T(8,128)S(1)} %get-tuple-element.11), channel_id=1, source_target_pairs={{1,0},{2,1},{3,2},{4,3},{5,4},{6,5},{7,6},{9,8},{10,9},{11,10},{12... | collective-permute-start | bytes 393224 | tf_op jit(solution)/shard_map/ppermute | solution.py:609
  110.8 5.6 %collective-permute-start.1 = (f32[16,2,8,128]{3,2,1,0:T(8,128)S(1)}, f32[16,2,8,128]{3,2,1,0:T(8,128)S(1)}, u32[]{:S(2)}, u32[]{:S(2)}) collective-permute-start(f32[16,2,8,128]{3,2,1,0:T(8,128)S(1)} %get-tuple-element.12), channel_id=1, source_target_pairs={{0,1},{1,2},{2,3},{3,4},{4,5},{5,6},{6,7},{8,9},{9,10},{10,11},{11... | collective-permute-start | bytes 393224 | tf_op jit(solution)/shard_map/ppermute | solution.py:610
  116.4 9.3 %collective-permute-start.3 = (f32[40,8,128]{2,1,0:T(8,128)S(1)}, f32[40,8,128]{2,1,0:T(8,128)S(1)}, u32[]{:S(2)}, u32[]{:S(2)}) collective-permute-start(f32[40,8,128]{2,1,0:T(8,128)S(1)} %pad_maximum_fusion.1), channel_id=1, source_target_pairs={{0,8},{8,16},{16,24},{24,32},{32,40},{40,48},{48,56},{56,64},{64,7... | collective-permute-start | bytes 491528 | tf_op jit(solution)/shard_map/ppermute | solution.py:615
  116.5 9.2 %collective-permute-start.2 = (f32[40,8,128]{2,1,0:T(8,128)S(1)}, f32[40,8,128]{2,1,0:T(8,128)S(1)}, u32[]{:S(2)}, u32[]{:S(2)}) collective-permute-start(f32[40,8,128]{2,1,0:T(8,128)S(1)} %pad_maximum_fusion), channel_id=1, source_target_pairs={{8,0},{16,8},{24,16},{32,24},{40,32},{48,40},{56,48},{64,56},{72,6... | collective-permute-start | bytes 491528 | tf_op jit(solution)/shard_map/ppermute | solution.py:614
  121.4 4.3 %copy-start.2 = (s32[32,384]{1,0:T(8,128)S(1)}, s32[32,384]{1,0:T(8,128)}, u32[]{:S(2)}) copy-start(s32[32,384]{1,0:T(8,128)} %constant.23.clone.cell_ref) | copy-start | bytes 147460
  154.4 51.4 %all-to-all-start.1 = ((f32[128,6,8,128]{3,2,1,0:T(8,128)}), f32[128,6,8,128]{3,2,1,0:T(8,128)S(1)}, u32[]{:S(2)}, u32[]{:S(2)}) async-start(f32[128,6,8,128]{3,2,1,0:T(8,128)} %bitcast.16), calls=%async_computation.1 | async-start | bytes 6291456 | tf_op jit(solution)/shard_map/all_to_all | solution.py:648
  164.3 41.5 %copy-start.3 = (s32[1,128]{1,0:T(1,128)S(1)}, s32[1,128]{1,0:T(1,128)}, u32[]{:S(2)}) copy-start(s32[1,128]{1,0:T(1,128)} %get-tuple-element.16.pos_ref) | copy-start | bytes 1540
  164.3 1.9 copy-start

commit v4 on v3

--- a/solution.py
+++ b/solution.py
@@ -13,10 +13,14 @@
 LANES = 128
 CORIOLIS = 0.5
 HALO = 6
-FIELDS = 7
+FIELDS = 6
+MESSAGE = 2 * FIELDS + 1
+EDGE = FIELDS + 2
+PER_RIM = 4
 ROWS = BX_DEV * B
 COLS = BY_DEV * B
-RIM = 4 * (FIELDS + 2)
+LAT_RIM = BX_DEV * 2 + BX_DEV // 8
+LON_RIM = 4 * (FIELDS + 2) + BY_DEV // 8
 SIDE = BX_DEV + 2
 GRID_LANES = -(-SIDE * SIDE // LANES) * LANES
 
@@ -46,6 +50,10 @@
 
 def grid_rows(bx, by):
     return pl.ds(pl.multiple_of(((bx + 1) * SIDE + by + 1) * 8, 8), 8)
+
+
+def grid_row(bx, by):
+    return pl.ds(pl.multiple_of(((bx + 1) * SIDE + by + 1) * 8, 8), 1)
 
 
 def pack_kernel(
@@ -62,6 +70,8 @@
     mass_ref,
     strength_ref,
     scr_ref,
+    edge_ref,
+    stage_ref,
     place_ref,
     sems,
 ):
@@ -125,53 +135,88 @@
     to_scalar = pltpu.make_async_copy(pos_ref, place_ref, sems.at[4])
     to_scalar.start()
 
-    def turn(field, load):
-        for s in range(8):
-            rows = jnp.concatenate([load(8 * q + s) for q in range(4)], axis=0)
-            scr_ref[field, pl.ds(s, slots, stride=8), :] = rows.T
+    def turn(field, planes):
+        scr_ref[field, pl.ds(planes[0], slots, stride=8), :] = jnp.concatenate(planes[1], axis=0).T
 
     def scatter(first, fields, sem):
         def body(slot, carry):
             rows = pl.ds(pl.multiple_of(slot * 8, 8), 8)
+            place = place_ref[0, slot]
             pltpu.make_async_copy(
                 scr_ref.at[pl.ds(first, fields), rows, :],
-                send_ref.at[place_ref[0, slot], pl.ds(first, fields)],
+                send_ref.at[place >> 1, pl.ds((place & 1) * (FIELDS + 1) + first, fields)],
                 sem,
             ).start()
             return carry
 
         lax.fori_loop(0, slots, body, 0, unroll=8)
-        everything = send_ref.at[pl.ds(0, slots), pl.ds(first, fields)]
+        everything = send_ref.at[pl.ds(0, slots), pl.ds(0, fields)]
         return pltpu.make_async_copy(everything, everything, sem)
+
+    first_row = row_ids((B, slots)) == 0
+
+    def south(x):
+        return jnp.where(first_row, 0.0, pltpu.roll(x, 1, 0))
+
+    def stresses(ci):
+        total, diff = str_ref[0, ci], str_ref[1, ci]
+        return 0.5 * (total + diff), 0.5 * (total - diff), str_ref[2, ci]
 
     fetches[0].wait()
     for c in range(2):
-        turn(c, lambda ci, c=c: vel_ref[c, ci])
+        for s in range(8):
+            turn(c, (s, [vel_ref[c, 8 * q + s] for q in range(4)]))
     fetches[1].wait()
-    for c in range(3):
-        turn(2 + c, lambda ci, c=c: str_ref[c, ci])
+    for s in range(8):
+        push_x, push_y = [], []
+        for q in range(4):
+            p, n, shear = stresses(8 * q + s)
+            gx = p + (shear - south(shear))
+            gy = shear + (n - south(n))
+            if q or s:
+                p_west, _, shear_west = stresses(8 * q + s - 1)
+                gx, gy = gx - p_west, gy - shear_west
+            push_x.append(gx)
+            push_y.append(gy)
+        turn(2, (s, push_x))
+        turn(3, (s, push_y))
+    p, _, shear = stresses(B - 1)
+    shear_top = str_ref[2, :, B - 1, :]
+    n_top = 0.5 * (str_ref[0, :, B - 1, :] - str_ref[1, :, B - 1, :])
+    edge_ref[...] = jnp.concatenate((p, shear, shear_top, n_top), axis=0).T
     to_scalar.wait()
-    early = scatter(0, 5, sems.at[5])
-    fetches[2].wait()
-    turn(5, lambda ci: mass_ref[ci])
-    fetches[3].wait()
-    turn(6, lambda ci: strength_ref[ci])
-    late = scatter(5, 2, sems.at[6])
-    early.wait()
-    late.wait()
+    waits = [scatter(0, 4, sems.at[5])]
+
+    def stage(slot, carry):
+        place = place_ref[0, slot]
+        stage_ref[place >> 1, pl.ds(place & 1, 1), :] = edge_ref[pl.ds(slot, 1), :]
+        return carry
+
+    lax.fori_loop(0, slots, stage, 0, unroll=8)
+    edges = pltpu.make_async_copy(stage_ref, send_ref.at[:, FIELDS], sems.at[7])
+    edges.start()
+    for field, ref in ((4, mass_ref), (5, strength_ref)):
+        fetches[field - 2].wait()
+        for s in range(8):
+            turn(field, (s, [ref[8 * q + s] for q in range(4)]))
+    waits.append(scatter(4, 2, sems.at[6]))
+    for wait in waits:
+        wait.wait()
+    edges.wait()
 
 
 def fetch_edges(tile_ref, recv_hbm, edge_ref, sem, places):
-    count = recv_hbm.shape[0] // 2
+    count = recv_hbm.shape[0]
 
     def fetch(i, carry):
         for side, (bx, by) in enumerate(places(i)):
-            source = (tile_ref[bx, by] & (count - 1)) * 2 + jnp.int32(bx >= BX_DEV // 2)
-            pltpu.make_async_copy(recv_hbm.at[source], edge_ref.at[side * BX_DEV + i], sem).start()
+            first = jnp.int32(bx >= BX_DEV // 2) * FIELDS
+            block = recv_hbm.at[tile_ref[bx, by] & (count - 1), pl.ds(first, FIELDS + 1)]
+            pltpu.make_async_copy(block, edge_ref.at[side * BX_DEV + i], sem).start()
         return carry
 
     lax.fori_loop(0, BX_DEV, fetch, 0, unroll=4)
-    pltpu.make_async_copy(recv_hbm.at[pl.ds(0, 2 * BX_DEV)], edge_ref, sem).wait()
+    pltpu.make_async_copy(edge_ref, edge_ref, sem).wait()
 
 
 def lat_kernel(tile_ref, recv_hbm, force_ref, north_ref, south_ref, edge_ref, sem):
@@ -179,26 +224,33 @@
     edges = (0, BY_DEV - 1)
     fetch_edges(tile_ref, recv_hbm, edge_ref, sem, lambda i: [(i, by) for by in edges])
 
-    def lat_rims(bx, carry):
-        for side, (by, ref, first) in enumerate(
-            zip(edges, (north_ref, south_ref), (0, B - HALO))
-        ):
-            for v in range(2):
-                total = jnp.zeros((8, LANES), jnp.float32)
-                for k in range(min(5, FIELDS + 2 - v * 5)):
-                    field = v * 5 + k
-                    if field >= FIELDS:
-                        got = force_ref[bx * BY_DEV + by, field - FIELDS]
-                    else:
-                        got = edge_ref[side * BX_DEV + bx, field]
-                        got = jnp.where(tile_ref[bx, by] >= 0, got, 0.0)
-                    mine = (in_group >= HALO * k) & (in_group < HALO * (k + 1))
-                    got = pltpu.roll(got, (HALO * k - first) % LANES, 1)
-                    total = jnp.where(mine, got, total)
-                ref[bx, v] = total
-        return carry
-
-    lax.fori_loop(0, BX_DEV, lat_rims, 0, unroll=2)
+    def lat_rims(half):
+        def body(bx, carry):
+            for side, (by, ref, first) in enumerate(
+                zip(edges, (north_ref, south_ref), (0, B - HALO))
+            ):
+                place = side * BX_DEV + bx
+                iced = tile_ref[bx, by] >= 0
+                for v in range(2):
+                    total = jnp.zeros((8, LANES), jnp.float32)
+                    for k in range(PER_RIM):
+                        field = v * PER_RIM + k
+                        if field >= FIELDS:
+                            got = force_ref[bx * BY_DEV + by, field - FIELDS]
+                        else:
+                            got = jnp.where(iced, edge_ref[place, half + field], 0.0)
+                        mine = (in_group >= HALO * k) & (in_group < HALO * (k + 1))
+                        got = pltpu.roll(got, (HALO * k - first) % LANES, 1)
+                        total = jnp.where(mine, got, total)
+                    ref[bx * 2 + v] = total
+                row = edge_ref[place, FIELDS * (1 - half), half : half + 1, :]
+                ref[BX_DEV * 2 + half, pl.ds(bx % 8, 1), :] = jnp.where(iced, row, 0.0)
+            return carry
+
+        return body
+
+    lax.fori_loop(0, BX_DEV // 2, lat_rims(0), 0, unroll=2)
+    lax.fori_loop(BX_DEV // 2, BX_DEV, lat_rims(1), 0, unroll=2)
 
 
 def lon_kernel(tile_ref, recv_hbm, force_ref, east_ref, west_ref, edge_ref, sem):
@@ -206,6 +258,7 @@
     edges = (0, BX_DEV - 1)
     fetch_edges(tile_ref, recv_hbm, edge_ref, sem, lambda i: [(bx, i) for bx in edges])
     for side, (bx, ref, group) in enumerate(zip(edges, (east_ref, west_ref), (0, 3))):
+        half = int(bx >= BX_DEV // 2)
         for part in range(4):
             for field in range(FIELDS + 2):
                 total = jnp.zeros((8, LANES), jnp.float32)
@@ -214,36 +267,46 @@
                     if field >= FIELDS:
                         got = force_ref[bx * BY_DEV + by, field - FIELDS]
                     else:
-                        got = edge_ref[side * BX_DEV + by, field]
+                        got = edge_ref[side * BX_DEV + by, half + field]
                         got = jnp.where(tile_ref[bx, by] >= 0, got, 0.0)
                     turned = pltpu.roll(got, ((p - group) * 32) % LANES, 1) if p != group else got
                     total = jnp.where(group_of == p, turned, total)
                 ref[field * 4 + part] = total
+        for by in range(BY_DEV):
+            row = edge_ref[side * BX_DEV + by, FIELDS * (1 - half), half : half + 1, :]
+            ref[4 * (FIELDS + 2) + by // 8, by % 8 : by % 8 + 1, :] = jnp.where(
+                tile_ref[bx, by] >= 0, row, 0.0
+            )
 
 
 def collect_kernel(tile_ref, recv_ref, force_ref, scr_ref):
-    count = recv_ref.shape[0] // 2
+    count = recv_ref.shape[0]
     rest = SIDE * SIDE * 8
-    for field in range(FIELDS + 2):
+    for field in range(FIELDS + 3):
         scr_ref[field, pl.ds(rest, GRID_LANES * 8 - rest), :] = jnp.zeros(
             (GRID_LANES * 8 - rest, LANES), jnp.float32
         )
 
-    def collect(bx, carry):
-        half = jnp.int32(bx >= BX_DEV // 2)
-        for by in range(BY_DEV):
-            number = tile_ref[bx, by]
-            source = (number & (count - 1)) * 2 + half
-            iced = number >= 0
-            for field in range(FIELDS):
-                scr_ref[field, grid_rows(bx, by), :] = jnp.where(
-                    iced, recv_ref[source, field], 0.0
-                )
-            for c in range(2):
-                scr_ref[FIELDS + c, grid_rows(bx, by), :] = force_ref[bx * BY_DEV + by, c]
-        return carry
-
-    lax.fori_loop(0, BX_DEV, collect, 0)
+    def collect(half):
+        def body(bx, carry):
+            for by in range(BY_DEV):
+                number = tile_ref[bx, by]
+                source = number & (count - 1)
+                iced = number >= 0
+                for field in range(FIELDS):
+                    scr_ref[field, grid_rows(bx, by), :] = jnp.where(
+                        iced, recv_ref[source, half * (FIELDS + 1) + field], 0.0
+                    )
+                for c in range(2):
+                    scr_ref[FIELDS + c, grid_rows(bx, by), :] = force_ref[bx * BY_DEV + by, c]
+                row = recv_ref[source, FIELDS, half : half + 1, :]
+                scr_ref[EDGE, grid_row(bx, by), :] = jnp.where(iced, row, 0.0)
+            return carry
+
+        return body
+
+    lax.fori_loop(0, BX_DEV // 2, collect(0), 0)
+    lax.fori_loop(BX_DEV // 2, BX_DEV, collect(1), 0)
 
 
 def force_kernel(force_ref, out_ref):
@@ -297,7 +360,7 @@
 
 
 def tile_kernel(
-    tile_ref,
+    place_ref,
     lat_ref,
     blocks_ref,
     cell_ref,
@@ -318,32 +381,42 @@
     fx_ref,
     fy_ref,
     w_ref,
+    gx_ref,
+    gy_ref,
     turn_ref,
+    edge_ref,
     send_ref,
     sems,
 ):
     del blocks_ref
     lane = lane_ids((8, LANES))
-    count = send_out_ref.shape[0] // 2
     tiles = GRID_LANES // LANES
     fields = FIELDS + 2
     spot = grid_rows
     in_group = lane % 32
 
-    def lat_rim(bx, north, south):
+    def lat_rim(bx, north, south, north_row, south_row):
         for field in range(fields):
-            v, k = divmod(field, 5)
+            v, k = divmod(field, PER_RIM)
             got = pltpu.roll(north(v), (-HALO * k) % LANES, 1)
             scr_ref[field, spot(bx, BY_DEV), :] = jnp.where(in_group < HALO, got, 0.0)
             got = pltpu.roll(south(v), (B - HALO - HALO * k) % LANES, 1)
             scr_ref[field, spot(bx, -1), :] = jnp.where(in_group >= B - HALO, got, 0.0)
+        scr_ref[EDGE, grid_row(bx, BY_DEV), :] = north_row
+        scr_ref[EDGE, grid_row(bx, -1), :] = south_row
 
     def lat_rims(bx, carry):
-        lat_rim(bx, lambda v: north_ref[bx, v], lambda v: south_ref[bx, v])
+        lat_rim(
+            bx,
+            lambda v: north_ref[bx * 2 + v],
+            lambda v: south_ref[bx * 2 + v],
+            north_ref[BX_DEV * 2 + bx // 8, pl.ds(bx % 8, 1), :],
+            south_ref[BX_DEV * 2 + bx // 8, pl.ds(bx % 8, 1), :],
+        )
         return carry
 
     lax.fori_loop(0, BX_DEV, lat_rims, 0)
-    for ref, bx, group in ((west_ref, -1, 3), (east_ref, BX_DEV, 0)):
+    for ref, bx, group, row in ((west_ref, -1, 3, 7), (east_ref, BX_DEV, 0, 0)):
         for field in range(fields):
             for part in range(4):
                 for p in range(4):
@@ -352,7 +425,29 @@
                     scr_ref[field, spot(bx, part * 4 + p), :] = jnp.where(
                         lane // 32 == group, got, 0.0
                     )
-        lat_rim(bx, lambda v: ref[RIM + v], lambda v: ref[RIM + 2 + v])
+        for by in range(BY_DEV):
+            scr_ref[EDGE, grid_row(bx, by), :] = ref[
+                fields * 4 + by // 8, by % 8 : by % 8 + 1, :
+            ]
+        lat_rim(
+            bx,
+            lambda v: ref[LON_RIM + v],
+            lambda v: ref[LON_RIM + 2 + v],
+            ref[LON_RIM + 4, row : row + 1, :],
+            ref[LON_RIM + 5, row : row + 1, :],
+        )
+
+    def turn_edges(t, carry):
+        start = pl.multiple_of(t * 8 * LANES, 8 * LANES)
+        edge_ref[:, pl.ds(pl.multiple_of(t * LANES, LANES), LANES)] = scr_ref[
+            EDGE, pl.ds(start, LANES, stride=8), :
+        ].T
+        return carry
+
+    lax.fori_loop(0, tiles, turn_edges, 0)
+    edge_ref[: 2 * B, :] = pltpu.roll(edge_ref[: 2 * B, :], SIDE, 1)
+    edge_ref[2 * B :, :] = pltpu.roll(edge_ref[2 * B :, :], 1, 1)
+    top_row = row_ids((8, LANES)) == 0
 
     def prepare(t, carry):
         cols = pl.ds(pl.multiple_of(t * LANES, LANES), LANES)
@@ -363,19 +458,30 @@
             ]
             for q in range(4):
                 plane = 8 * q + s
-                zonal, merid, total, diff, shear, mass, strength, fzonal, fmerid = [
+                zonal, merid, push_x, push_y, mass, strength, fzonal, fmerid = [
                     x[q * B : (q + 1) * B] for x in turned
                 ]
+
+                def less(push, base):
+                    row = edge_ref[base + plane : base + plane + 1, cols]
+                    top = push[:8] - jnp.where(top_row, row, 0.0)
+                    return jnp.concatenate((top, push[8:]), axis=0)
+
+                push_x, push_y = less(push_x, 2 * B), less(push_y, 3 * B)
+                if plane == 0:
+                    push_x = push_x - edge_ref[:B, cols]
+                    push_y = push_y - edge_ref[B : 2 * B, cols]
                 drag = jnp.where(mass > 0.0, 0.5 / (mass + 0.5), 0.0)
                 z_ref[plane + 1, :, cols] = zonal
                 m_ref[plane + 1, :, cols] = merid
-                p_ref[plane + 1, :, cols] = 0.5 * (total + diff)
-                q_ref[plane + 1, :, cols] = 0.5 * (total - diff)
-                s_ref[plane + 1, :, cols] = shear
+                for ref in (p_ref, q_ref, s_ref):
+                    ref[plane + 1, :, cols] = jnp.zeros((B, LANES), jnp.float32)
                 a_ref[plane, :, cols] = 2.0 * mass * drag
                 b_ref[plane, :, cols] = drag
                 fx_ref[plane, :, cols] = drag * fzonal
                 fy_ref[plane, :, cols] = drag * fmerid
+                gx_ref[plane, :, cols] = drag * push_x
+                gy_ref[plane, :, cols] = drag * push_y
                 w_ref[plane, :, cols] = 0.25 * strength
         return carry
 
@@ -419,7 +525,7 @@
             q_ref[k, :, cols] = 0.5 * q_ref[k, :, cols] + (mean - dev)
             s_ref[k, :, cols] = 0.5 * s_ref[k, :, cols] + quarter * she
 
-    def momentum_plane(k):
+    def momentum_plane(k, share):
         s_edge = pltpu.roll(s_ref[k, pl.ds(B - 8, 8), :], 1, 1)
         q_edge = pltpu.roll(q_ref[k, pl.ds(B - 8, 8), :], 1, 1)
         for t in range(tiles):
@@ -432,10 +538,14 @@
             )
             push_y = (s - s_ref[k - 1, :, cols]) + (q - south_of(q, q_edge[:, cols]))
             turn = a * turn_ref[:, cols]
-            z_ref[k, :, cols] = a * z + b * push_x + fx_ref[k - 1, :, cols] + turn * m
-            m_ref[k, :, cols] = a * m + b * push_y + fy_ref[k - 1, :, cols] - turn * z
-
-    def sweep(step, carry):
+            z_ref[k, :, cols] = (
+                a * z + b * push_x + (fx_ref[k - 1, :, cols] + share * gx_ref[k - 1, :, cols]) + turn * m
+            )
+            m_ref[k, :, cols] = (
+                a * m + b * push_y + (fy_ref[k - 1, :, cols] + share * gy_ref[k - 1, :, cols]) - turn * z
+            )
+
+    def sweep(step, share):
         for ref in (z_ref, m_ref):
             ref[B + 1] = pltpu.roll(ref[1], GRID_LANES - SIDE, 1)
         stress_plane(B)
@@ -445,15 +555,15 @@
 
         def body(k, carry):
             stress_plane(k + 1)
-            momentum_plane(k)
+            momentum_plane(k, share)
             return carry
 
         lax.fori_loop(1, B - 1, body, 0, unroll=True)
         for k in (B - 1, B):
-            momentum_plane(k)
-        return carry
-
-    lax.fori_loop(0, ITERS, sweep, 0)
+            momentum_plane(k, share)
+        return 0.5 * share
+
+    lax.fori_loop(0, ITERS, sweep, jnp.float32(0.5))
     copies = [
         pltpu.make_async_copy(ref.at[pl.ds(1, B)], vel_out_ref.at[c], sems.at[c])
         for c, ref in enumerate((z_ref, m_ref))
@@ -461,57 +571,68 @@
     for copy in copies:
         copy.start()
 
-    def turn_back(t, carry):
-        cols = pl.ds(pl.multiple_of(t * LANES, LANES), LANES)
-        for s in range(8):
-            rows = pl.ds(pl.multiple_of(t * 8 * LANES, 8 * LANES) + s, LANES, stride=8)
-            planes = [8 * q + s + 1 for q in range(4)]
-            p_all = jnp.concatenate([p_ref[k, :, cols] for k in planes], axis=0)
-            q_all = jnp.concatenate([q_ref[k, :, cols] for k in planes], axis=0)
-            s_all = jnp.concatenate([s_ref[k, :, cols] for k in planes], axis=0)
-            scr_ref[0, rows, :] = (p_all + q_all).T
-            scr_ref[1, rows, :] = (p_all - q_all).T
-            scr_ref[2, rows, :] = s_all.T
-        return carry
-
-    lax.fori_loop(0, tiles, turn_back, 0)
-
-    def deal(half):
-        def body(bx, carry):
+    def total(k, cols):
+        return p_ref[k, :, cols] + q_ref[k, :, cols]
+
+    def difference(k, cols):
+        return p_ref[k, :, cols] - q_ref[k, :, cols]
+
+    def shear(k, cols):
+        return s_ref[k, :, cols]
+
+    for c, value in enumerate((total, difference, shear)):
+        for t in range(tiles):
+            cols = slice(t * LANES, (t + 1) * LANES)
+            for s in range(8):
+                cells = [value(8 * q + s + 1, cols) for q in range(4)]
+                scr_ref[c, pl.ds(t * 8 * LANES + s, LANES, stride=8), :] = jnp.concatenate(
+                    cells, axis=0
+                ).T
+
+        def deal(bx, carry, c=c):
             for by in range(BY_DEV):
-                number = tile_ref[bx, by]
-                place = jnp.where(number >= 0, (number & (count - 1)) * 2 + half, 2 * count)
-                for c in range(3):
-                    send_ref[place, c] = scr_ref[c, spot(bx, by), :]
+                send_ref[place_ref[bx, by], c] = scr_ref[c, spot(bx, by), :]
             return carry
 
-        return body
-
-    lax.fori_loop(0, BX_DEV // 2, deal(0), 0)
-    lax.fori_loop(BX_DEV // 2, BX_DEV, deal(1), 0)
-    copies.append(
-        pltpu.make_async_copy(send_ref.at[pl.ds(0, 2 * count)], send_out_ref, sems.at[2])
-    )
-    copies[2].start()
+        lax.fori_loop(0, BX_DEV, deal, 0, unroll=2)
+        copies.append(
+            pltpu.make_async_copy(
+                send_ref.at[pl.ds(0, send_out_ref.shape[0]), c],
+                send_out_ref.at[:, c],
+                sems.at[2 + c],
+            )
+        )
+        copies[-1].start()
     for copy in copies:
         copy.wait()
 
 
-def unpack_kernel(pos_ref, recv_ref, out_ref, scr_ref):
+def unpack_kernel(pos_ref, recv_ref, stress_hbm, out_hbm, out_ref, stress_ref, scr_ref, sems):
     slots = out_ref.shape[-1]
+    old, done = [], []
+    for c in range(3):
+        old.append(pltpu.make_async_copy(stress_hbm.at[c], stress_ref.at[c], sems.at[c]))
+        done.append(pltpu.make_async_copy(out_ref.at[c], out_hbm.at[c], sems.at[3 + c]))
+        old[c].start()
 
     def gather(slot, carry):
         place = pos_ref[0, slot]
+        rows = pl.ds(pl.multiple_of(slot * 8, 8), 8)
         for c in range(3):
-            scr_ref[c, pl.ds(pl.multiple_of(slot * 8, 8), 8), :] = recv_ref[place, c]
+            scr_ref[c, rows, :] = recv_ref[place, c]
         return carry
 
-    lax.fori_loop(0, slots, gather, 0, unroll=4)
+    lax.fori_loop(0, slots, gather, 0, unroll=8)
     for c in range(3):
+        old[c].wait()
         for s in range(8):
             turned = scr_ref[c, pl.ds(s, slots, stride=8), :].T
             for q in range(4):
-                out_ref[c, 8 * q + s] = turned[q * B : (q + 1) * B]
+                ci = 8 * q + s
+                out_ref[c, ci] = turned[q * B : (q + 1) * B] + 0.5**ITERS * stress_ref[c, ci]
+        done[c].start()
+    for copy in done:
+        copy.wait()
 
 
 VMEM = pl.BlockSpec(memory_space=pltpu.VMEM)
@@ -546,7 +667,7 @@
     send, pos = pl.pallas_call(
         pack_kernel,
         out_shape=(
-            pltpu.HBM((devices * 2, FIELDS, 8, LANES), jnp.float32),
+            pltpu.HBM((devices, MESSAGE, 8, LANES), jnp.float32),
             jax.ShapeDtypeStruct((1, slots), jnp.int32),
         ),
         in_specs=[SMEM, VMEM] + [HBM] * 4,
@@ -557,14 +678,14 @@
             pltpu.VMEM(block, jnp.float32),
             pltpu.VMEM(block, jnp.float32),
             pltpu.VMEM((FIELDS, slots * 8, LANES), jnp.float32),
+            pltpu.VMEM((slots, LANES), jnp.float32),
+            pltpu.VMEM((devices, 8, LANES), jnp.float32),
             pltpu.SMEM((1, slots), jnp.int32),
-            pltpu.SemaphoreType.DMA((7,)),
+            pltpu.SemaphoreType.DMA((8,)),
         ],
         compiler_params=params(61),
     )(own_index.reshape(1).astype(jnp.int32), owner, velocity, stress, mass, strength)
-    recv = lax.all_to_all(
-        send.reshape(devices, 2 * FIELDS, 8, LANES), ("lon", "lat"), 0, 0, tiled=True
-    ).reshape(devices * 2, FIELDS, 8, LANES)
+    recv = lax.all_to_all(send, ("lon", "lat"), 0, 0, tiled=True)
 
     force_blocks = pl.pallas_call(
         force_kernel,
@@ -575,12 +696,12 @@
         compiler_params=params(12),
     )(forcing)
     edge_scratch = [
-        pltpu.VMEM((2 * BX_DEV, FIELDS, 8, LANES), jnp.float32),
+        pltpu.VMEM((2 * BX_DEV, FIELDS + 1, 8, LANES), jnp.float32),
         pltpu.SemaphoreType.DMA(()),
     ]
     north, south = pl.pallas_call(
         lat_kernel,
-        out_shape=(f32(BX_DEV, 2, 8, LANES),) * 2,
+        out_shape=(f32(LAT_RIM, 8, LANES),) * 2,
         in_specs=[SMEM, HBM, VMEM],
         out_specs=(VMEM,) * 2,
         scratch_shapes=edge_scratch,
@@ -589,7 +710,7 @@
     )(my_tile, recv, force_blocks)
     east, west = pl.pallas_call(
         lon_kernel,
-        out_shape=(f32(RIM, 8, LANES),) * 2,
+        out_shape=(f32(LON_RIM, 8, LANES),) * 2,
         in_specs=[SMEM, HBM, VMEM],
         out_specs=(VMEM,) * 2,
         scratch_shapes=edge_scratch,
@@ -598,7 +719,7 @@
     )(my_tile, recv, force_blocks)
     blocks = pl.pallas_call(
         collect_kernel,
-        out_shape=pltpu.VMEM((FIELDS + 2, GRID_LANES * 8, LANES), jnp.float32),
+        out_shape=pltpu.VMEM((FIELDS + 3, GRID_LANES * 8, LANES), jnp.float32),
         in_specs=[SMEM, VMEM, VMEM],
         out_specs=VMEM,
         cost_estimate=cost(24),
@@ -609,18 +730,27 @@
     got_north = lax.ppermute(north, "lat", [(k, j) for j, k in ahead])
     got_south = lax.ppermute(south, "lat", ahead)
     ring = [(i, (i + 1) % lon_count) for i in range(lon_count)]
-    east = jnp.concatenate((east, got_north[0], got_south[0]), axis=0)
-    west = jnp.concatenate((west, got_north[-1], got_south[-1]), axis=0)
+    end = BX_DEV * 2
+
+    def with_corners(rim, bx):
+        pairs = [x[bx * 2 : bx * 2 + 2] for x in (got_north, got_south)]
+        rows = [x[end + bx // 8 : end + bx // 8 + 1] for x in (got_north, got_south)]
+        return jnp.concatenate([rim] + pairs + rows, axis=0)
+
+    east = with_corners(east, 0)
+    west = with_corners(west, BX_DEV - 1)
     got_east = lax.ppermute(east, "lon", [(k, i) for i, k in ring])
     got_west = lax.ppermute(west, "lon", ring)
     grid = np.arange(GRID_LANES) % SIDE - 1
     cells = jnp.asarray(grid[None, :] * B + np.arange(B)[:, None], jnp.int32)
     state = (B + 2, B, GRID_LANES)
     constant = (B, B, GRID_LANES)
+    half = (jnp.arange(BX_DEV, dtype=jnp.int32) // (BX_DEV // 2))[:, None]
+    places = jnp.where(my_tile >= 0, (my_tile & (devices - 1)) * 2 + half, 2 * devices)
     _, cell_velocity, back = pl.pallas_call(
         tile_kernel,
         out_shape=(
-            pltpu.VMEM((FIELDS + 2, GRID_LANES * 8, LANES), jnp.float32),
+            pltpu.VMEM((FIELDS + 3, GRID_LANES * 8, LANES), jnp.float32),
             pltpu.HBM((2, B, B, GRID_LANES), jnp.float32),
             pltpu.HBM((devices * 2, 3, 8, LANES), jnp.float32),
         ),
@@ -628,15 +758,16 @@
         out_specs=(VMEM, HBM, HBM),
         input_output_aliases={2: 0},
         scratch_shapes=[pltpu.VMEM(state, jnp.float32)] * 5
-        + [pltpu.VMEM(constant, jnp.float32)] * 5
+        + [pltpu.VMEM(constant, jnp.float32)] * 7
         + [
             pltpu.VMEM((B, GRID_LANES), jnp.float32),
+            pltpu.VMEM((4 * B, GRID_LANES), jnp.float32),
             pltpu.VMEM((devices * 2 + 1, 3, 8, LANES), jnp.float32),
-            pltpu.SemaphoreType.DMA((3,)),
+            pltpu.SemaphoreType.DMA((5,)),
         ],
         compiler_params=params(26),
     )(
-        my_tile,
+        places,
         jnp.stack((lat_index, lat_count)).astype(jnp.int32),
         blocks,
         cells,
@@ -659,12 +790,17 @@
     )(cell_velocity)
     new_stress = pl.pallas_call(
         unpack_kernel,
-        out_shape=f32(3, B, B, slots),
-        in_specs=[SMEM, VMEM],
-        out_specs=VMEM,
-        scratch_shapes=[pltpu.VMEM((3, slots * 8, LANES), jnp.float32)],
+        out_shape=pltpu.HBM((3,) + block, jnp.float32),
+        in_specs=[SMEM, VMEM, HBM],
+        out_specs=HBM,
+        scratch_shapes=[
+            pltpu.VMEM((3,) + block, jnp.float32),
+            pltpu.VMEM((3,) + block, jnp.float32),
+            pltpu.VMEM((3, slots * 8, LANES), jnp.float32),
+            pltpu.SemaphoreType.DMA((6,)),
+        ],
         compiler_params=params(16),
-    )(pos, returned)
+    )(pos, returned, pltpu.with_memory_space_constraint(stress, pltpu.HBM))
     return (new_velocity, new_stress)
 
 

time: 209 us -> 204 us (0.976)
  waiting for transfers between devices: 116 us -> 110 us
  Pallas kernels: 53.8 us -> 57.4 us
  starting transfers between devices: 33.3 us -> 30.9 us
    all_to_all x1, waiting for transfers between devices: 81.4 us -> 75.7 us  [on_device(): recv = lax.all_to_all(send, ('lon', 'lat'), 0, 0, tiled=True)]
    pallas_call x6, Pallas kernels: 45.9 us -> 49.5 us  [the longest x1 29.8 us: on_device(): pl.pallas_call(tile_kernel, out_shape=(pltpu.VMEM((FIELDS + 3, GRID_LANES...]
where the time goes in v4:
time: 204 us
  waiting for transfers between devices  110 us (54%)
  Pallas kernels  57.4 us (28%)
  starting transfers between devices  30.9 us (15%)
  local copies, waits for them, and re-layouts  3.51 us (2%)
    all_to_all x1, waiting for transfers between devices, on_device(): recv = lax.all_to_all(send, ('lon', 'lat'), 0, 0, tiled=True)  75.7 us
    all_to_all x1, waiting for transfers between devices, on_device(): lax.all_to_all(back.reshape(devices, 6, 8, LANES), ('lon', 'lat'), 0, 0,...  34.7 us
    pallas_call x1, Pallas kernels, on_device(): pl.pallas_call(tile_kernel, out_shape=(pltpu.VMEM((FIELDS + 3, GRID_LANES...  29.8 us
    all_to_all x1, starting transfers between devices, on_device(): recv = lax.all_to_all(send, ('lon', 'lat'), 0, 0, tiled=True)  11.9 us
    all_to_all x1, starting transfers between devices, on_device(): lax.all_to_all(back.reshape(devices, 6, 8, LANES), ('lon', 'lat'), 0, 0,...  8.03 us
    pallas_call x1, Pallas kernels, on_device(): pl.pallas_call(pack_kernel, out_shape=(pltpu.HBM((devices, MESSAGE, 8, LA...  5.94 us
    pallas_call x1, Pallas kernels, on_device(): pl.pallas_call(velocity_kernel, out_shape=f32(2, ROWS, COLS), in_specs=[V...  4.96 us
    ppermute x1, starting transfers between devices, on_device(): got_east = lax.ppermute(east, 'lon', [(k, i) for i, k in ring])  4.77 us
  transfers between devices with their start and end apart: 6, of which 2 were waited for; matrix products, arithmetic and copies ran while one was open for 0% of the time, Pallas kernels for 7%

profile of v4, /device:TPU:1, one launch (start us, length us, event | category | flops | bytes accessed | tf_op | source)
XLA Modules:
  0.0 203.9 jit_solution(8168863792665852012)
XLA Ops:
  0.6 5.9 %shard_map.86 = (f32[128,13,8,128]{3,2,1,0:T(8,128)}, s32[1,128]{1,0:T(1,128)}) custom-call(s32[1]{0:T(128)} %bitcast.1.own_ref, s32[256,128]{1,0:T(8,128)} %owner_ref.1, f32[2,32,32,128]{3,2,1,0:T(8,128)} %vel_hbm.1, f32[3,32,32,128]{3,2,1,0:T(8,128)} %stress_hbm.1, f32[32,32,128]{2,1,0:T(8,128)} %mass_hbm.1, f32[32,32,128]{2,1,0:T(8,128)} %strength_hbm.1), custom_call_target="tpu_custom_call" | custom-call | tf_op jit(solution)/shard_map/pallas_call | solution.py:667
  6.6 11.9 %all-to-all-start = ((f32[128,13,8,128]{3,2,1,0:T(8,128)}), f32[128,13,8,128]{3,2,1,0:T(8,128)}, u32[]{:S(2)}, u32[]{:S(2)}) async-start(f32[128,13,8,128]{3,2,1,0:T(8,128)} %get-tuple-element.10), calls=%async_computation | async-start | bytes 13631488 | tf_op jit(solution)/shard_map/all_to_all | solution.py:688
  18.5 0.0 copy-start.1
  18.5 1.6 copy-done.1
  20.1 2.9 %shard_map.87.force_ref = f32[256,2,8,128]{3,2,1,0:T(8,128)S(1)} custom-call(f32[2,512,512]{2,1,0:T(8,128)S(1)} %copy-done.1), custom_call_target="tpu_custom_call" | custom-call | flops 10000000 | bytes 4194304 | tf_op jit(solution)/shard_map/pallas_call | solution.py:690
  23.0 0.8 add_select_fusion
  23.8 75.7 %all-to-all-done.recv_ref.recv_hbm = f32[128,13,8,128]{3,2,1,0:T(8,128)} async-done(((f32[128,13,8,128]{3,2,1,0:T(8,128)}), f32[128,13,8,128]{3,2,1,0:T(8,128)}, u32[]{:S(2)}, u32[]{:S(2)}) %all-to-all-start) | async-done | bytes 6815776 | tf_op jit(solution)/shard_map/all_to_all | solution.py:688
  99.5 3.7 %shard_map.89 = (f32[34,8,128]{2,1,0:T(8,128)S(1)}, f32[34,8,128]{2,1,0:T(8,128)S(1)}) custom-call(s32[16,16]{1,0:T(8,128)S(1)} %get-tuple-element.19.tile_ref, f32[128,13,8,128]{3,2,1,0:T(8,128)} %all-to-all-done.recv_ref.recv_hbm, f32[256,2,8,128]{3,2,1,0:T(8,128)S(1)} %shard_map.87.force_ref), custom_call_target="tpu_custom_call" | custom-call | flops 10000000 | bytes 4194304 | tf_op jit(solution)/shard_map/pallas_call | solution.py:702
  103.1 1.9 collective-permute-start
  105.1 4.2 %collective-permute-start.1 = (f32[34,8,128]{2,1,0:T(8,128)S(1)}, f32[34,8,128]{2,1,0:T(8,128)S(1)}, u32[]{:S(2)}, u32[]{:S(2)}) collective-permute-start(f32[34,8,128]{2,1,0:T(8,128)S(1)} %get-tuple-element.12), channel_id=1, source_target_pairs={{0,1},{1,2},{2,3},{3,4},{4,5},{5,6},{6,7},{8,9},{9,10},{10,11},{11... | collective-permute-start | bytes 417800 | tf_op jit(solution)/shard_map/ppermute | solution.py:731
  109.3 3.1 %shard_map.90 = (f32[34,8,128]{2,1,0:T(8,128)S(1)}, f32[34,8,128]{2,1,0:T(8,128)S(1)}) custom-call(s32[16,16]{1,0:T(8,128)S(1)} %get-tuple-element.19.tile_ref, f32[128,13,8,128]{3,2,1,0:T(8,128)} %all-to-all-done.recv_ref.recv_hbm, f32[256,2,8,128]{3,2,1,0:T(8,128)S(1)} %shard_map.87.force_ref), custom_call_target="tpu_custom_call" | custom-call | flops 10000000 | bytes 6291456 | tf_op jit(solution)/shard_map/pallas_call | solution.py:711
  112.4 0.0 collective-permute-done.north_ref
  112.5 0.0 collective-permute-done.1.south_ref
  112.5 0.1 collective-permute-start.3
  112.6 4.8 %collective-permute-start.2 = (f32[40,8,128]{2,1,0:T(8,128)S(1)}, f32[40,8,128]{2,1,0:T(8,128)S(1)}, u32[]{:S(2)}, u32[]{:S(2)}) collective-permute-start(f32[40,8,128]{2,1,0:T(8,128)S(1)} %get-tuple-element.21), channel_id=1, source_target_pairs={{8,0},{16,8},{24,16},{32,24},{40,32},{48,40},{56,48},{64,56},{72,6... | collective-permute-start | bytes 491528 | tf_op jit(solution)/shard_map/ppermute | solution.py:742
  117.4 0.1 pad_add_fusion.lat_ref
  117.4 0.0 copy-start.2
  117.4 4.0 %shard_map.88.blocks_ref = f32[9,3072,128]{2,1,0:T(8,128)S(1)} custom-call(s32[16,16]{1,0:T(8,128)S(1)} %get-tuple-element.19.tile_ref, f32[128,13,8,128]{3,2,1,0:T(8,128)} %all-to-all-done.recv_ref.recv_hbm, f32[256,2,8,128]{3,2,1,0:T(8,128)S(1)} %shard_map.87.force_ref), custom_call_target="tpu_custom_call" | custom-call | flops 10000000 | bytes 25165824 | tf_op jit(solution)/shard_map/pallas_call | solution.py:720
  121.5 0.0 collective-permute-done.3.west_ref
  121.5 0.0 collective-permute-done.2.east_ref
  121.5 0.0 copy-done.2
  121.5 29.8 %shard_map.91 = (f32[9,3072,128]{2,1,0:T(8,128)S(1)}, f32[2,32,32,384]{3,2,1,0:T(8,128)}, f32[256,3,8,128]{3,2,1,0:T(8,128)}) custom-call(s32[16,16]{1,0:T(8,128)S(1)} %get-tuple-element.18.place_ref, s32[2]{0:T(128)S(1)} %pad_add_fusion.lat_ref, f32[9,3072,128]{2,1,0:T(8,128)S(1)} %shard_map.88.blocks_ref, ...), custom_call_target="tpu_custom_call", output_to_operand_aliasing={{0}: (2, {})} | custom-call | tf_op jit(solution)/shard_map/pallas_call | solution.py:750
  151.3 8.0 %all-to-all-start.1 = ((f32[128,6,8,128]{3,2,1,0:T(8,128)}), f32[128,6,8,128]{3,2,1,0:T(8,128)S(1)}, u32[]{:S(2)}, u32[]{:S(2)}) async-start(f32[128,6,8,128]{3,2,1,0:T(8,128)} %bitcast.5), calls=%async_computation.1 | async-start | bytes 6291456 | tf_op jit(solution)/shard_map/all_to_all | solution.py:779
  159.3 0.0 copy-start.3
  159.3 0.0 copy-start
  159.3 1.9 copy-done
  161.2 5.0 %shard_map.92 = f32[2,512,512]{2,1,0:T(8,128)} custom-call(f32[2,32,32,384]{3,2,1,0:T(8,128)S(1)} %copy-done), custom_call_target="tpu_custom_call" | custom-call | flops 10000000 | bytes 6291456 | tf_op jit(solution)/shard_map/pallas_call | solution.py:782
  166.2 34.7 %all-to-all-done.1 = f32[128,6,8,128]{3,2,1,0:T(8,128)S(1)} async-done(((f32[128,6,8,128]{3,2,1,0:T(8,128)}), f32[128,6,8,128]{3,2,1,0:T(8,128)S(1)}, u32[]{:S(2)}, u32[]{:S(2)}) %all-to-all-start.1) | async-done | bytes 3145760 | tf_op jit(solution)/shard_map/all_to_all | solution.py:779
  200.8 0.0 copy-done.3
  200.8 3.0 %shard_map.93 = f32[3,32,32,128]{3,2,1,0:T(8,128)} custom-call(s32[1,128]{1,0:T(1,128)S(1)} %copy-done.3, f32[256,3,8,128]{3,2,1,0:T(8,128)S(1)} %bitcast.4, f32[3,32,32,128]{3,2,1,0:T(8,128)} %stress_hbm.1), custom_call_target="tpu_custom_call" | custom-call | tf_op jit(solution)/shard_map/pallas_call | solution.py:791
  (6 shorter events, 0.0 us)
Async XLA Ops:
  6.6 92.9 %all-to-all-start = ((f32[128,13,8,128]{3,2,1,0:T(8,128)}), f32[128,13,8,128]{3,2,1,0:T(8,128)}, u32[]{:S(2)}, u32[]{:S(2)}) async-start(f32[128,13,8,128]{3,2,1,0:T(8,128)} %get-tuple-element.10), calls=%async_computation | async-start | bytes 13631488 | tf_op jit(solution)/shard_map/all_to_all | solution.py:688
  18.5 1.6 copy-start.1
  103.1 9.3 %collective-permute-start = (f32[34,8,128]{2,1,0:T(8,128)S(1)}, f32[34,8,128]{2,1,0:T(8,128)S(1)}, u32[]{:S(2)}, u32[]{:S(2)}) collective-permute-start(f32[34,8,128]{2,1,0:T(8,128)S(1)} %get-tuple-element.11), channel_id=1, source_target_pairs={{1,0},{2,1},{3,2},{4,3},{5,4},{6,5},{7,6},{9,8},{10,9},{11,10},{12... | collective-permute-start | bytes 417800 | tf_op jit(solution)/shard_map/ppermute | solution.py:730
  105.1 7.4 %collective-permute-start.1 = (f32[34,8,128]{2,1,0:T(8,128)S(1)}, f32[34,8,128]{2,1,0:T(8,128)S(1)}, u32[]{:S(2)}, u32[]{:S(2)}) collective-permute-start(f32[34,8,128]{2,1,0:T(8,128)S(1)} %get-tuple-element.12), channel_id=1, source_target_pairs={{0,1},{1,2},{2,3},{3,4},{4,5},{5,6},{6,7},{8,9},{9,10},{10,11},{11... | collective-permute-start | bytes 417800 | tf_op jit(solution)/shard_map/ppermute | solution.py:731
  112.5 9.0 %collective-permute-start.3 = (f32[40,8,128]{2,1,0:T(8,128)S(1)}, f32[40,8,128]{2,1,0:T(8,128)S(1)}, u32[]{:S(2)}, u32[]{:S(2)}) collective-permute-start(f32[40,8,128]{2,1,0:T(8,128)S(1)} %get-tuple-element.20), channel_id=1, source_target_pairs={{0,8},{8,16},{16,24},{24,32},{32,40},{40,48},{48,56},{56,64},{64,7... | collective-permute-start | bytes 491528 | tf_op jit(solution)/shard_map/ppermute | solution.py:743
  112.6 8.9 %collective-permute-start.2 = (f32[40,8,128]{2,1,0:T(8,128)S(1)}, f32[40,8,128]{2,1,0:T(8,128)S(1)}, u32[]{:S(2)}, u32[]{:S(2)}) collective-permute-start(f32[40,8,128]{2,1,0:T(8,128)S(1)} %get-tuple-element.21), channel_id=1, source_target_pairs={{8,0},{16,8},{24,16},{32,24},{40,32},{48,40},{56,48},{64,56},{72,6... | collective-permute-start | bytes 491528 | tf_op jit(solution)/shard_map/ppermute | solution.py:742
  117.4 4.1 %copy-start.2 = (s32[32,384]{1,0:T(8,128)S(1)}, s32[32,384]{1,0:T(8,128)}, u32[]{:S(2)}) copy-start(s32[32,384]{1,0:T(8,128)} %constant.44.clone.cell_ref) | copy-start | bytes 147460
  151.3 49.6 %all-to-all-start.1 = ((f32[128,6,8,128]{3,2,1,0:T(8,128)}), f32[128,6,8,128]{3,2,1,0:T(8,128)S(1)}, u32[]{:S(2)}, u32[]{:S(2)}) async-start(f32[128,6,8,128]{3,2,1,0:T(8,128)} %bitcast.5), calls=%async_computation.1 | async-start | bytes 6291456 | tf_op jit(solution)/shard_map/all_to_all | solution.py:779
  159.3 41.5 %copy-start.3 = (s32[1,128]{1,0:T(1,128)S(1)}, s32[1,128]{1,0:T(1,128)}, u32[]{:S(2)}) copy-start(s32[1,128]{1,0:T(1,128)} %get-tuple-element.16.pos_ref) | copy-start | bytes 1540
  159.3 1.9 copy-start

commit v5 on v4

--- a/solution.py
+++ b/solution.py
@@ -219,18 +219,18 @@
     pltpu.make_async_copy(edge_ref, edge_ref, sem).wait()
 
 
-def lat_kernel(tile_ref, recv_hbm, force_ref, north_ref, south_ref, edge_ref, sem):
+def lat_kernel(tile_ref, even_ref, recv_hbm, force_ref, near_ref, far_ref, edge_ref, sem):
     in_group = lane_ids((8, LANES)) % 32
     edges = (0, BY_DEV - 1)
     fetch_edges(tile_ref, recv_hbm, edge_ref, sem, lambda i: [(i, by) for by in edges])
 
     def lat_rims(half):
         def body(bx, carry):
-            for side, (by, ref, first) in enumerate(
-                zip(edges, (north_ref, south_ref), (0, B - HALO))
-            ):
+            found = []
+            for side, (by, first) in enumerate(zip(edges, (0, B - HALO))):
                 place = side * BX_DEV + bx
                 iced = tile_ref[bx, by] >= 0
+                vectors = []
                 for v in range(2):
                     total = jnp.zeros((8, LANES), jnp.float32)
                     for k in range(PER_RIM):
@@ -242,9 +242,15 @@
                         mine = (in_group >= HALO * k) & (in_group < HALO * (k + 1))
                         got = pltpu.roll(got, (HALO * k - first) % LANES, 1)
                         total = jnp.where(mine, got, total)
-                    ref[bx * 2 + v] = total
+                    vectors.append(total)
                 row = edge_ref[place, FIELDS * (1 - half), half : half + 1, :]
-                ref[BX_DEV * 2 + half, pl.ds(bx % 8, 1), :] = jnp.where(iced, row, 0.0)
+                found.append(vectors + [jnp.where(iced, row, 0.0)])
+            even = even_ref[0] == 1
+            for ref, kept in ((near_ref, even), (far_ref, jnp.logical_not(even))):
+                first_v, second_v, row = [jnp.where(kept, y, x) for x, y in zip(*found)]
+                ref[bx * 2] = first_v
+                ref[bx * 2 + 1] = second_v
+                ref[BX_DEV * 2 + half, pl.ds(bx % 8, 1), :] = row
             return carry
 
         return body
@@ -364,8 +370,8 @@
     lat_ref,
     blocks_ref,
     cell_ref,
-    north_ref,
-    south_ref,
+    near_ref,
+    far_ref,
     east_ref,
     west_ref,
     scr_ref,
@@ -395,12 +401,19 @@
     spot = grid_rows
     in_group = lane % 32
 
-    def lat_rim(bx, north, south, north_row, south_row):
+    even = lat_ref[2] == 1
+
+    def either(x, y):
+        return jnp.where(even, x, y), jnp.where(even, y, x)
+
+    def lat_rim(bx, near, far, near_row, far_row):
+        north_row, south_row = either(near_row, far_row)
         for field in range(fields):
             v, k = divmod(field, PER_RIM)
-            got = pltpu.roll(north(v), (-HALO * k) % LANES, 1)
+            north, south = either(near(v), far(v))
+            got = pltpu.roll(north, (-HALO * k) % LANES, 1)
             scr_ref[field, spot(bx, BY_DEV), :] = jnp.where(in_group < HALO, got, 0.0)
-            got = pltpu.roll(south(v), (B - HALO - HALO * k) % LANES, 1)
+            got = pltpu.roll(south, (B - HALO - HALO * k) % LANES, 1)
             scr_ref[field, spot(bx, -1), :] = jnp.where(in_group >= B - HALO, got, 0.0)
         scr_ref[EDGE, grid_row(bx, BY_DEV), :] = north_row
         scr_ref[EDGE, grid_row(bx, -1), :] = south_row
@@ -408,10 +421,10 @@
     def lat_rims(bx, carry):
         lat_rim(
             bx,
-            lambda v: north_ref[bx * 2 + v],
-            lambda v: south_ref[bx * 2 + v],
-            north_ref[BX_DEV * 2 + bx // 8, pl.ds(bx % 8, 1), :],
-            south_ref[BX_DEV * 2 + bx // 8, pl.ds(bx % 8, 1), :],
+            lambda v: near_ref[bx * 2 + v],
+            lambda v: far_ref[bx * 2 + v],
+            near_ref[BX_DEV * 2 + bx // 8, pl.ds(bx % 8, 1), :],
+            far_ref[BX_DEV * 2 + bx // 8, pl.ds(bx % 8, 1), :],
         )
         return carry
 
@@ -537,12 +550,12 @@
                 s - south_of(s, s_edge[:, cols])
             )
             push_y = (s - s_ref[k - 1, :, cols]) + (q - south_of(q, q_edge[:, cols]))
-            turn = a * turn_ref[:, cols]
+            turn = turn_ref[:, cols]
             z_ref[k, :, cols] = (
-                a * z + b * push_x + (fx_ref[k - 1, :, cols] + share * gx_ref[k - 1, :, cols]) + turn * m
+                a * (z + turn * m) + b * push_x + (fx_ref[k - 1, :, cols] + share * gx_ref[k - 1, :, cols])
             )
             m_ref[k, :, cols] = (
-                a * m + b * push_y + (fy_ref[k - 1, :, cols] + share * gy_ref[k - 1, :, cols]) - turn * z
+                a * (m - turn * z) + b * push_y + (fy_ref[k - 1, :, cols] + share * gy_ref[k - 1, :, cols])
             )
 
     def sweep(step, share):
@@ -699,15 +712,16 @@
         pltpu.VMEM((2 * BX_DEV, FIELDS + 1, 8, LANES), jnp.float32),
         pltpu.SemaphoreType.DMA(()),
     ]
-    north, south = pl.pallas_call(
+    even = 1 - lat_index % 2
+    near, far = pl.pallas_call(
         lat_kernel,
         out_shape=(f32(LAT_RIM, 8, LANES),) * 2,
-        in_specs=[SMEM, HBM, VMEM],
+        in_specs=[SMEM, SMEM, HBM, VMEM],
         out_specs=(VMEM,) * 2,
         scratch_shapes=edge_scratch,
         cost_estimate=cost(4),
         compiler_params=params(8),
-    )(my_tile, recv, force_blocks)
+    )(my_tile, even.reshape(1).astype(jnp.int32), recv, force_blocks)
     east, west = pl.pallas_call(
         lon_kernel,
         out_shape=(f32(LON_RIM, 8, LANES),) * 2,
@@ -726,15 +740,18 @@
         compiler_params=params(12),
     )(my_tile, recv, force_blocks)
 
-    ahead = [(j, j + 1) for j in range(lat_count - 1)]
-    got_north = lax.ppermute(north, "lat", [(k, j) for j, k in ahead])
-    got_south = lax.ppermute(south, "lat", ahead)
+    def exchange(rim, first):
+        pairs = [(j, j + 1) for j in range(first, lat_count - 1, 2)]
+        return lax.ppermute(rim, "lat", pairs + [(k, j) for j, k in pairs])
+
+    got_near = exchange(near, 0)
+    got_far = exchange(far, 1)
     ring = [(i, (i + 1) % lon_count) for i in range(lon_count)]
     end = BX_DEV * 2
 
     def with_corners(rim, bx):
-        pairs = [x[bx * 2 : bx * 2 + 2] for x in (got_north, got_south)]
-        rows = [x[end + bx // 8 : end + bx // 8 + 1] for x in (got_north, got_south)]
+        pairs = [x[bx * 2 : bx * 2 + 2] for x in (got_near, got_far)]
+        rows = [x[end + bx // 8 : end + bx // 8 + 1] for x in (got_near, got_far)]
         return jnp.concatenate([rim] + pairs + rows, axis=0)
 
     east = with_corners(east, 0)
@@ -768,11 +785,11 @@
         compiler_params=params(26),
     )(
         places,
-        jnp.stack((lat_index, lat_count)).astype(jnp.int32),
+        jnp.stack((lat_index, lat_count, even)).astype(jnp.int32),
         blocks,
         cells,
-        got_north,
-        got_south,
+        got_near,
+        got_far,
         got_east,
         got_west,
     )

time: 204 us -> 202 us (level)
  no operation moved by 1% of the time
where the time goes in v5:
time: 202 us
  waiting for transfers between devices  110 us (54%)
  Pallas kernels  57.2 us (28%)
  starting transfers between devices  28.9 us (14%)
  local copies, waits for them, and re-layouts  3.51 us (2%)
    all_to_all x1, waiting for transfers between devices, on_device(): recv = lax.all_to_all(send, ('lon', 'lat'), 0, 0, tiled=True)  75.7 us
    all_to_all x1, waiting for transfers between devices, on_device(): lax.all_to_all(back.reshape(devices, 6, 8, LANES), ('lon', 'lat'), 0, 0,...  34.7 us
    pallas_call x1, Pallas kernels, on_device(): pl.pallas_call(tile_kernel, out_shape=(pltpu.VMEM((FIELDS + 3, GRID_LANES...  29.4 us
    all_to_all x1, starting transfers between devices, on_device(): recv = lax.all_to_all(send, ('lon', 'lat'), 0, 0, tiled=True)  11.9 us
    all_to_all x1, starting transfers between devices, on_device(): lax.all_to_all(back.reshape(devices, 6, 8, LANES), ('lon', 'lat'), 0, 0,...  8 us
    pallas_call x1, Pallas kernels, on_device(): pl.pallas_call(pack_kernel, out_shape=(pltpu.HBM((devices, MESSAGE, 8, LA...  5.93 us
    pallas_call x1, Pallas kernels, on_device(): pl.pallas_call(velocity_kernel, out_shape=f32(2, ROWS, COLS), in_specs=[V...  4.96 us
    ppermute x1, starting transfers between devices, on_device(): got_east = lax.ppermute(east, 'lon', [(k, i) for i, k in ring])  4.77 us
  transfers between devices with their start and end apart: 6, of which 2 were waited for; matrix products, arithmetic and copies ran while one was open for 0% of the time, Pallas kernels for 7%

profile of v5, /device:TPU:1, one launch (start us, length us, event | category | flops | bytes accessed | tf_op | source)
XLA Modules:
  0.0 201.6 jit_solution(7615201582726488425)
XLA Ops:
  0.6 5.9 %shard_map.86 = (f32[128,13,8,128]{3,2,1,0:T(8,128)}, s32[1,128]{1,0:T(1,128)}) custom-call(s32[1]{0:T(128)} %bitcast.2.own_ref, s32[256,128]{1,0:T(8,128)} %owner_ref.1, f32[2,32,32,128]{3,2,1,0:T(8,128)} %vel_hbm.1, f32[3,32,32,128]{3,2,1,0:T(8,128)} %stress_hbm.1, f32[32,32,128]{2,1,0:T(8,128)} %mass_hbm.1, f32[32,32,128]{2,1,0:T(8,128)} %strength_hbm.1), custom_call_target="tpu_custom_call" | custom-call | tf_op jit(solution)/shard_map/pallas_call | solution.py:680
  6.6 11.9 %all-to-all-start = ((f32[128,13,8,128]{3,2,1,0:T(8,128)}), f32[128,13,8,128]{3,2,1,0:T(8,128)}, u32[]{:S(2)}, u32[]{:S(2)}) async-start(f32[128,13,8,128]{3,2,1,0:T(8,128)} %get-tuple-element.10), calls=%async_computation | async-start | bytes 13631488 | tf_op jit(solution)/shard_map/all_to_all | solution.py:701
  18.5 0.0 copy-start.1
  18.5 1.6 copy-done.1
  20.1 2.9 %shard_map.87.force_ref = f32[256,2,8,128]{3,2,1,0:T(8,128)S(1)} custom-call(f32[2,512,512]{2,1,0:T(8,128)S(1)} %copy-done.1), custom_call_target="tpu_custom_call" | custom-call | flops 10000000 | bytes 4194304 | tf_op jit(solution)/shard_map/pallas_call | solution.py:703
  23.1 0.8 add_select_fusion
  23.8 75.7 %all-to-all-done.recv_ref.recv_hbm = f32[128,13,8,128]{3,2,1,0:T(8,128)} async-done(((f32[128,13,8,128]{3,2,1,0:T(8,128)}), f32[128,13,8,128]{3,2,1,0:T(8,128)}, u32[]{:S(2)}, u32[]{:S(2)}) %all-to-all-start) | async-done | bytes 6815776 | tf_op jit(solution)/shard_map/all_to_all | solution.py:701
  99.5 3.8 %shard_map.89 = (f32[34,8,128]{2,1,0:T(8,128)S(1)}, f32[34,8,128]{2,1,0:T(8,128)S(1)}) custom-call(s32[16,16]{1,0:T(8,128)S(1)} %get-tuple-element.19.tile_ref, s32[1]{0:T(128)} %bitcast.1.even_ref, f32[128,13,8,128]{3,2,1,0:T(8,128)} %all-to-all-done.recv_ref.recv_hbm, f32[256,2,8,128]{3,2,1,0:T(8,128)S(1)} %shard_map.87.force_ref), custom_call_target="tpu_custom_call" | custom-call | flops 10000000 | bytes 4194304 | tf_op jit(solution)/shard_map/pallas_call | solution.py:716
  103.3 0.1 collective-permute-start
  103.4 4.1 %collective-permute-start.1 = (f32[34,8,128]{2,1,0:T(8,128)S(1)}, f32[34,8,128]{2,1,0:T(8,128)S(1)}, u32[]{:S(2)}, u32[]{:S(2)}) collective-permute-start(f32[34,8,128]{2,1,0:T(8,128)S(1)} %get-tuple-element.12), channel_id=1, source_target_pairs={{1,2},{3,4},{5,6},{2,1},{4,3},{6,5},{9,10},{11,12},{13,14},{10,9},... | collective-permute-start | bytes 417800 | tf_op jit(solution)/shard_map/ppermute | solution.py:745
  107.4 3.1 %shard_map.90 = (f32[34,8,128]{2,1,0:T(8,128)S(1)}, f32[34,8,128]{2,1,0:T(8,128)S(1)}) custom-call(s32[16,16]{1,0:T(8,128)S(1)} %get-tuple-element.19.tile_ref, f32[128,13,8,128]{3,2,1,0:T(8,128)} %all-to-all-done.recv_ref.recv_hbm, f32[256,2,8,128]{3,2,1,0:T(8,128)S(1)} %shard_map.87.force_ref), custom_call_target="tpu_custom_call" | custom-call | flops 10000000 | bytes 6291456 | tf_op jit(solution)/shard_map/pallas_call | solution.py:725
  110.5 0.0 collective-permute-done.near_ref
  110.6 0.0 collective-permute-done.1.far_ref
  110.6 0.1 collective-permute-start.3
  110.7 4.8 %collective-permute-start.2 = (f32[40,8,128]{2,1,0:T(8,128)S(1)}, f32[40,8,128]{2,1,0:T(8,128)S(1)}, u32[]{:S(2)}, u32[]{:S(2)}) collective-permute-start(f32[40,8,128]{2,1,0:T(8,128)S(1)} %get-tuple-element.21), channel_id=1, source_target_pairs={{8,0},{16,8},{24,16},{32,24},{40,32},{48,40},{56,48},{64,56},{72,6... | collective-permute-start | bytes 491528 | tf_op jit(solution)/shard_map/ppermute | solution.py:759
  115.5 0.1 pad_add_fusion.lat_ref
  115.5 0.0 copy-start.2
  115.5 4.0 %shard_map.88.blocks_ref = f32[9,3072,128]{2,1,0:T(8,128)S(1)} custom-call(s32[16,16]{1,0:T(8,128)S(1)} %get-tuple-element.19.tile_ref, f32[128,13,8,128]{3,2,1,0:T(8,128)} %all-to-all-done.recv_ref.recv_hbm, f32[256,2,8,128]{3,2,1,0:T(8,128)S(1)} %shard_map.87.force_ref), custom_call_target="tpu_custom_call" | custom-call | flops 10000000 | bytes 25165824 | tf_op jit(solution)/shard_map/pallas_call | solution.py:734
  119.6 0.0 collective-permute-done.3.west_ref
  119.6 0.0 collective-permute-done.2.east_ref
  119.6 0.0 copy-done.2
  119.6 29.4 %shard_map.91 = (f32[9,3072,128]{2,1,0:T(8,128)S(1)}, f32[2,32,32,384]{3,2,1,0:T(8,128)}, f32[256,3,8,128]{3,2,1,0:T(8,128)}) custom-call(s32[16,16]{1,0:T(8,128)S(1)} %get-tuple-element.18.place_ref, s32[3]{0:T(128)S(1)} %pad_add_fusion.lat_ref, f32[9,3072,128]{2,1,0:T(8,128)S(1)} %shard_map.88.blocks_ref, ...), custom_call_target="tpu_custom_call", output_to_operand_aliasing={{0}: (2, {})} | custom-call | tf_op jit(solution)/shard_map/pallas_call | solution.py:767
  149.0 8.0 %all-to-all-start.1 = ((f32[128,6,8,128]{3,2,1,0:T(8,128)}), f32[128,6,8,128]{3,2,1,0:T(8,128)S(1)}, u32[]{:S(2)}, u32[]{:S(2)}) async-start(f32[128,6,8,128]{3,2,1,0:T(8,128)} %bitcast.6), calls=%async_computation.1 | async-start | bytes 6291456 | tf_op jit(solution)/shard_map/all_to_all | solution.py:796
  157.1 0.0 copy-start.3
  157.1 0.0 copy-start
  157.1 1.9 copy-done
  159.0 5.0 %shard_map.92 = f32[2,512,512]{2,1,0:T(8,128)} custom-call(f32[2,32,32,384]{3,2,1,0:T(8,128)S(1)} %copy-done), custom_call_target="tpu_custom_call" | custom-call | flops 10000000 | bytes 6291456 | tf_op jit(solution)/shard_map/pallas_call | solution.py:799
  163.9 34.7 %all-to-all-done.1 = f32[128,6,8,128]{3,2,1,0:T(8,128)S(1)} async-done(((f32[128,6,8,128]{3,2,1,0:T(8,128)}), f32[128,6,8,128]{3,2,1,0:T(8,128)S(1)}, u32[]{:S(2)}, u32[]{:S(2)}) %all-to-all-start.1) | async-done | bytes 3145760 | tf_op jit(solution)/shard_map/all_to_all | solution.py:796
  198.6 0.0 copy-done.3
  198.6 3.0 %shard_map.93 = f32[3,32,32,128]{3,2,1,0:T(8,128)} custom-call(s32[1,128]{1,0:T(1,128)S(1)} %copy-done.3, f32[256,3,8,128]{3,2,1,0:T(8,128)S(1)} %bitcast.5, f32[3,32,32,128]{3,2,1,0:T(8,128)} %stress_hbm.1), custom_call_target="tpu_custom_call" | custom-call | tf_op jit(solution)/shard_map/pallas_call | solution.py:808
  (6 shorter events, 0.0 us)
Async XLA Ops:
  6.6 92.9 %all-to-all-start = ((f32[128,13,8,128]{3,2,1,0:T(8,128)}), f32[128,13,8,128]{3,2,1,0:T(8,128)}, u32[]{:S(2)}, u32[]{:S(2)}) async-start(f32[128,13,8,128]{3,2,1,0:T(8,128)} %get-tuple-element.10), calls=%async_computation | async-start | bytes 13631488 | tf_op jit(solution)/shard_map/all_to_all | solution.py:701
  18.5 1.6 copy-start.1
  103.3 7.3 %collective-permute-start = (f32[34,8,128]{2,1,0:T(8,128)S(1)}, f32[34,8,128]{2,1,0:T(8,128)S(1)}, u32[]{:S(2)}, u32[]{:S(2)}) collective-permute-start(f32[34,8,128]{2,1,0:T(8,128)S(1)} %get-tuple-element.11), channel_id=1, source_target_pairs={{0,1},{2,3},{4,5},{6,7},{1,0},{3,2},{5,4},{7,6},{8,9},{10,11},{12,... | collective-permute-start | bytes 417800 | tf_op jit(solution)/shard_map/ppermute | solution.py:745
  103.4 7.2 %collective-permute-start.1 = (f32[34,8,128]{2,1,0:T(8,128)S(1)}, f32[34,8,128]{2,1,0:T(8,128)S(1)}, u32[]{:S(2)}, u32[]{:S(2)}) collective-permute-start(f32[34,8,128]{2,1,0:T(8,128)S(1)} %get-tuple-element.12), channel_id=1, source_target_pairs={{1,2},{3,4},{5,6},{2,1},{4,3},{6,5},{9,10},{11,12},{13,14},{10,9},... | collective-permute-start | bytes 417800 | tf_op jit(solution)/shard_map/ppermute | solution.py:745
  110.6 9.0 %collective-permute-start.3 = (f32[40,8,128]{2,1,0:T(8,128)S(1)}, f32[40,8,128]{2,1,0:T(8,128)S(1)}, u32[]{:S(2)}, u32[]{:S(2)}) collective-permute-start(f32[40,8,128]{2,1,0:T(8,128)S(1)} %get-tuple-element.20), channel_id=1, source_target_pairs={{0,8},{8,16},{16,24},{24,32},{32,40},{40,48},{48,56},{56,64},{64,7... | collective-permute-start | bytes 491528 | tf_op jit(solution)/shard_map/ppermute | solution.py:760
  110.7 8.9 %collective-permute-start.2 = (f32[40,8,128]{2,1,0:T(8,128)S(1)}, f32[40,8,128]{2,1,0:T(8,128)S(1)}, u32[]{:S(2)}, u32[]{:S(2)}) collective-permute-start(f32[40,8,128]{2,1,0:T(8,128)S(1)} %get-tuple-element.21), channel_id=1, source_target_pairs={{8,0},{16,8},{24,16},{32,24},{40,32},{48,40},{56,48},{64,56},{72,6... | collective-permute-start | bytes 491528 | tf_op jit(solution)/shard_map/ppermute | solution.py:759
  115.5 4.1 %copy-start.2 = (s32[32,384]{1,0:T(8,128)S(1)}, s32[32,384]{1,0:T(8,128)}, u32[]{:S(2)}) copy-start(s32[32,384]{1,0:T(8,128)} %constant.55.clone.cell_ref) | copy-start | bytes 147460
  149.0 49.5 %all-to-all-start.1 = ((f32[128,6,8,128]{3,2,1,0:T(8,128)}), f32[128,6,8,128]{3,2,1,0:T(8,128)S(1)}, u32[]{:S(2)}, u32[]{:S(2)}) async-start(f32[128,6,8,128]{3,2,1,0:T(8,128)} %bitcast.6), calls=%async_computation.1 | async-start | bytes 6291456 | tf_op jit(solution)/shard_map/all_to_all | solution.py:796
  157.1 41.5 %copy-start.3 = (s32[1,128]{1,0:T(1,128)S(1)}, s32[1,128]{1,0:T(1,128)}, u32[]{:S(2)}) copy-start(s32[1,128]{1,0:T(1,128)} %get-tuple-element.16.pos_ref) | copy-start | bytes 1540
  157.1 1.9 copy-start

commit v6 on v5

--- a/solution.py
+++ b/solution.py
@@ -259,14 +259,21 @@
     lax.fori_loop(BX_DEV // 2, BX_DEV, lat_rims(1), 0, unroll=2)
 
 
-def lon_kernel(tile_ref, recv_hbm, force_ref, east_ref, west_ref, edge_ref, sem):
+def lon_kernel(tile_ref, even_ref, recv_hbm, force_ref, near_ref, far_ref, edge_ref, sem):
     group_of = lane_ids((8, LANES)) // 32
     edges = (0, BX_DEV - 1)
+    even = even_ref[0] == 1
     fetch_edges(tile_ref, recv_hbm, edge_ref, sem, lambda i: [(bx, i) for bx in edges])
-    for side, (bx, ref, group) in enumerate(zip(edges, (east_ref, west_ref), (0, 3))):
-        half = int(bx >= BX_DEV // 2)
-        for part in range(4):
-            for field in range(FIELDS + 2):
+
+    def keep(first, last, index):
+        near_ref[index] = jnp.where(even, last, first)
+        far_ref[index] = jnp.where(even, first, last)
+
+    for part in range(4):
+        for field in range(FIELDS + 2):
+            found = []
+            for side, (bx, group) in enumerate(zip(edges, (0, 3))):
+                half = int(bx >= BX_DEV // 2)
                 total = jnp.zeros((8, LANES), jnp.float32)
                 for p in range(4):
                     by = part * 4 + p
@@ -277,12 +284,21 @@
                         got = jnp.where(tile_ref[bx, by] >= 0, got, 0.0)
                     turned = pltpu.roll(got, ((p - group) * 32) % LANES, 1) if p != group else got
                     total = jnp.where(group_of == p, turned, total)
-                ref[field * 4 + part] = total
-        for by in range(BY_DEV):
-            row = edge_ref[side * BX_DEV + by, FIELDS * (1 - half), half : half + 1, :]
-            ref[4 * (FIELDS + 2) + by // 8, by % 8 : by % 8 + 1, :] = jnp.where(
-                tile_ref[bx, by] >= 0, row, 0.0
-            )
+                found.append(total)
+            keep(*found, field * 4 + part)
+    sub = row_ids((8, LANES))
+    for v in range(BY_DEV // 8):
+        found = []
+        for side, bx in enumerate(edges):
+            half = int(bx >= BX_DEV // 2)
+            total = jnp.zeros((8, LANES), jnp.float32)
+            for r in range(8):
+                by = v * 8 + r
+                row = edge_ref[side * BX_DEV + by, FIELDS * (1 - half), half : half + 1, :]
+                row = jnp.where(tile_ref[bx, by] >= 0, row, 0.0)
+                total = jnp.where(sub == r, row, total)
+            found.append(total)
+        keep(*found, 4 * (FIELDS + 2) + v)
 
 
 def collect_kernel(tile_ref, recv_ref, force_ref, scr_ref):
@@ -372,8 +388,8 @@
     cell_ref,
     near_ref,
     far_ref,
-    east_ref,
-    west_ref,
+    lon_near_ref,
+    lon_far_ref,
     scr_ref,
     vel_out_ref,
     send_out_ref,
@@ -429,25 +445,31 @@
         return carry
 
     lax.fori_loop(0, BX_DEV, lat_rims, 0)
-    for ref, bx, group, row in ((west_ref, -1, 3, 7), (east_ref, BX_DEV, 0, 0)):
+    lon_even = lat_ref[3] == 1
+
+    def west(i):
+        return jnp.where(lon_even, lon_far_ref[i], lon_near_ref[i])
+
+    def east(i):
+        return jnp.where(lon_even, lon_near_ref[i], lon_far_ref[i])
+
+    for rim, bx, group, row in ((west, -1, 3, 7), (east, BX_DEV, 0, 0)):
         for field in range(fields):
             for part in range(4):
+                whole = rim(field * 4 + part)
                 for p in range(4):
-                    got = ref[field * 4 + part]
-                    got = pltpu.roll(got, ((group - p) * 32) % LANES, 1)
+                    got = pltpu.roll(whole, ((group - p) * 32) % LANES, 1)
                     scr_ref[field, spot(bx, part * 4 + p), :] = jnp.where(
                         lane // 32 == group, got, 0.0
                     )
         for by in range(BY_DEV):
-            scr_ref[EDGE, grid_row(bx, by), :] = ref[
-                fields * 4 + by // 8, by % 8 : by % 8 + 1, :
-            ]
+            scr_ref[EDGE, grid_row(bx, by), :] = rim(fields * 4 + by // 8)[by % 8 : by % 8 + 1]
         lat_rim(
             bx,
-            lambda v: ref[LON_RIM + v],
-            lambda v: ref[LON_RIM + 2 + v],
-            ref[LON_RIM + 4, row : row + 1, :],
-            ref[LON_RIM + 5, row : row + 1, :],
+            lambda v: rim(LON_RIM + v),
+            lambda v: rim(LON_RIM + 2 + v),
+            rim(LON_RIM + 4)[row : row + 1],
+            rim(LON_RIM + 5)[row : row + 1],
         )
 
     def turn_edges(t, carry):
@@ -722,15 +744,16 @@
         cost_estimate=cost(4),
         compiler_params=params(8),
     )(my_tile, even.reshape(1).astype(jnp.int32), recv, force_blocks)
-    east, west = pl.pallas_call(
+    lon_even = 1 - lon_index % 2
+    lon_near, lon_far = pl.pallas_call(
         lon_kernel,
         out_shape=(f32(LON_RIM, 8, LANES),) * 2,
-        in_specs=[SMEM, HBM, VMEM],
+        in_specs=[SMEM, SMEM, HBM, VMEM],
         out_specs=(VMEM,) * 2,
         scratch_shapes=edge_scratch,
         cost_estimate=cost(6),
         compiler_params=params(8),
-    )(my_tile, recv, force_blocks)
+    )(my_tile, lon_even.reshape(1).astype(jnp.int32), recv, force_blocks)
     blocks = pl.pallas_call(
         collect_kernel,
         out_shape=pltpu.VMEM((FIELDS + 3, GRID_LANES * 8, LANES), jnp.float32),
@@ -746,18 +769,20 @@
 
     got_near = exchange(near, 0)
     got_far = exchange(far, 1)
-    ring = [(i, (i + 1) % lon_count) for i in range(lon_count)]
     end = BX_DEV * 2
-
-    def with_corners(rim, bx):
-        pairs = [x[bx * 2 : bx * 2 + 2] for x in (got_near, got_far)]
-        rows = [x[end + bx // 8 : end + bx // 8 + 1] for x in (got_near, got_far)]
-        return jnp.concatenate([rim] + pairs + rows, axis=0)
-
-    east = with_corners(east, 0)
-    west = with_corners(west, BX_DEV - 1)
-    got_east = lax.ppermute(east, "lon", [(k, i) for i, k in ring])
-    got_west = lax.ppermute(west, "lon", ring)
+    rows = BX_DEV // 8
+
+    def with_corners(rim, last):
+        pairs = [jnp.where(last, x[end - 2 : end], x[:2]) for x in (got_near, got_far)]
+        edge = [jnp.where(last, x[end + rows - 1 :], x[end : end + 1]) for x in (got_near, got_far)]
+        return jnp.concatenate([rim] + pairs + edge, axis=0)
+
+    def exchange_lon(rim, first):
+        pairs = [(i, (i + 1) % lon_count) for i in range(first, lon_count, 2)]
+        return lax.ppermute(rim, "lon", pairs + [(k, i) for i, k in pairs])
+
+    got_lon_near = exchange_lon(with_corners(lon_near, lon_even == 1), 0)
+    got_lon_far = exchange_lon(with_corners(lon_far, lon_even == 0), 1)
     grid = np.arange(GRID_LANES) % SIDE - 1
     cells = jnp.asarray(grid[None, :] * B + np.arange(B)[:, None], jnp.int32)
     state = (B + 2, B, GRID_LANES)
@@ -785,13 +810,13 @@
         compiler_params=params(26),
     )(
         places,
-        jnp.stack((lat_index, lat_count, even)).astype(jnp.int32),
+        jnp.stack((lat_index, lat_count, even, lon_even)).astype(jnp.int32),
         blocks,
         cells,
         got_near,
         got_far,
-        got_east,
-        got_west,
+        got_lon_near,
+        got_lon_far,
     )
     returned = lax.all_to_all(
         back.reshape(devices, 6, 8, LANES), ("lon", "lat"), 0, 0, tiled=True

time: 202 us -> 201 us (level)
    ppermute x2, starting transfers between devices: 4.85 us -> 2.67 us  [exchange_lon(): return lax.ppermute(rim, 'lon', pairs + [(k, i) for i, k in pairs])]
  transfers between devices with their start and end apart: 6 -> 6, of which waited for: 2 -> 4; matrix products, arithmetic and copies ran while one was open for 0% -> 0% of each run, Pallas kernels for 7% -> 7%
where the time goes in v6:
time: 201 us; the launch traced here: 200 us
  waiting for transfers between devices  112 us (56%)
  Pallas kernels  55.2 us (27%)
  starting transfers between devices  27.1 us (13%)
  local copies, waits for them, and re-layouts  3.5 us (2%)
    all_to_all x1, waiting for transfers between devices, on_device(): recv = lax.all_to_all(send, ('lon', 'lat'), 0, 0, tiled=True)  75.7 us
    all_to_all x1, waiting for transfers between devices, on_device(): lax.all_to_all(back.reshape(devices, 6, 8, LANES), ('lon', 'lat'), 0, 0,...  34.7 us
    pallas_call x1, Pallas kernels, on_device(): pl.pallas_call(tile_kernel, out_shape=(pltpu.VMEM((FIELDS + 3, GRID_LANES...  29.4 us
    all_to_all x1, starting transfers between devices, on_device(): recv = lax.all_to_all(send, ('lon', 'lat'), 0, 0, tiled=True)  11.9 us
    all_to_all x1, starting transfers between devices, on_device(): lax.all_to_all(back.reshape(devices, 6, 8, LANES), ('lon', 'lat'), 0, 0,...  7.71 us
    pallas_call x1, Pallas kernels, on_device(): pl.pallas_call(pack_kernel, out_shape=(pltpu.HBM((devices, MESSAGE, 8, LA...  5.93 us
    pallas_call x1, Pallas kernels, on_device(): pl.pallas_call(velocity_kernel, out_shape=f32(2, ROWS, COLS), in_specs=[V...  4.96 us
    ppermute x2, starting transfers between devices, exchange(): return lax.ppermute(rim, 'lat', pairs + [(k, j) for j, k in pairs])  4.75 us
  transfers between devices with their start and end apart: 6, of which 4 were waited for; matrix products, arithmetic and copies ran while one was open for 0% of the time, Pallas kernels for 7%

profile of v6, /device:TPU:1, one launch (start us, length us, event | category | flops | bytes accessed | tf_op | source)
XLA Modules:
  0.0 199.8 jit_solution(13450651246383604223)
XLA Ops:
  0.6 5.9 %shard_map.86 = (f32[128,13,8,128]{3,2,1,0:T(8,128)}, s32[1,128]{1,0:T(1,128)}) custom-call(s32[1]{0:T(128)} %bitcast.3.own_ref, s32[256,128]{1,0:T(8,128)} %owner_ref.1, f32[2,32,32,128]{3,2,1,0:T(8,128)} %vel_hbm.1, f32[3,32,32,128]{3,2,1,0:T(8,128)} %stress_hbm.1, f32[32,32,128]{2,1,0:T(8,128)} %mass_hbm.1, f32[32,32,128]{2,1,0:T(8,128)} %strength_hbm.1), custom_call_target="tpu_custom_call" | custom-call | tf_op jit(solution)/shard_map/pallas_call | solution.py:702
  6.6 11.9 %all-to-all-start = ((f32[128,13,8,128]{3,2,1,0:T(8,128)}), f32[128,13,8,128]{3,2,1,0:T(8,128)}, u32[]{:S(2)}, u32[]{:S(2)}) async-start(f32[128,13,8,128]{3,2,1,0:T(8,128)} %get-tuple-element.10), calls=%async_computation | async-start | bytes 13631488 | tf_op jit(solution)/shard_map/all_to_all | solution.py:723
  18.5 0.0 copy-start.1
  18.5 1.6 copy-done.1
  20.1 2.9 %shard_map.87.force_ref = f32[256,2,8,128]{3,2,1,0:T(8,128)S(1)} custom-call(f32[2,512,512]{2,1,0:T(8,128)S(1)} %copy-done.1), custom_call_target="tpu_custom_call" | custom-call | flops 10000000 | bytes 4194304 | tf_op jit(solution)/shard_map/pallas_call | solution.py:725
  23.1 0.8 add_select_fusion
  23.8 75.7 %all-to-all-done.recv_ref.recv_hbm = f32[128,13,8,128]{3,2,1,0:T(8,128)} async-done(((f32[128,13,8,128]{3,2,1,0:T(8,128)}), f32[128,13,8,128]{3,2,1,0:T(8,128)}, u32[]{:S(2)}, u32[]{:S(2)}) %all-to-all-start) | async-done | bytes 6815776 | tf_op jit(solution)/shard_map/all_to_all | solution.py:723
  99.5 2.7 %shard_map.89 = (f32[34,8,128]{2,1,0:T(8,128)S(1)}, f32[34,8,128]{2,1,0:T(8,128)S(1)}) custom-call(s32[16,16]{1,0:T(8,128)S(1)} %get-tuple-element.19.tile_ref, s32[1]{0:T(128)} %bitcast.1.even_ref, f32[128,13,8,128]{3,2,1,0:T(8,128)} %all-to-all-done.recv_ref.recv_hbm, f32[256,2,8,128]{3,2,1,0:T(8,128)S(1)} %shard_map.87.force_ref), custom_call_target="tpu_custom_call" | custom-call | flops 10000000 | bytes 4194304 | tf_op jit(solution)/shard_map/pallas_call | solution.py:738
  102.2 1.9 collective-permute-start
  104.1 2.8 %collective-permute-start.1 = (f32[34,8,128]{2,1,0:T(8,128)S(1)}, f32[34,8,128]{2,1,0:T(8,128)S(1)}, u32[]{:S(2)}, u32[]{:S(2)}) collective-permute-start(f32[34,8,128]{2,1,0:T(8,128)S(1)} %get-tuple-element.12), channel_id=1, source_target_pairs={{1,2},{3,4},{5,6},{2,1},{4,3},{6,5},{9,10},{11,12},{13,14},{10,9},... | collective-permute-start | bytes 417800 | tf_op jit(solution)/shard_map/ppermute | solution.py:768
  106.9 2.1 %shard_map.90 = (f32[34,8,128]{2,1,0:T(8,128)S(1)}, f32[34,8,128]{2,1,0:T(8,128)S(1)}) custom-call(s32[16,16]{1,0:T(8,128)S(1)} %get-tuple-element.19.tile_ref, s32[1]{0:T(128)} %bitcast.2.even_ref, f32[128,13,8,128]{3,2,1,0:T(8,128)} %all-to-all-done.recv_ref.recv_hbm, f32[256,2,8,128]{3,2,1,0:T(8,128)S(1)} %shard_map.87.force_ref), custom_call_target="tpu_custom_call" | custom-call | flops 10000000 | bytes 6291456 | tf_op jit(solution)/shard_map/pallas_call | solution.py:748
  109.1 0.0 collective-permute-done.near_ref
  109.1 1.3 collective-permute-done.1.far_ref
  110.5 2.7 %collective-permute-start.3 = (f32[40,8,128]{2,1,0:T(8,128)S(1)}, f32[40,8,128]{2,1,0:T(8,128)S(1)}, u32[]{:S(2)}, u32[]{:S(2)}) collective-permute-start(f32[40,8,128]{2,1,0:T(8,128)S(1)} %get-tuple-element.20), channel_id=1, source_target_pairs={{8,16},{24,32},{40,48},{56,64},{72,80},{88,96},{104,112},{120,0},{... | collective-permute-start | bytes 491528 | tf_op jit(solution)/shard_map/ppermute | solution.py:782
  113.2 0.0 collective-permute-start.2
  113.2 0.1 pad_add_fusion.lat_ref
  113.2 0.0 copy-start.2
  113.2 4.1 %shard_map.88.blocks_ref = f32[9,3072,128]{2,1,0:T(8,128)S(1)} custom-call(s32[16,16]{1,0:T(8,128)S(1)} %get-tuple-element.19.tile_ref, f32[128,13,8,128]{3,2,1,0:T(8,128)} %all-to-all-done.recv_ref.recv_hbm, f32[256,2,8,128]{3,2,1,0:T(8,128)S(1)} %shard_map.87.force_ref), custom_call_target="tpu_custom_call" | custom-call | flops 10000000 | bytes 25165824 | tf_op jit(solution)/shard_map/pallas_call | solution.py:757
  117.3 0.7 collective-permute-done.3.lon_far_ref
  118.1 0.0 collective-permute-done.2.lon_near_ref
  118.1 0.0 copy-done.2
  118.1 29.4 %shard_map.91 = (f32[9,3072,128]{2,1,0:T(8,128)S(1)}, f32[2,32,32,384]{3,2,1,0:T(8,128)}, f32[256,3,8,128]{3,2,1,0:T(8,128)}) custom-call(s32[16,16]{1,0:T(8,128)S(1)} %get-tuple-element.18.place_ref, s32[4]{0:T(128)S(1)} %pad_add_fusion.lat_ref, f32[9,3072,128]{2,1,0:T(8,128)S(1)} %shard_map.88.blocks_ref, ...), custom_call_target="tpu_custom_call", output_to_operand_aliasing={{0}: (2, {})} | custom-call | tf_op jit(solution)/shard_map/pallas_call | solution.py:792
  147.5 7.7 %all-to-all-start.1 = ((f32[128,6,8,128]{3,2,1,0:T(8,128)}), f32[128,6,8,128]{3,2,1,0:T(8,128)S(1)}, u32[]{:S(2)}, u32[]{:S(2)}) async-start(f32[128,6,8,128]{3,2,1,0:T(8,128)} %bitcast.7), calls=%async_computation.1 | async-start | bytes 6291456 | tf_op jit(solution)/shard_map/all_to_all | solution.py:821
  155.2 0.0 copy-start.3
  155.2 0.0 copy-start
  155.2 1.9 copy-done
  157.1 5.0 %shard_map.92 = f32[2,512,512]{2,1,0:T(8,128)} custom-call(f32[2,32,32,384]{3,2,1,0:T(8,128)S(1)} %copy-done), custom_call_target="tpu_custom_call" | custom-call | flops 10000000 | bytes 6291456 | tf_op jit(solution)/shard_map/pallas_call | solution.py:824
  162.1 34.7 %all-to-all-done.1 = f32[128,6,8,128]{3,2,1,0:T(8,128)S(1)} async-done(((f32[128,6,8,128]{3,2,1,0:T(8,128)}), f32[128,6,8,128]{3,2,1,0:T(8,128)S(1)}, u32[]{:S(2)}, u32[]{:S(2)}) %all-to-all-start.1) | async-done | bytes 3145760 | tf_op jit(solution)/shard_map/all_to_all | solution.py:821
  196.7 0.0 copy-done.3
  196.7 3.0 %shard_map.93 = f32[3,32,32,128]{3,2,1,0:T(8,128)} custom-call(s32[1,128]{1,0:T(1,128)S(1)} %copy-done.3, f32[256,3,8,128]{3,2,1,0:T(8,128)S(1)} %bitcast.6, f32[3,32,32,128]{3,2,1,0:T(8,128)} %stress_hbm.1), custom_call_target="tpu_custom_call" | custom-call | tf_op jit(solution)/shard_map/pallas_call | solution.py:833
  (6 shorter events, 0.0 us)
Async XLA Ops:
  6.6 92.9 %all-to-all-start = ((f32[128,13,8,128]{3,2,1,0:T(8,128)}), f32[128,13,8,128]{3,2,1,0:T(8,128)}, u32[]{:S(2)}, u32[]{:S(2)}) async-start(f32[128,13,8,128]{3,2,1,0:T(8,128)} %get-tuple-element.10), calls=%async_computation | async-start | bytes 13631488 | tf_op jit(solution)/shard_map/all_to_all | solution.py:723
  18.5 1.6 copy-start.1
  102.2 6.9 %collective-permute-start = (f32[34,8,128]{2,1,0:T(8,128)S(1)}, f32[34,8,128]{2,1,0:T(8,128)S(1)}, u32[]{:S(2)}, u32[]{:S(2)}) collective-permute-start(f32[34,8,128]{2,1,0:T(8,128)S(1)} %get-tuple-element.11), channel_id=1, source_target_pairs={{0,1},{2,3},{4,5},{6,7},{1,0},{3,2},{5,4},{7,6},{8,9},{10,11},{12,... | collective-permute-start | bytes 417800 | tf_op jit(solution)/shard_map/ppermute | solution.py:768
  104.1 6.4 %collective-permute-start.1 = (f32[34,8,128]{2,1,0:T(8,128)S(1)}, f32[34,8,128]{2,1,0:T(8,128)S(1)}, u32[]{:S(2)}, u32[]{:S(2)}) collective-permute-start(f32[34,8,128]{2,1,0:T(8,128)S(1)} %get-tuple-element.12), channel_id=1, source_target_pairs={{1,2},{3,4},{5,6},{2,1},{4,3},{6,5},{9,10},{11,12},{13,14},{10,9},... | collective-permute-start | bytes 417800 | tf_op jit(solution)/shard_map/ppermute | solution.py:768
  110.5 7.6 %collective-permute-start.3 = (f32[40,8,128]{2,1,0:T(8,128)S(1)}, f32[40,8,128]{2,1,0:T(8,128)S(1)}, u32[]{:S(2)}, u32[]{:S(2)}) collective-permute-start(f32[40,8,128]{2,1,0:T(8,128)S(1)} %get-tuple-element.20), channel_id=1, source_target_pairs={{8,16},{24,32},{40,48},{56,64},{72,80},{88,96},{104,112},{120,0},{... | collective-permute-start | bytes 491528 | tf_op jit(solution)/shard_map/ppermute | solution.py:782
  113.2 4.9 %collective-permute-start.2 = (f32[40,8,128]{2,1,0:T(8,128)S(1)}, f32[40,8,128]{2,1,0:T(8,128)S(1)}, u32[]{:S(2)}, u32[]{:S(2)}) collective-permute-start(f32[40,8,128]{2,1,0:T(8,128)S(1)} %get-tuple-element.21), channel_id=1, source_target_pairs={{0,8},{16,24},{32,40},{48,56},{64,72},{80,88},{96,104},{112,120},{... | collective-permute-start | bytes 491528 | tf_op jit(solution)/shard_map/ppermute | solution.py:782
  113.2 4.8 %copy-start.2 = (s32[32,384]{1,0:T(8,128)S(1)}, s32[32,384]{1,0:T(8,128)}, u32[]{:S(2)}) copy-start(s32[32,384]{1,0:T(8,128)} %constant.59.clone.cell_ref) | copy-start | bytes 147460
  147.5 49.2 %all-to-all-start.1 = ((f32[128,6,8,128]{3,2,1,0:T(8,128)}), f32[128,6,8,128]{3,2,1,0:T(8,128)S(1)}, u32[]{:S(2)}, u32[]{:S(2)}) async-start(f32[128,6,8,128]{3,2,1,0:T(8,128)} %bitcast.7), calls=%async_computation.1 | async-start | bytes 6291456 | tf_op jit(solution)/shard_map/all_to_all | solution.py:821
  155.2 41.5 %copy-start.3 = (s32[1,128]{1,0:T(1,128)S(1)}, s32[1,128]{1,0:T(1,128)}, u32[]{:S(2)}) copy-start(s32[1,128]{1,0:T(1,128)} %get-tuple-element.16.pos_ref) | copy-start | bytes 1540
  155.2 1.9 copy-start

commit v7 on v6

--- a/solution.py
+++ b/solution.py
@@ -205,24 +205,37 @@
     edges.wait()
 
 
-def fetch_edges(tile_ref, recv_hbm, edge_ref, sem, places):
+def start_edges(tile_ref, recv_hbm, edge_ref, sem, places, first, last):
     count = recv_hbm.shape[0]
 
     def fetch(i, carry):
         for side, (bx, by) in enumerate(places(i)):
-            first = jnp.int32(bx >= BX_DEV // 2) * FIELDS
-            block = recv_hbm.at[tile_ref[bx, by] & (count - 1), pl.ds(first, FIELDS + 1)]
+            start = jnp.int32(bx >= BX_DEV // 2) * FIELDS
+            block = recv_hbm.at[tile_ref[bx, by] & (count - 1), pl.ds(start, FIELDS + 1)]
             pltpu.make_async_copy(block, edge_ref.at[side * BX_DEV + i], sem).start()
         return carry
 
-    lax.fori_loop(0, BX_DEV, fetch, 0, unroll=4)
-    pltpu.make_async_copy(edge_ref, edge_ref, sem).wait()
-
-
-def lat_kernel(tile_ref, even_ref, recv_hbm, force_ref, near_ref, far_ref, edge_ref, sem):
+    lax.fori_loop(first, last, fetch, 0, unroll=4)
+    everything = edge_ref.at[pl.ds(0, 2 * (last - first))]
+    return pltpu.make_async_copy(everything, everything, sem)
+
+
+def lat_kernel(tile_ref, even_ref, recv_hbm, force_ref, near_ref, far_ref, edge_ref, sems):
     in_group = lane_ids((8, LANES)) % 32
     edges = (0, BY_DEV - 1)
-    fetch_edges(tile_ref, recv_hbm, edge_ref, sem, lambda i: [(i, by) for by in edges])
+    middle = BX_DEV // 2
+    waits = [
+        start_edges(
+            tile_ref,
+            recv_hbm,
+            edge_ref,
+            sems.at[half],
+            lambda i: [(i, by) for by in edges],
+            half * middle,
+            (half + 1) * middle,
+        )
+        for half in range(2)
+    ]
 
     def lat_rims(half):
         def body(bx, carry):
@@ -255,15 +268,18 @@
 
         return body
 
-    lax.fori_loop(0, BX_DEV // 2, lat_rims(0), 0, unroll=2)
-    lax.fori_loop(BX_DEV // 2, BX_DEV, lat_rims(1), 0, unroll=2)
+    waits[0].wait()
+    lax.fori_loop(0, middle, lat_rims(0), 0, unroll=2)
+    waits[1].wait()
+    lax.fori_loop(middle, BX_DEV, lat_rims(1), 0, unroll=2)
 
 
 def lon_kernel(tile_ref, even_ref, recv_hbm, force_ref, near_ref, far_ref, edge_ref, sem):
     group_of = lane_ids((8, LANES)) // 32
     edges = (0, BX_DEV - 1)
     even = even_ref[0] == 1
-    fetch_edges(tile_ref, recv_hbm, edge_ref, sem, lambda i: [(bx, i) for bx in edges])
+    places = lambda i: [(bx, i) for bx in edges]
+    start_edges(tile_ref, recv_hbm, edge_ref, sem, places, 0, BY_DEV).wait()
 
     def keep(first, last, index):
         near_ref[index] = jnp.where(even, last, first)
@@ -740,7 +756,7 @@
         out_shape=(f32(LAT_RIM, 8, LANES),) * 2,
         in_specs=[SMEM, SMEM, HBM, VMEM],
         out_specs=(VMEM,) * 2,
-        scratch_shapes=edge_scratch,
+        scratch_shapes=[edge_scratch[0], pltpu.SemaphoreType.DMA((2,))],
         cost_estimate=cost(4),
         compiler_params=params(8),
     )(my_tile, even.reshape(1).astype(jnp.int32), recv, force_blocks)

time: 201 us -> 201 us (level)
  transfers between devices with their start and end apart: 6 -> 6, of which waited for: 4 -> 3; matrix products, arithmetic and copies ran while one was open for 0% -> 0% of each run, Pallas kernels for 7% -> 7%
where the time goes in v7:
time: 201 us; the launch traced here: 200 us
  waiting for transfers between devices  111 us (55%)
  Pallas kernels  55.2 us (27%)
  starting transfers between devices  28.6 us (14%)
  local copies, waits for them, and re-layouts  3.5 us (2%)
    all_to_all x1, waiting for transfers between devices, on_device(): recv = lax.all_to_all(send, ('lon', 'lat'), 0, 0, tiled=True)  75.7 us
    all_to_all x1, waiting for transfers between devices, on_device(): lax.all_to_all(back.reshape(devices, 6, 8, LANES), ('lon', 'lat'), 0, 0,...  34.7 us
    pallas_call x1, Pallas kernels, on_device(): pl.pallas_call(tile_kernel, out_shape=(pltpu.VMEM((FIELDS + 3, GRID_LANES...  29.4 us
    all_to_all x1, starting transfers between devices, on_device(): recv = lax.all_to_all(send, ('lon', 'lat'), 0, 0, tiled=True)  11.9 us
    all_to_all x1, starting transfers between devices, on_device(): lax.all_to_all(back.reshape(devices, 6, 8, LANES), ('lon', 'lat'), 0, 0,...  8.16 us
    pallas_call x1, Pallas kernels, on_device(): pl.pallas_call(pack_kernel, out_shape=(pltpu.HBM((devices, MESSAGE, 8, LA...  5.94 us
    ppermute x2, starting transfers between devices, exchange(): return lax.ppermute(rim, 'lat', pairs + [(k, j) for j, k in pairs])  5.05 us
    pallas_call x1, Pallas kernels, on_device(): pl.pallas_call(velocity_kernel, out_shape=f32(2, ROWS, COLS), in_specs=[V...  4.96 us
  transfers between devices with their start and end apart: 6, of which 3 were waited for; matrix products, arithmetic and copies ran while one was open for 0% of the time, Pallas kernels for 7%

profile of v7, /device:TPU:1, one launch (start us, length us, event | category | flops | bytes accessed | tf_op | source)
XLA Modules:
  0.0 199.6 jit_solution(11807993936925085616)
XLA Ops:
  0.6 5.9 %shard_map.86 = (f32[128,13,8,128]{3,2,1,0:T(8,128)}, s32[1,128]{1,0:T(1,128)}) custom-call(s32[1]{0:T(128)} %bitcast.3.own_ref, s32[256,128]{1,0:T(8,128)} %owner_ref.1, f32[2,32,32,128]{3,2,1,0:T(8,128)} %vel_hbm.1, f32[3,32,32,128]{3,2,1,0:T(8,128)} %stress_hbm.1, f32[32,32,128]{2,1,0:T(8,128)} %mass_hbm.1, f32[32,32,128]{2,1,0:T(8,128)} %strength_hbm.1), custom_call_target="tpu_custom_call" | custom-call | tf_op jit(solution)/shard_map/pallas_call | solution.py:718
  6.6 11.9 %all-to-all-start = ((f32[128,13,8,128]{3,2,1,0:T(8,128)}), f32[128,13,8,128]{3,2,1,0:T(8,128)}, u32[]{:S(2)}, u32[]{:S(2)}) async-start(f32[128,13,8,128]{3,2,1,0:T(8,128)} %get-tuple-element.10), calls=%async_computation | async-start | bytes 13631488 | tf_op jit(solution)/shard_map/all_to_all | solution.py:739
  18.5 0.0 copy-start.1
  18.5 1.6 copy-done.1
  20.1 2.9 %shard_map.87.force_ref = f32[256,2,8,128]{3,2,1,0:T(8,128)S(1)} custom-call(f32[2,512,512]{2,1,0:T(8,128)S(1)} %copy-done.1), custom_call_target="tpu_custom_call" | custom-call | flops 10000000 | bytes 4194304 | tf_op jit(solution)/shard_map/pallas_call | solution.py:741
  23.0 0.8 add_select_fusion
  23.8 75.7 %all-to-all-done.recv_ref.recv_hbm = f32[128,13,8,128]{3,2,1,0:T(8,128)} async-done(((f32[128,13,8,128]{3,2,1,0:T(8,128)}), f32[128,13,8,128]{3,2,1,0:T(8,128)}, u32[]{:S(2)}, u32[]{:S(2)}) %all-to-all-start) | async-done | bytes 6815776 | tf_op jit(solution)/shard_map/all_to_all | solution.py:739
  99.5 2.5 %shard_map.89 = (f32[34,8,128]{2,1,0:T(8,128)S(1)}, f32[34,8,128]{2,1,0:T(8,128)S(1)}) custom-call(s32[16,16]{1,0:T(8,128)S(1)} %get-tuple-element.19.tile_ref, s32[1]{0:T(128)} %bitcast.1.even_ref, f32[128,13,8,128]{3,2,1,0:T(8,128)} %all-to-all-done.recv_ref.recv_hbm, f32[256,2,8,128]{3,2,1,0:T(8,128)S(1)} %shard_map.87.force_ref), custom_call_target="tpu_custom_call" | custom-call | flops 10000000 | bytes 4194304 | tf_op jit(solution)/shard_map/pallas_call | solution.py:754
  102.0 1.3 collective-permute-start
  103.3 3.8 %collective-permute-start.1 = (f32[34,8,128]{2,1,0:T(8,128)S(1)}, f32[34,8,128]{2,1,0:T(8,128)S(1)}, u32[]{:S(2)}, u32[]{:S(2)}) collective-permute-start(f32[34,8,128]{2,1,0:T(8,128)S(1)} %get-tuple-element.12), channel_id=1, source_target_pairs={{1,2},{3,4},{5,6},{2,1},{4,3},{6,5},{9,10},{11,12},{13,14},{10,9},... | collective-permute-start | bytes 417800 | tf_op jit(solution)/shard_map/ppermute | solution.py:784
  107.1 2.3 %shard_map.90 = (f32[34,8,128]{2,1,0:T(8,128)S(1)}, f32[34,8,128]{2,1,0:T(8,128)S(1)}) custom-call(s32[16,16]{1,0:T(8,128)S(1)} %get-tuple-element.19.tile_ref, s32[1]{0:T(128)} %bitcast.2.even_ref, f32[128,13,8,128]{3,2,1,0:T(8,128)} %all-to-all-done.recv_ref.recv_hbm, f32[256,2,8,128]{3,2,1,0:T(8,128)S(1)} %shard_map.87.force_ref), custom_call_target="tpu_custom_call" | custom-call | flops 10000000 | bytes 6291456 | tf_op jit(solution)/shard_map/pallas_call | solution.py:764
  109.5 0.0 collective-permute-done.near_ref
  109.5 0.3 collective-permute-done.1.far_ref
  109.8 3.4 %collective-permute-start.3 = (f32[40,8,128]{2,1,0:T(8,128)S(1)}, f32[40,8,128]{2,1,0:T(8,128)S(1)}, u32[]{:S(2)}, u32[]{:S(2)}) collective-permute-start(f32[40,8,128]{2,1,0:T(8,128)S(1)} %get-tuple-element.20), channel_id=1, source_target_pairs={{8,16},{24,32},{40,48},{56,64},{72,80},{88,96},{104,112},{120,0},{... | collective-permute-start | bytes 491528 | tf_op jit(solution)/shard_map/ppermute | solution.py:798
  113.3 0.0 collective-permute-start.2
  113.3 0.1 pad_add_fusion.lat_ref
  113.4 0.0 copy-start.2
  113.4 4.1 %shard_map.88.blocks_ref = f32[9,3072,128]{2,1,0:T(8,128)S(1)} custom-call(s32[16,16]{1,0:T(8,128)S(1)} %get-tuple-element.19.tile_ref, f32[128,13,8,128]{3,2,1,0:T(8,128)} %all-to-all-done.recv_ref.recv_hbm, f32[256,2,8,128]{3,2,1,0:T(8,128)S(1)} %shard_map.87.force_ref), custom_call_target="tpu_custom_call" | custom-call | flops 10000000 | bytes 25165824 | tf_op jit(solution)/shard_map/pallas_call | solution.py:773
  117.4 0.0 collective-permute-done.3.lon_far_ref
  117.4 0.0 collective-permute-done.2.lon_near_ref
  117.5 0.0 copy-done.2
  117.5 29.4 %shard_map.91 = (f32[9,3072,128]{2,1,0:T(8,128)S(1)}, f32[2,32,32,384]{3,2,1,0:T(8,128)}, f32[256,3,8,128]{3,2,1,0:T(8,128)}) custom-call(s32[16,16]{1,0:T(8,128)S(1)} %get-tuple-element.18.place_ref, s32[4]{0:T(128)S(1)} %pad_add_fusion.lat_ref, f32[9,3072,128]{2,1,0:T(8,128)S(1)} %shard_map.88.blocks_ref, ...), custom_call_target="tpu_custom_call", output_to_operand_aliasing={{0}: (2, {})} | custom-call | tf_op jit(solution)/shard_map/pallas_call | solution.py:808
  146.9 8.2 %all-to-all-start.1 = ((f32[128,6,8,128]{3,2,1,0:T(8,128)}), f32[128,6,8,128]{3,2,1,0:T(8,128)S(1)}, u32[]{:S(2)}, u32[]{:S(2)}) async-start(f32[128,6,8,128]{3,2,1,0:T(8,128)} %bitcast.7), calls=%async_computation.1 | async-start | bytes 6291456 | tf_op jit(solution)/shard_map/all_to_all | solution.py:837
  155.1 0.0 copy-start.3
  155.1 0.0 copy-start
  155.1 1.9 copy-done
  157.0 5.0 %shard_map.92 = f32[2,512,512]{2,1,0:T(8,128)} custom-call(f32[2,32,32,384]{3,2,1,0:T(8,128)S(1)} %copy-done), custom_call_target="tpu_custom_call" | custom-call | flops 10000000 | bytes 6291456 | tf_op jit(solution)/shard_map/pallas_call | solution.py:840
  161.9 34.7 %all-to-all-done.1 = f32[128,6,8,128]{3,2,1,0:T(8,128)S(1)} async-done(((f32[128,6,8,128]{3,2,1,0:T(8,128)}), f32[128,6,8,128]{3,2,1,0:T(8,128)S(1)}, u32[]{:S(2)}, u32[]{:S(2)}) %all-to-all-start.1) | async-done | bytes 3145760 | tf_op jit(solution)/shard_map/all_to_all | solution.py:837
  196.6 0.0 copy-done.3
  196.6 3.0 %shard_map.93 = f32[3,32,32,128]{3,2,1,0:T(8,128)} custom-call(s32[1,128]{1,0:T(1,128)S(1)} %copy-done.3, f32[256,3,8,128]{3,2,1,0:T(8,128)S(1)} %bitcast.6, f32[3,32,32,128]{3,2,1,0:T(8,128)} %stress_hbm.1), custom_call_target="tpu_custom_call" | custom-call | tf_op jit(solution)/shard_map/pallas_call | solution.py:849
  (6 shorter events, 0.0 us)
Async XLA Ops:
  6.6 92.9 %all-to-all-start = ((f32[128,13,8,128]{3,2,1,0:T(8,128)}), f32[128,13,8,128]{3,2,1,0:T(8,128)}, u32[]{:S(2)}, u32[]{:S(2)}) async-start(f32[128,13,8,128]{3,2,1,0:T(8,128)} %get-tuple-element.10), calls=%async_computation | async-start | bytes 13631488 | tf_op jit(solution)/shard_map/all_to_all | solution.py:739
  18.5 1.6 copy-start.1
  102.0 7.4 %collective-permute-start = (f32[34,8,128]{2,1,0:T(8,128)S(1)}, f32[34,8,128]{2,1,0:T(8,128)S(1)}, u32[]{:S(2)}, u32[]{:S(2)}) collective-permute-start(f32[34,8,128]{2,1,0:T(8,128)S(1)} %get-tuple-element.11), channel_id=1, source_target_pairs={{0,1},{2,3},{4,5},{6,7},{1,0},{3,2},{5,4},{7,6},{8,9},{10,11},{12,... | collective-permute-start | bytes 417800 | tf_op jit(solution)/shard_map/ppermute | solution.py:784
  103.3 6.5 %collective-permute-start.1 = (f32[34,8,128]{2,1,0:T(8,128)S(1)}, f32[34,8,128]{2,1,0:T(8,128)S(1)}, u32[]{:S(2)}, u32[]{:S(2)}) collective-permute-start(f32[34,8,128]{2,1,0:T(8,128)S(1)} %get-tuple-element.12), channel_id=1, source_target_pairs={{1,2},{3,4},{5,6},{2,1},{4,3},{6,5},{9,10},{11,12},{13,14},{10,9},... | collective-permute-start | bytes 417800 | tf_op jit(solution)/shard_map/ppermute | solution.py:784
  109.8 7.6 %collective-permute-start.3 = (f32[40,8,128]{2,1,0:T(8,128)S(1)}, f32[40,8,128]{2,1,0:T(8,128)S(1)}, u32[]{:S(2)}, u32[]{:S(2)}) collective-permute-start(f32[40,8,128]{2,1,0:T(8,128)S(1)} %get-tuple-element.20), channel_id=1, source_target_pairs={{8,16},{24,32},{40,48},{56,64},{72,80},{88,96},{104,112},{120,0},{... | collective-permute-start | bytes 491528 | tf_op jit(solution)/shard_map/ppermute | solution.py:798
  113.3 4.2 %collective-permute-start.2 = (f32[40,8,128]{2,1,0:T(8,128)S(1)}, f32[40,8,128]{2,1,0:T(8,128)S(1)}, u32[]{:S(2)}, u32[]{:S(2)}) collective-permute-start(f32[40,8,128]{2,1,0:T(8,128)S(1)} %get-tuple-element.21), channel_id=1, source_target_pairs={{0,8},{16,24},{32,40},{48,56},{64,72},{80,88},{96,104},{112,120},{... | collective-permute-start | bytes 491528 | tf_op jit(solution)/shard_map/ppermute | solution.py:798
  113.4 4.1 %copy-start.2 = (s32[32,384]{1,0:T(8,128)S(1)}, s32[32,384]{1,0:T(8,128)}, u32[]{:S(2)}) copy-start(s32[32,384]{1,0:T(8,128)} %constant.59.clone.cell_ref) | copy-start | bytes 147460
  146.9 49.7 %all-to-all-start.1 = ((f32[128,6,8,128]{3,2,1,0:T(8,128)}), f32[128,6,8,128]{3,2,1,0:T(8,128)S(1)}, u32[]{:S(2)}, u32[]{:S(2)}) async-start(f32[128,6,8,128]{3,2,1,0:T(8,128)} %bitcast.7), calls=%async_computation.1 | async-start | bytes 6291456 | tf_op jit(solution)/shard_map/all_to_all | solution.py:837
  155.1 41.5 %copy-start.3 = (s32[1,128]{1,0:T(1,128)S(1)}, s32[1,128]{1,0:T(1,128)}, u32[]{:S(2)}) copy-start(s32[1,128]{1,0:T(1,128)} %get-tuple-element.16.pos_ref) | copy-start | bytes 1540
  155.1 1.9 copy-start
